TPU v7x, 512 devices: a whole 4x8x8 slice. The times are simulated.
512 devices in a mesh: dom: 64 (over x, y, z_lo), band: 8 (over z_hi, core).
Axes of the slice: x: 4, y: 8, z: 8 (z_hi: 4, z_lo: 2; z = z_hi * 2 + z_lo), core: 2. Of those that a mesh axis runs over, the one named last changes fastest.
Arguments:
- orbitals: float32 [128, 512, 648], P('band', 'dom'), may hold values from -6 to 6
- cell_operator: float32 [729, 729], replicated, may hold values from -0.21875 to 0.21875
- cell_scale: float32 [512], P('dom'), may hold values from 0.5 to 2
- density: float32 [131072, 729], P(('dom', 'band')), may hold values from 0.01 to 1
- block_owner: int32 [131072, 1], P(('dom', 'band')), may hold values from 0 to 63; in each aligned block of 256 rows (0 to 255, 256 to 511, ...) at most 8 rows name the same one
- block_cell: int32 [131072], P(('dom', 'band')), may hold values from 0 to 7
Outputs:
- basis: float32 [128, 512, 648], P(None, ('dom', 'band'))
Inputs may be any that keep to these rules, and one draw needn't show every extreme that they name: `block_owner`: among the rows of one device no domain is named more than 8 times, a bound that some block reaches.
All inputs are finite; a program needn't handle non-finite values.
Results may differ from a plain program's by a relative error of at most 0.000071.
Values sent between devices are 32-bit elements; how exact they have to be, the bound alone decides.
No kernel may reach another device: no remote copies, remote signals or barrier semaphores. Data moves between devices by JAX's collectives and lax.ppermute only.
A program may use at most 64 MiB of HBM per device.

v0:
```python
import jax
import jax.numpy as jnp
from jax import lax
from jax.sharding import PartitionSpec as P

CAP = 8
FACE = 81
OWN = 648


CENTER = -1.0
HALF_WIDTH = 2.5


def shifted(value, axis, steps):
    count = lax.axis_size(axis)
    leading, last = (max(0, -steps), min(count, count - steps))
    return lax.ppermute(value, axis, [(source, source + steps) for source in range(leading, last)])


def cell_products(field, incoming, scales, potential, operator):
    layer = jnp.concatenate([field[:, 1:, :FACE], incoming], 1)
    cellvec = jnp.concatenate([field, layer], 2)
    product = jnp.einsum("ncj,jk->nck", cellvec, operator, precision=lax.Precision.HIGHEST)
    return scales[None, :, None] * product + potential[None] * cellvec


def assemble(result, carried):
    owned = result[:, :, :OWN]
    tail = result[:, :, OWN:]
    addition = jnp.concatenate([carried, tail[:, :-1]], 1)
    return jnp.concatenate([owned[:, :, :FACE] + addition, owned[:, :, FACE:]], 2)


def apply_operator(field, scales, potential, operator):
    incoming = shifted(field[:, :1, :FACE], "dom", -1)
    result = cell_products(field, incoming, scales, potential, operator)
    carried = shifted(result[:, -1:, OWN:], "dom", 1)
    return assemble(result, carried)


def body(orbitals, cell_operator, cell_scale, density, block_owner, block_cell):
    dom_count = lax.axis_size("dom")
    band_count = lax.axis_size("band")
    cells_dom = cell_scale.shape[0]
    owner = block_owner[:, 0]
    onehot = (owner[:, None] == jnp.arange(dom_count, dtype=jnp.int32)[None, :]).astype(jnp.int32)
    slots = jnp.sum(jnp.cumsum(onehot, axis=0) * onehot, axis=1) - 1
    send = jnp.zeros((dom_count, CAP, density.shape[1]), jnp.float32).at[owner, slots].set(density)
    send_cells = jnp.full((dom_count, CAP), cells_dom, jnp.int32).at[owner, slots].set(block_cell)
    got, got_cells = (
        lax.all_to_all(send, "dom", split_axis=0, concat_axis=0, tiled=True),
        lax.all_to_all(send_cells, "dom", split_axis=0, concat_axis=0, tiled=True),
    )
    table = (
        got_cells.reshape(-1)[:, None] == jnp.arange(cells_dom, dtype=jnp.int32)[None, :]
    ).astype(jnp.float32)
    partial_value = jnp.dot(
        table.T, got.reshape(-1, density.shape[1]), precision=lax.Precision.HIGHEST
    )
    rho = lax.psum(partial_value, "band")
    potential = -0.7386 * jnp.cbrt(rho)

    def step(values):
        return (
            apply_operator(values, cell_scale, potential, cell_operator) - CENTER * values
        ) / HALF_WIDTH

    first = step(orbitals)
    second = 2.0 * step(first) - orbitals
    filtered = 2.0 * step(second) - first
    filtered = lax.all_to_all(filtered, "band", split_axis=1, concat_axis=0, tiled=True)
    count = filtered.shape[0]
    flat = filtered.reshape(count, -1)
    total = flat.shape[1] * dom_count * band_count
    partial_intersection = jnp.dot(flat, flat.T, precision=lax.Precision.HIGHEST)
    intersection = lax.psum(partial_intersection, ("dom", "band")) / total
    lower = jnp.linalg.cholesky(intersection)
    basis = jax.scipy.linalg.solve_triangular(lower, flat, lower=True)
    return basis.reshape(filtered.shape)


def solution(mesh):
    return jax.shard_map(
        body,
        mesh=mesh,
        in_specs=(
            P("band", "dom", None),
            P(),
            P("dom"),
            P(("dom", "band"), None),
            P(("dom", "band"), None),
            P(("dom", "band")),
        ),
        out_specs=P(None, ("dom", "band"), None),
        check_vma=False,
    )
```

profile of v0, /device:TPU:1, one launch (start us, length us, event | category | flops | bytes accessed | tf_op | source)
XLA Modules:
  0.0 509.8 jit_solution(6131569619982550109)
XLA Ops:
  6.5 0.8 fusion.37
  8.2 0.8 fusion.34
  9.7 21.2 %scatter_fusion = s32[64,8]{0,1:T(8,128)S(1)} fusion(s32[64,8]{0,1:T(8,128)S(1)} %broadcast_in_dim.5, s32[256]{0:T(256)S(1)} %bitcast.63, s32[256]{0:T(256)} %param.11), kind=kCustom, calls=%fused_computation | custom fusion | bytes 5120 | tf_op jit(solution)/shard_map/scatter | solution.py:50
  30.9 0.7 copy.16
  31.6 12.9 %all-to-all-start = ((s32[64,1,8]{2,1,0:T(1,128)}), s32[64,1,8]{2,1,0:T(1,128)S(1)}, u32[]{:S(2)}, u32[]{:S(2)}) async-start(s32[64,1,8]{2,1,0:T(1,128)} %copy.16), calls=%async_computation | async-start | bytes 65536 | tf_op jit(solution)/shard_map/all_to_all | solution.py:53
  44.6 1.4 copy.17
  46.0 1.2 broadcast_in_dim.6
  47.2 34.2 %scatter_fusion.1 = f32[64,8,729]{2,1,0:T(8,128)} fusion(f32[64,8,729]{2,1,0:T(8,128)} %broadcast_in_dim.6, s32[256]{0:T(256)S(1)} %bitcast.64, f32[256,729]{1,0:T(8,128)S(1)} %copy.17), kind=kCustom, calls=%fused_computation.1 | custom fusion | bytes 2241536 | tf_op jit(solution)/shard_map/scatter | solution.py:49
  81.4 10.9 %all-to-all-start.1 = ((f32[64,8,729]{2,1,0:T(8,128)}), f32[64,8,729]{2,1,0:T(8,128)}, u32[]{:S(2)}, u32[]{:S(2)}) async-start(f32[64,8,729]{2,1,0:T(8,128)} %scatter_fusion.1), calls=%async_computation.1 | async-start | bytes 3145728 | tf_op jit(solution)/shard_map/all_to_all | solution.py:52
  92.4 1.3 collective-permute-start
  94.2 0.7 reduce.11
  95.1 34.7 %all-to-all-done.1 = f32[64,8,729]{2,1,0:T(8,128)} async-done(((f32[64,8,729]{2,1,0:T(8,128)}), f32[64,8,729]{2,1,0:T(8,128)}, u32[]{:S(2)}, u32[]{:S(2)}) %all-to-all-start.1) | async-done | bytes 1493024 | tf_op jit(solution)/shard_map/all_to_all | solution.py:52
  129.8 2.1 fusion.6
  131.9 31.3 %psum.14 = f32[8,729]{1,0:T(8,128)S(1)} all-reduce(f32[8,729]{1,0:T(8,128)S(1)} %fusion.6), channel_id=1, replica_groups=mesh['dom'=64,'band'=8] {'band'}, use_global_device_ids=true, to_apply=%region_5.6 | all-reduce | flops 5832 | bytes 46656 | tf_op jit(solution)/shard_map/psum | solution.py:61
  163.3 1.4 fusion.23
  164.8 2.3 collective-permute-start.1
  168.1 1.3 collective-permute-start.2
  169.4 3.3 collective-permute-done.2
  172.7 1.4 fusion.20
  174.3 4.4 collective-permute-start.3
  179.8 1.3 collective-permute-start.4
  181.1 3.6 collective-permute-done.4
  184.7 1.4 fusion.17
  186.2 4.3 collective-permute-start.5
  191.6 27.6 %all_to_all.29 = f32[16,8,648]{2,0,1:T(8,128)S(1)} all-to-all(f32[16,8,648]{2,0,1:T(8,128)S(1)} %copy.18), channel_id=1, replica_groups=mesh['dom'=64,'band'=8] {'band'}, dimensions={1} | all-to-all | bytes 663552 | tf_op jit(solution)/shard_map/all_to_all | solution.py:72
  219.3 1.1 fusion.42
  220.4 256.3 %all-reduce.2.cloned.1.call-done = f32[128,128]{0,1:T(8,128)} async-done(((f32[128,128]{0,1:T(8,128)}), f32[128,128]{0,1:T(8,128)}) %all-reduce.2.cloned.1.call-update) | async-done | bytes 65552 | tf_op jit(solution)/shard_map/psum | solution.py:77
  476.7 0.8 broadcast_multiply_fusion
  477.7 0.9 fusion.36
  478.5 11.7 %cholesky.16 = f32[128,128]{1,0:T(8,128)S(1)} custom-call(f32[128,128]{1,0:T(8,128)S(1)} %fusion.36), custom_call_target="Cholesky" | custom-call | tf_op jit(solution)/shard_map/jit(cholesky)/cholesky | solution.py:78
  491.6 9.8 %custom-call.7 = f32[1,128,128]{1,2,0:T(8,128)S(1)} custom-call(f32[1,128,128]{2,1,0:T(8,128)S(1)} %fusion.32), custom_call_target="InvertDiagBlocksLowerTriangular" | custom-call | tf_op jit(solution)/shard_map/jit(_solve_triangular)/triangular_solve | solution.py:79
  501.4 1.5 convolution_bitcast_fusion
  (49 shorter events, 7.1 us)
Async XLA Ops:
  6.5 156.7 %copy-start = (f32[729,729]{1,0:T(8,128)S(1)}, f32[729,729]{1,0:T(8,128)}, u32[]{:S(2)}) copy-start(f32[729,729]{1,0:T(8,128)} %param.7) | copy-start | bytes 6377296
  31.6 49.7 %all-to-all-start = ((s32[64,1,8]{2,1,0:T(1,128)}), s32[64,1,8]{2,1,0:T(1,128)S(1)}, u32[]{:S(2)}, u32[]{:S(2)}) async-start(s32[64,1,8]{2,1,0:T(1,128)} %copy.16), calls=%async_computation | async-start | bytes 65536 | tf_op jit(solution)/shard_map/all_to_all | solution.py:53
  81.4 11.0 %copy-start.1 = (f32[16,8,648]{2,1,0:T(8,128)S(1)}, f32[16,8,648]{2,1,0:T(8,128)}, u32[]{:S(2)}) copy-start(f32[16,8,648]{2,1,0:T(8,128)} %param.6) | copy-start | bytes 995332
  81.4 81.9 %copy-start.2 = (f32[8]{0:T(128)S(1)}, f32[8]{0:T(128)}, u32[]{:S(2)}) copy-start(f32[8]{0:T(128)} %param.8) | copy-start | bytes 100
  81.4 48.4 %all-to-all-start.1 = ((f32[64,8,729]{2,1,0:T(8,128)}), f32[64,8,729]{2,1,0:T(8,128)}, u32[]{:S(2)}, u32[]{:S(2)}) async-start(f32[64,8,729]{2,1,0:T(8,128)} %scatter_fusion.1), calls=%async_computation.1 | async-start | bytes 3145728 | tf_op jit(solution)/shard_map/all_to_all | solution.py:52
  92.3 384.4 %all-reduce.2.cloned.1.call-start = ((), (), s32[]{:S(2)}) async-start(), calls=%async_computation.3 | async-start | bytes 131072 | tf_op jit(solution)/shard_map/psum | solution.py:77
  92.4 70.8 %collective-permute-start = (f32[16,1,81]{2,1,0:T(1,128)S(1)}, f32[16,1,81]{2,1,0:T(1,128)S(1)}, u32[]{:S(2)}, u32[]{:S(2)}) collective-permute-start(f32[16,1,81]{2,1,0:T(1,128)S(1)} %slice.88), channel_id=1, source_target_pairs={{8,0},{16,8},{24,16},{32,24},{40,32},{48,40},{56,48},{64,56},{72,6... | collective-permute-start | bytes 15560 | tf_op jit(solution)/shard_map/ppermute | solution.py:18
  164.8 3.1 collective-permute-start.1
  168.1 4.7 collective-permute-start.2
  174.3 5.2 %collective-permute-start.3 = (f32[16,1,81]{2,1,0:T(1,128)S(1)}, f32[16,1,81]{2,1,0:T(1,128)S(1)}, u32[]{:S(2)}, u32[]{:S(2)}) collective-permute-start(f32[16,1,81]{2,1,0:T(1,128)S(1)} %slice.119), channel_id=1, source_target_pairs={{0,8},{8,16},{16,24},{24,32},{32,40},{40,48},{48,56},{56,64},{64,7... | collective-permute-start | bytes 15560 | tf_op jit(solution)/shard_map/ppermute | solution.py:18
  179.8 4.9 collective-permute-start.4
  186.2 5.1 collective-permute-start.5
Sparse Core Ops, SparseCore 0:
  220.5 256.1 all-reduce.1
where the time goes:
time: 512 us; the launch traced here: 510 us
  waiting for transfers between devices  300 us (59%)
  local copies, waits for them, and re-layouts  60.8 us (12%)
  blocking collectives  58.9 us (12%)
  starting transfers between devices  38.8 us (8%)
  other arithmetic  29 us (6%)
  between operations  13.7 us (3%)
  matrix products  8.98 us (2%)
    psum x1, waiting for transfers between devices, body(): intersection = lax.psum(partial_intersection, ('dom', 'band')) / total  256 us
    all_to_all x1, waiting for transfers between devices, body(): lax.all_to_all(send, 'dom', split_axis=0, concat_axis=0, tiled=True)  34.7 us
    scatter x1, local copies, waits for them, and re-layouts, body(): jnp.zeros((dom_count, CAP, density.shape[1]), jnp.float32).at[owner, slots]  34.2 us
    psum x1, blocking collectives, body(): rho = lax.psum(partial_value, 'band')  31.3 us
    all_to_all x1, blocking collectives, body(): lax.all_to_all(filtered, 'band', split_axis=1, concat_axis=0, tiled=True)  27.6 us
    scatter x1, local copies, waits for them, and re-layouts, body(): jnp.full((dom_count, CAP), cells_dom, jnp.int32).at[owner, slots]  21.2 us
    ppermute x6, starting transfers between devices, shifted(): lax.ppermute(value, axis, [(source, source + steps) for source in range(l...  14.9 us
    all_to_all x1, starting transfers between devices, body(): lax.all_to_all(send_cells, 'dom', split_axis=0, concat_axis=0, tiled=True)  12.9 us
  transfers between devices with their start and end apart: 9, of which 7 were waited for; matrix products, arithmetic and copies ran while one was open for 8% of the time, Pallas kernels for 0%

commit v1 on v0

v1 whole, which is shorter than its diff:
```python
import jax
import jax.numpy as jnp
from jax import lax
from jax.experimental import pallas as pl
from jax.experimental.pallas import tpu as pltpu
from jax.sharding import PartitionSpec as P

FACE = 81
OWN = 648
NODES = 729
WIDE = 768
HALF = 384
SLAB = 136
TILE5 = 640
SPLIT = OWN - TILE5

CENTER = -1.0
HALF_WIDTH = 2.5

X_GROUPS = [[x * 16 + r for x in range(4)] for r in range(16)]
YZ_GROUPS = [[x * 16 + r for r in range(16)] for x in range(4)]


def exchange(value, axis, groups=None):
    return lax.all_to_all(value, axis, split_axis=0, concat_axis=0, tiled=True, axis_index_groups=groups)


def split2(value):
    high = value.astype(jnp.bfloat16)
    low = (value - high.astype(jnp.float32)).astype(jnp.bfloat16)
    return high, low


def dot(a, b):
    return jnp.dot(a, b, preferred_element_type=jnp.float32)


def deliver_kernel(core_ref, target_ref, density_ref, mine_ref, theirs_ref, wide_ref):
    rows = 4 * SLAB
    count = density_ref.shape[0]
    wide_ref[:, TILE5:] = jnp.zeros((count, WIDE - TILE5), jnp.float32)
    wide_ref[:, :NODES] = density_ref[...]
    row = lax.broadcasted_iota(jnp.int32, (rows, count), 0)
    slab = (row >= SLAB).astype(jnp.int32) + (row >= 2 * SLAB).astype(jnp.int32) + (row >= 3 * SLAB).astype(jnp.int32)
    cell = row - 8 * slab - 3
    onehot = jnp.where(target_ref[...] == cell, 1.0, 0.0).astype(jnp.bfloat16)
    for half in range(2):
        values = wide_ref[:, half * HALF:(half + 1) * HALF]
        first = values.astype(jnp.bfloat16)
        rest = values - first.astype(jnp.float32)
        second = rest.astype(jnp.bfloat16)
        third = (rest - second.astype(jnp.float32)).astype(jnp.bfloat16)
        total = dot(onehot, first) + dot(onehot, second) + dot(onehot, third)

        @pl.when(core_ref[0] == half)
        def _():
            mine_ref[...] = total

        @pl.when(core_ref[0] != half)
        def _():
            theirs_ref[...] = total


def filter_kernel(last_ref, own_ref, left_ref, right_ref, scale_ref, rho_ref, operator_ref, out_ref,
                  kwide, khigh, klow, v0, v1, v2, chigh, clow, cell_buf, product, pot):
    kwide[720:, :] = jnp.zeros((WIDE - 720, WIDE), jnp.float32)
    kwide[:, TILE5:] = jnp.zeros((WIDE, WIDE - TILE5), jnp.float32)
    kwide[:NODES, :NODES] = operator_ref[...]
    for i in range(0, WIDE, 128):
        high, low = split2(kwide[i:i + 128, :])
        khigh[i:i + 128, :] = high
        klow[i:i + 128, :] = low
    for half in range(2):
        rho = rho_ref[half]
        pot[:, half * HALF:(half + 1) * HALF] = jnp.where(
            rho > 0.0, -0.7386 * jnp.exp(jnp.log(jnp.where(rho > 0.0, rho, 1.0)) * (1.0 / 3.0)), 0.0)
    lane = lax.broadcasted_iota(jnp.int32, (16, 128), 1)
    is_face = lane < FACE
    is_own5 = lane < SPLIT
    zero5 = jnp.zeros((16, WIDE - TILE5), jnp.float32)

    def place(i, value):
        v0[16 * i:16 * i + 16, TILE5:] = zero5
        v0[16 * i:16 * i + 16, :OWN] = value

    for i in range(3):
        place(i, left_ref[i])
        place(11 + i, right_ref[i])
    for i in range(8):
        place(3 + i, own_ref[i])

    def scale_of(i):
        if i < 3:
            line = left_ref[3, 5 + i:6 + i, :128]
        elif i < 11:
            line = scale_ref[i - 3:i - 2, :]
        else:
            line = right_ref[3, i - 11:i - 10, :128]
        return line

    alive = last_ref[0].astype(jnp.float32)

    def apply(source, begin, end, combine):
        for i in range(begin, end):
            r = slice(16 * i, 16 * i + 16)
            n = slice(16 * i + 16, 16 * i + 32)
            for t in range(6):
                c = slice(128 * t, 128 * t + 128)
                value = source[r, c]
                if t == 5:
                    face = jnp.where(is_face, source[n, :128], 0.0)
                    value = value + pltpu.roll(face, SPLIT, 1)
                cell_buf[r, c] = value
                high, low = split2(value)
                chigh[r, c] = high
                clow[r, c] = low
        r = slice(16 * begin, 16 * end)
        a, b = chigh[r, :], clow[r, :]
        product[r, :] = dot(a, khigh[...]) + dot(b, khigh[...]) + dot(a, klow[...])
        tail = None
        for i in range(begin, end):
            r = slice(16 * i, 16 * i + 16)
            scale = scale_of(i)
            parts = []
            for t in range(6):
                c = slice(128 * t, 128 * t + 128)
                parts.append(scale * product[r, c] + pot[i:i + 1, c] * cell_buf[r, c])
            if tail is not None:
                add = jnp.where(is_face, pltpu.roll(tail, 128 - SPLIT, 1), 0.0)
                if i == 11:
                    add = add * alive
                parts[0] = parts[0] + add
                for t in range(6):
                    value = parts[t]
                    if t == 5:
                        value = jnp.where(is_own5, value, 0.0)
                    combine(i, t, value)
            tail = parts[5]

    def at(ref, i, t):
        return ref[16 * i:16 * i + 16, 128 * t:128 * t + 128]

    def first(i, t, value):
        v1[16 * i:16 * i + 16, 128 * t:128 * t + 128] = (value - CENTER * at(v0, i, t)) * (1.0 / HALF_WIDTH)

    def second(i, t, value):
        v2[16 * i:16 * i + 16, 128 * t:128 * t + 128] = (value - CENTER * at(v1, i, t)) * (2.0 / HALF_WIDTH) - at(v0, i, t)

    def third(i, t, value):
        result = (value - CENTER * at(v2, i, t)) * (2.0 / HALF_WIDTH) - at(v1, i, t)
        if t < 5:
            out_ref[i - 3, :, 128 * t:128 * t + 128] = result
        else:
            out_ref[i - 3, :, TILE5:OWN] = result[:, :SPLIT]

    apply(v0, 0, 13, first)
    apply(v1, 1, 12, second)
    apply(v2, 2, 11, third)


def body(orbitals, cell_operator, cell_scale, density, block_owner, block_cell):
    dom_count = lax.axis_size("dom")
    band_count = lax.axis_size("band")
    dom = lax.axis_index("dom")
    core = jnp.reshape(lax.axis_index("band") % 2, (1,)).astype(jnp.int32)
    alive = jnp.reshape((dom < dom_count - 1).astype(jnp.int32), (1,))
    smem = pl.BlockSpec(memory_space=pltpu.SMEM)
    vmem = pl.BlockSpec(memory_space=pltpu.VMEM)
    params = pltpu.CompilerParams(vmem_limit_bytes=48 << 20)

    target = (block_owner[:, 0] * 8 + block_cell).reshape(1, -1)
    half_shape = jax.ShapeDtypeStruct((4 * SLAB, HALF), jnp.float32)
    mine, theirs = pl.pallas_call(
        deliver_kernel,
        out_shape=(half_shape, half_shape),
        in_specs=[smem, vmem, vmem],
        out_specs=(vmem, vmem),
        scratch_shapes=[pltpu.VMEM((density.shape[0], WIDE), jnp.float32)],
        compiler_params=params,
        name="deliver",
    )(core, target, density)
    other = lax.ppermute(theirs, "band", [(i, i ^ 1) for i in range(band_count)])

    cells = jnp.transpose(orbitals, (1, 0, 2))
    scales = jnp.broadcast_to(cell_scale[:, None], (8, OWN))
    scales16 = jnp.concatenate([scales, scales], 0)[None]
    left = lax.ppermute(jnp.concatenate([cells[5:], scales16], 0), "dom", [(i, i + 1) for i in range(dom_count - 1)])
    right = lax.ppermute(jnp.concatenate([cells[:3], scales16], 0), "dom", [(i + 1, i) for i in range(dom_count - 1)])

    part = exchange((mine + other).reshape(4, SLAB, HALF), "dom", X_GROUPS)
    slab = jnp.sum(part, 0)
    windows = jnp.concatenate([slab[:128].reshape(16, 8, HALF), slab[8:].reshape(16, 8, HALF)], 1)
    part = exchange(windows, "dom", YZ_GROUPS)
    window = jnp.sum(part, 0)
    part = exchange(jnp.broadcast_to(window[None], (band_count, 16, HALF)), "band")
    rho = jnp.sum(part.reshape(4, 2, 16, HALF), 0)

    filtered = pl.pallas_call(
        filter_kernel,
        out_shape=jax.ShapeDtypeStruct((8, 16, OWN), jnp.float32),
        in_specs=[smem] + [vmem] * 6,
        out_specs=vmem,
        scratch_shapes=[
            pltpu.VMEM((WIDE, WIDE), jnp.float32),
            pltpu.VMEM((WIDE, WIDE), jnp.bfloat16),
            pltpu.VMEM((WIDE, WIDE), jnp.bfloat16),
            pltpu.VMEM((224, WIDE), jnp.float32),
            pltpu.VMEM((224, WIDE), jnp.float32),
            pltpu.VMEM((224, WIDE), jnp.float32),
            pltpu.VMEM((224, WIDE), jnp.bfloat16),
            pltpu.VMEM((224, WIDE), jnp.bfloat16),
            pltpu.VMEM((224, WIDE), jnp.float32),
            pltpu.VMEM((224, WIDE), jnp.float32),
            pltpu.VMEM((16, WIDE), jnp.float32),
        ],
        compiler_params=params,
        name="chebyshev",
    )(alive, cells, left, right, scales[:, :128], rho, cell_operator)

    flat = exchange(filtered, "band").reshape(128, OWN)
    total = OWN * dom_count * band_count
    gram = jnp.dot(flat, flat.T, precision=lax.Precision.HIGHEST)
    part = jnp.sum(exchange(gram.reshape(dom_count, 2, 128), "dom"), 0)
    part = jnp.sum(exchange(jnp.broadcast_to(part[None], (band_count, 2, 128)), "band"), 0)
    intersection = exchange(jnp.broadcast_to(part[None], (dom_count, 2, 128)), "dom").reshape(128, 128) / total
    lower = jnp.linalg.cholesky(intersection)
    basis = jax.scipy.linalg.solve_triangular(lower, flat, lower=True)
    return basis.reshape(128, 1, OWN)


def solution(mesh):
    return jax.shard_map(
        body,
        mesh=mesh,
        in_specs=(
            P("band", "dom", None),
            P(),
            P("dom"),
            P(("dom", "band"), None),
            P(("dom", "band"), None),
            P(("dom", "band")),
        ),
        out_specs=P(None, ("dom", "band"), None),
        check_vma=False,
    )
```

time: 512 us -> 167 us (0.33)
  waiting for transfers between devices: 300 us -> 25.3 us
  local copies, waits for them, and re-layouts: 60.8 us -> 2.8 us
  blocking collectives: 58.9 us -> 74.6 us
  between operations: 13.7 us -> 0.19 us
  starting transfers between devices: 38.8 us -> 29.9 us
  matrix products: 8.98 us -> 2 us
  Pallas kernels: 0 us -> 5.44 us
    psum x1 -> x0, waiting for transfers between devices: 256 us -> none  [body(): intersection = lax.psum(partial_intersection, ('dom', 'band')) / total]
    scatter x2 -> x0, local copies, waits for them, and re-layouts: 55.4 us -> none  [the longest x1 34.2 us: body(): jnp.zeros((dom_count, CAP, density.shape[1]), jnp.float32).at[owner, slots]]
    all_to_all x1 -> x5, blocking collectives: 27.6 us -> 74.6 us  [exchange(): lax.all_to_all(value, axis, split_axis=0, concat_axis=0, tiled=True, axis...]
    psum x1 -> x0, blocking collectives: 31.3 us -> none  [body(): rho = lax.psum(partial_value, 'band')]
    all_to_all x2, waiting for transfers between devices: 34.7 us -> 16.5 us  [exchange(): lax.all_to_all(value, axis, split_axis=0, concat_axis=0, tiled=True, axis...]
    dot_general x5 -> x1, matrix products: 7.46 us -> 0.48 us  [body(): gram = jnp.dot(flat, flat.T, precision=lax.Precision.HIGHEST)]
    all_to_all x2, starting transfers between devices: 23.9 us -> 17.8 us  [exchange(): lax.all_to_all(value, axis, split_axis=0, concat_axis=0, tiled=True, axis...]
    pallas_call x0 -> x2, Pallas kernels: none -> 5.44 us  [the longest x1 4.03 us: body(): pl.pallas_call(filter_kernel, out_shape=jax.ShapeDtypeStruct((8, 16, OWN)...]
  transfers between devices with their start and end apart: 9 -> 5, of which waited for: 7 -> 5; matrix products, arithmetic and copies ran while one was open for 8% -> 1% of each run, Pallas kernels for 0% -> 0%
where the time goes in v1:
time: 167 us; the launch traced here: 166 us
  blocking collectives  74.6 us (45%)
  starting transfers between devices  29.9 us (18%)
  other arithmetic  26 us (16%)
  waiting for transfers between devices  25.3 us (15%)
  Pallas kernels  5.44 us (3%)
  local copies, waits for them, and re-layouts  2.8 us (2%)
  matrix products  2 us (1%)
    all_to_all x5, blocking collectives, exchange(): lax.all_to_all(value, axis, split_axis=0, concat_axis=0, tiled=True, axis...  74.6 us
    all_to_all x2, starting transfers between devices, exchange(): lax.all_to_all(value, axis, split_axis=0, concat_axis=0, tiled=True, axis...  17.8 us
    all_to_all x2, waiting for transfers between devices, exchange(): lax.all_to_all(value, axis, split_axis=0, concat_axis=0, tiled=True, axis...  16.5 us
    another operation x3, other arithmetic, body(): lower = jnp.linalg.cholesky(intersection)  12.4 us
    another operation x2, other arithmetic, body(): basis = jax.scipy.linalg.solve_triangular(lower, flat, lower=True)  10.5 us
    ppermute x1, starting transfers between devices, body(): lax.ppermute(theirs, 'band', [(i, i ^ 1) for i in range(band_count)])  8.79 us
    ppermute x1, waiting for transfers between devices, body(): lax.ppermute(jnp.concatenate([cells[5:], scales16], 0), 'dom', [(i, i + 1...  4.76 us
    pallas_call x1, Pallas kernels, body(): pl.pallas_call(filter_kernel, out_shape=jax.ShapeDtypeStruct((8, 16, OWN)...  4.03 us
  transfers between devices with their start and end apart: 5, of which 5 were waited for; matrix products, arithmetic and copies ran while one was open for 1% of the time, Pallas kernels for 0%

profile of v1, /device:TPU:1, one launch (start us, length us, event | category | flops | bytes accessed | tf_op | source)
XLA Modules:
  0.0 166.2 jit_solution(14192523679970867336)
XLA Ops:
  0.0 1.4 copy.30.density_ref
  1.4 0.7 broadcast_multiply_fusion.1
  2.1 0.7 add.23
  2.8 1.4 deliver.1
  4.2 8.8 %collective-permute-start.2 = (f32[544,384]{1,0:T(8,128)S(1)}, f32[544,384]{1,0:T(8,128)S(1)}, u32[]{:S(2)}, u32[]{:S(2)}) collective-permute-start(f32[544,384]{1,0:T(8,128)S(1)} %get-tuple-element.8), channel_id=1, source_target_pairs={{0,1},{1,0},{2,3},{3,2},{4,5},{5,4},{6,7},{7,6},{8,9},{9,8},{10,11... | collective-permute-start | bytes 2506760 | tf_op jit(solution)/shard_map/ppermute | solution.py:182
  13.0 2.0 %collective-permute-done.2 = f32[544,384]{1,0:T(8,128)S(1)} collective-permute-done((f32[544,384]{1,0:T(8,128)S(1)}, f32[544,384]{1,0:T(8,128)S(1)}, u32[]{:S(2)}, u32[]{:S(2)}) %collective-permute-start.2) | collective-permute-done | bytes 835616 | tf_op jit(solution)/shard_map/ppermute | solution.py:182
  15.0 14.8 %all_to_all.35 = f32[4,136,384]{2,1,0:T(8,128)S(1)} all-to-all(f32[4,136,384]{2,1,0:T(8,128)S(1)} %bitcast.37), channel_id=1, replica_groups={{0,128,256,384},{8,136,264,392},{16,144,272,400},{24,152,280,408},{32,1..., dimensions={0} | all-to-all | bytes 1671168 | tf_op jit(solution)/shard_map/all_to_all | solution.py:25
  29.9 0.8 pad_maximum_fusion
  30.7 4.9 %all-to-all-start.1 = ((f32[16,16,384]{2,1,0:T(8,128)}), f32[16,16,384]{2,1,0:T(8,128)S(1)}, u32[]{:S(2)}, u32[]{:S(2)}) async-start(f32[16,16,384]{2,1,0:T(8,128)} %pad_maximum_fusion), calls=%async_computation.1 | async-start | bytes 786432 | tf_op jit(solution)/shard_map/all_to_all | solution.py:25
  35.6 0.1 copy.42
  35.7 11.9 %all-to-all-done.1 = f32[16,16,384]{2,1,0:T(8,128)S(1)} async-done(((f32[16,16,384]{2,1,0:T(8,128)}), f32[16,16,384]{2,1,0:T(8,128)S(1)}, u32[]{:S(2)}, u32[]{:S(2)}) %all-to-all-start.1) | async-done | bytes 393248 | tf_op jit(solution)/shard_map/all_to_all | solution.py:25
  47.7 0.7 broadcast_in_dim.13
  48.4 12.9 %all-to-all-start.2 = ((f32[8,16,384]{2,1,0:T(8,128)}), f32[8,16,384]{2,1,0:T(8,128)S(1)}, u32[]{:S(2)}, u32[]{:S(2)}) async-start(f32[8,16,384]{2,1,0:T(8,128)} %broadcast_in_dim.13), calls=%async_computation.2 | async-start | bytes 393216 | tf_op jit(solution)/shard_map/all_to_all | solution.py:25
  61.4 0.7 pad_maximum_fusion.1
  62.1 2.1 %collective-permute-start = (f32[4,16,648]{2,1,0:T(8,128)}, f32[4,16,648]{2,1,0:T(8,128)S(1)}, u32[]{:S(2)}, u32[]{:S(2)}) collective-permute-start(f32[4,16,648]{2,1,0:T(8,128)} %get-tuple-element.14), channel_id=1, source_target_pairs={{0,8},{8,16},{16,24},{24,32},{32,40},{40,48},{48,56},{56,64},{64,7... | collective-permute-start | bytes 497672 | tf_op jit(solution)/shard_map/ppermute | solution.py:187
  64.2 1.3 collective-permute-start.1
  65.5 4.6 %all-to-all-done.2 = f32[8,16,384]{2,1,0:T(8,128)S(1)} async-done(((f32[8,16,384]{2,1,0:T(8,128)}), f32[8,16,384]{2,1,0:T(8,128)S(1)}, u32[]{:S(2)}, u32[]{:S(2)}) %all-to-all-start.2) | async-done | bytes 196640 | tf_op jit(solution)/shard_map/all_to_all | solution.py:25
  70.1 4.8 %collective-permute-done.left_ref = f32[4,16,648]{2,1,0:T(8,128)S(1)} collective-permute-done((f32[4,16,648]{2,1,0:T(8,128)}, f32[4,16,648]{2,1,0:T(8,128)S(1)}, u32[]{:S(2)}, u32[]{:S(2)}) %collective-permute-start) | collective-permute-done | bytes 165920 | tf_op jit(solution)/shard_map/ppermute | solution.py:187
  74.8 2.0 %collective-permute-done.1.right_ref = f32[4,16,648]{2,1,0:T(8,128)S(1)} collective-permute-done((f32[4,16,648]{2,1,0:T(8,128)S(1)}, f32[4,16,648]{2,1,0:T(8,128)S(1)}, u32[]{:S(2)}, u32[]{:S(2)}) %collective-permute-start.1) | collective-permute-done | bytes 165920 | tf_op jit(solution)/shard_map/ppermute | solution.py:188
  76.9 4.0 %chebyshev.1 = f32[8,16,648]{2,1,0:T(8,128)S(1)} custom-call(s32[1]{0:T(128)} %bitcast.last_ref, f32[8,16,648]{2,1,0:T(8,128)S(1)} %bitcast.33, f32[4,16,648]{2,1,0:T(8,128)S(1)} %collective-permute-done.left_ref, f32[4,16,648]{2,1,0:T(8,128)S(1)} %collective-permute-done.1.right_ref, f32[8,128]{1,0:T(8,128)S(1)} %slice.29.scale_ref, ...), custom_call_target="tpu_custom_call" | custom-call | tf_op jit(solution)/shard_map/chebyshev/pallas_call | solution.py:198
  81.0 20.3 %all_to_all.36 = f32[8,16,648]{2,1,0:T(8,128)S(1)} all-to-all(f32[8,16,648]{2,1,0:T(8,128)S(1)} %chebyshev.1), channel_id=1, replica_groups=mesh['dom'=64,'band'=8] {'band'}, dimensions={0} | all-to-all | bytes 663552 | tf_op jit(solution)/shard_map/all_to_all | solution.py:25
  101.2 0.2 dot_general.5
  101.5 0.5 fusion
  102.0 14.8 %all_to_all.37 = f32[64,2,128]{2,1,0:T(2,128)S(1)} all-to-all(f32[64,2,128]{2,1,0:T(2,128)S(1)} %copy.33), channel_id=1, replica_groups=mesh['dom'=64,'band'=8] {'dom'}, dimensions={0} | all-to-all | bytes 131072 | tf_op jit(solution)/shard_map/all_to_all | solution.py:25
  116.9 11.7 %all_to_all.38 = f32[8,2,128]{2,1,0:T(2,128)S(1)} all-to-all(f32[8,2,128]{2,1,0:T(2,128)S(1)} %broadcast_in_dim.14), channel_id=1, replica_groups=mesh['dom'=64,'band'=8] {'band'}, dimensions={0} | all-to-all | bytes 16384 | tf_op jit(solution)/shard_map/all_to_all | solution.py:25
  128.6 13.1 %all_to_all.39 = f32[64,2,128]{2,1,0:T(2,128)S(1)} all-to-all(f32[64,2,128]{2,1,0:T(2,128)S(1)} %broadcast_in_dim.15), channel_id=1, replica_groups=mesh['dom'=64,'band'=8] {'dom'}, dimensions={0} | all-to-all | bytes 131072 | tf_op jit(solution)/shard_map/all_to_all | solution.py:25
  141.7 0.1 copy.35
  141.8 11.7 %cholesky.16 = f32[128,128]{1,0:T(8,128)S(1)} custom-call(f32[128,128]{1,0:T(8,128)S(1)} %fusion.4), custom_call_target="Cholesky" | custom-call | tf_op jit(solution)/shard_map/jit(cholesky)/cholesky | solution.py:226
  153.6 0.6 compare_reduce_fusion
  154.2 0.7 fusion.2
  154.9 9.8 %custom-call.7 = f32[1,128,128]{1,2,0:T(8,128)S(1)} custom-call(f32[1,128,128]{2,1,0:T(8,128)S(1)} %fusion.2), custom_call_target="InvertDiagBlocksLowerTriangular" | custom-call | tf_op jit(solution)/shard_map/jit(_solve_triangular)/triangular_solve | solution.py:227
  164.7 1.5 convolution_bitcast_fusion
  (23 shorter events, 0.6 us)
Async XLA Ops:
  4.2 10.8 %collective-permute-start.2 = (f32[544,384]{1,0:T(8,128)S(1)}, f32[544,384]{1,0:T(8,128)S(1)}, u32[]{:S(2)}, u32[]{:S(2)}) collective-permute-start(f32[544,384]{1,0:T(8,128)S(1)} %get-tuple-element.8), channel_id=1, source_target_pairs={{0,1},{1,0},{2,3},{3,2},{4,5},{5,4},{6,7},{7,6},{8,9},{9,8},{10,11... | collective-permute-start | bytes 2506760 | tf_op jit(solution)/shard_map/ppermute | solution.py:182
  15.0 20.6 %copy-start.1 = (f32[16,8,648]{2,1,0:T(8,128)S(1)}, f32[16,8,648]{2,1,0:T(8,128)}, u32[]{:S(2)}) copy-start(f32[16,8,648]{2,1,0:T(8,128)} %param.6) | copy-start | bytes 995332
  29.9 31.4 %copy-start.2 = (f32[8]{0:T(128)S(1)}, f32[8]{0:T(128)}, u32[]{:S(2)}) copy-start(f32[8]{0:T(128)} %param.8) | copy-start | bytes 100
  30.7 46.2 %copy-start = (f32[729,729]{1,0:T(8,128)S(1)}, f32[729,729]{1,0:T(8,128)}, u32[]{:S(2)}) copy-start(f32[729,729]{1,0:T(8,128)} %operator_ref.1) | copy-start | bytes 6377296
  30.7 17.0 %all-to-all-start.1 = ((f32[16,16,384]{2,1,0:T(8,128)}), f32[16,16,384]{2,1,0:T(8,128)S(1)}, u32[]{:S(2)}, u32[]{:S(2)}) async-start(f32[16,16,384]{2,1,0:T(8,128)} %pad_maximum_fusion), calls=%async_computation.1 | async-start | bytes 786432 | tf_op jit(solution)/shard_map/all_to_all | solution.py:25
  48.4 21.6 %all-to-all-start.2 = ((f32[8,16,384]{2,1,0:T(8,128)}), f32[8,16,384]{2,1,0:T(8,128)S(1)}, u32[]{:S(2)}, u32[]{:S(2)}) async-start(f32[8,16,384]{2,1,0:T(8,128)} %broadcast_in_dim.13), calls=%async_computation.2 | async-start | bytes 393216 | tf_op jit(solution)/shard_map/all_to_all | solution.py:25
  62.1 12.7 %collective-permute-start = (f32[4,16,648]{2,1,0:T(8,128)}, f32[4,16,648]{2,1,0:T(8,128)S(1)}, u32[]{:S(2)}, u32[]{:S(2)}) collective-permute-start(f32[4,16,648]{2,1,0:T(8,128)} %get-tuple-element.14), channel_id=1, source_target_pairs={{0,8},{8,16},{16,24},{24,32},{32,40},{40,48},{48,56},{56,64},{64,7... | collective-permute-start | bytes 497672 | tf_op jit(solution)/shard_map/ppermute | solution.py:187
  64.2 12.7 %collective-permute-start.1 = (f32[4,16,648]{2,1,0:T(8,128)S(1)}, f32[4,16,648]{2,1,0:T(8,128)S(1)}, u32[]{:S(2)}, u32[]{:S(2)}) collective-permute-start(f32[4,16,648]{2,1,0:T(8,128)S(1)} %get-tuple-element.13), channel_id=1, source_target_pairs={{8,0},{16,8},{24,16},{32,24},{40,32},{48,40},{56,48},{64,56},{72,6... | collective-permute-start | bytes 497672 | tf_op jit(solution)/shard_map/ppermute | solution.py:188

commit v2 on v1

--- a/solution.py
+++ b/solution.py
@@ -1,3 +1,5 @@
+import functools
+
 import jax
 import jax.numpy as jnp
 from jax import lax
@@ -19,6 +21,7 @@
 
 X_GROUPS = [[x * 16 + r for x in range(4)] for r in range(16)]
 YZ_GROUPS = [[x * 16 + r for r in range(16)] for x in range(4)]
+XB_GROUPS = [[(x * 16 + r) * 8 + b for x in range(4) for b in range(8)] for r in range(16)]
 
 
 def exchange(value, axis, groups=None):
@@ -35,22 +38,26 @@
     return jnp.dot(a, b, preferred_element_type=jnp.float32)
 
 
-def deliver_kernel(core_ref, target_ref, density_ref, mine_ref, theirs_ref, wide_ref):
+def dot_nt(a, b):
+    return lax.dot_general(a, b, (((1,), (1,)), ((), ())), preferred_element_type=jnp.float32)
+
+
+def deliver_kernel(core_ref, owner_ref, cell_ref, density_ref, mine_ref, theirs_ref, wide_ref):
     rows = 4 * SLAB
-    count = density_ref.shape[0]
-    wide_ref[:, TILE5:] = jnp.zeros((count, WIDE - TILE5), jnp.float32)
-    wide_ref[:, :NODES] = density_ref[...]
+    count = density_ref.shape[1]
+    wide_ref[720:, :] = jnp.zeros((WIDE - 720, count), jnp.float32)
+    wide_ref[:NODES, :] = density_ref[...]
     row = lax.broadcasted_iota(jnp.int32, (rows, count), 0)
     slab = (row >= SLAB).astype(jnp.int32) + (row >= 2 * SLAB).astype(jnp.int32) + (row >= 3 * SLAB).astype(jnp.int32)
     cell = row - 8 * slab - 3
-    onehot = jnp.where(target_ref[...] == cell, 1.0, 0.0).astype(jnp.bfloat16)
+    onehot = jnp.where(owner_ref[...] * 8 + cell_ref[...] == cell, 1.0, 0.0).astype(jnp.bfloat16)
     for half in range(2):
-        values = wide_ref[:, half * HALF:(half + 1) * HALF]
+        values = wide_ref[half * HALF:(half + 1) * HALF, :]
         first = values.astype(jnp.bfloat16)
         rest = values - first.astype(jnp.float32)
         second = rest.astype(jnp.bfloat16)
         third = (rest - second.astype(jnp.float32)).astype(jnp.bfloat16)
-        total = dot(onehot, first) + dot(onehot, second) + dot(onehot, third)
+        total = dot_nt(onehot, first) + dot_nt(onehot, second) + dot_nt(onehot, third)
 
         @pl.when(core_ref[0] == half)
         def _():
@@ -61,8 +68,20 @@
             theirs_ref[...] = total
 
 
-def filter_kernel(last_ref, own_ref, left_ref, right_ref, scale_ref, rho_ref, operator_ref, out_ref,
-                  kwide, khigh, klow, v0, v1, v2, chigh, clow, cell_buf, product, pot):
+def prepare_kernel(scale_ref, orbitals_ref, operator_ref, cells_ref, left_ref, right_ref, khigh, klow, kwide):
+    for c in range(8):
+        value = orbitals_ref[:, c, :]
+        cells_ref[c] = value
+        if c >= 5:
+            left_ref[c - 5] = value
+        if c < 3:
+            right_ref[c] = value
+    for c in range(8):
+        line = jnp.full((1, OWN), scale_ref[c], jnp.float32)
+        left_ref[3, c:c + 1, :] = line
+        right_ref[3, c:c + 1, :] = line
+    left_ref[3, 8:, :] = jnp.zeros((8, OWN), jnp.float32)
+    right_ref[3, 8:, :] = jnp.zeros((8, OWN), jnp.float32)
     kwide[720:, :] = jnp.zeros((WIDE - 720, WIDE), jnp.float32)
     kwide[:, TILE5:] = jnp.zeros((WIDE, WIDE - TILE5), jnp.float32)
     kwide[:NODES, :NODES] = operator_ref[...]
@@ -70,6 +89,10 @@
         high, low = split2(kwide[i:i + 128, :])
         khigh[i:i + 128, :] = high
         klow[i:i + 128, :] = low
+
+
+def filter_kernel(last_ref, scale_ref, own_ref, left_ref, right_ref, rho_ref, khigh, klow, out_ref,
+                  v0, v1, v2, chigh, clow, cell_buf, product, pot):
     for half in range(2):
         rho = rho_ref[half]
         pot[:, half * HALF:(half + 1) * HALF] = jnp.where(
@@ -93,7 +116,7 @@
         if i < 3:
             line = left_ref[3, 5 + i:6 + i, :128]
         elif i < 11:
-            line = scale_ref[i - 3:i - 2, :]
+            line = scale_ref[i - 3]
         else:
             line = right_ref[3, i - 11:i - 10, :128]
         return line
@@ -158,6 +181,80 @@
     apply(v2, 2, 11, third)
 
 
+def solve_kernel(total, gram_ref, flat_ref, out_ref, inverse_ref):
+    shape = (8, 128)
+    col = lax.broadcasted_iota(jnp.int32, shape, 1)
+    row = lax.broadcasted_iota(jnp.int32, shape, 0)
+    a = [gram_ref[8 * i:8 * i + 8, :] * (1.0 / total) for i in range(16)]
+    w = [jnp.where(col == row + 8 * i, 1.0, 0.0) for i in range(16)]
+
+    def columns(block, k):
+        return [jnp.broadcast_to(block[:, 8 * k + j:8 * k + j + 1], shape) for j in range(8)]
+
+    def line(block, i):
+        return jnp.broadcast_to(block[i:i + 1, :], shape)
+
+    for k in range(16):
+        own = columns(a[k], k)
+        s = [[line(own[j], i) for j in range(i + 1)] for i in range(8)]
+        low = [[None] * 8 for _ in range(8)]
+        inv = [None] * 8
+        for j in range(8):
+            inv[j] = 1.0 / s[j][j]
+            for i in range(j + 1, 8):
+                low[i][j] = s[i][j] * inv[j]
+            for i in range(j + 1, 8):
+                for m in range(j + 1, i + 1):
+                    s[i][m] = s[i][m] - low[i][j] * s[m][j]
+        n = [[None] * 8 for _ in range(8)]
+        for i in range(8):
+            for j in range(i):
+                value = low[i][j]
+                for m in range(j + 1, i):
+                    value = value + low[i][m] * n[m][j]
+                n[i][j] = -value
+
+        def forward(block):
+            lines = [line(block, i) for i in range(8)]
+            result = []
+            for i in range(8):
+                value = lines[i]
+                for j in range(i):
+                    value = value + n[i][j] * lines[j]
+                result.append(value)
+            return result
+
+        def backward(lines):
+            scaled = [inv[i] * lines[i] for i in range(8)]
+            result = []
+            for j in range(8):
+                value = scaled[j]
+                for i in range(j + 1, 8):
+                    value = value + n[i][j] * scaled[i]
+                result.append(value)
+            return result
+
+        lines_w = forward(w[k])
+        final = jnp.zeros(shape, jnp.float32)
+        for i in range(8):
+            final = jnp.where(row == i, lines_w[i] * jnp.sqrt(inv[i]), final)
+        inverse_ref[8 * k:8 * k + 8, :] = final
+        if k < 15:
+            za = backward(forward(a[k]))
+            zw = backward(lines_w)
+            for i in range(k + 1, 16):
+                c = columns(a[i], k)
+                for j in range(8):
+                    a[i] = a[i] - c[j] * za[j]
+                    w[i] = w[i] - c[j] * zw[j]
+    inverse_high, inverse_low = split2(inverse_ref[...])
+    for begin in range(0, OWN, 128):
+        c = slice(begin, min(begin + 128, OWN))
+        flat_high, flat_low = split2(jnp.transpose(flat_ref[:, c]))
+        out_ref[c, :] = (dot_nt(flat_high, inverse_high) + dot_nt(flat_low, inverse_high)
+                         + dot_nt(flat_high, inverse_low))
+
+
 def body(orbitals, cell_operator, cell_scale, density, block_owner, block_cell):
     dom_count = lax.axis_size("dom")
     band_count = lax.axis_size("band")
@@ -168,42 +265,47 @@
     vmem = pl.BlockSpec(memory_space=pltpu.VMEM)
     params = pltpu.CompilerParams(vmem_limit_bytes=48 << 20)
 
-    target = (block_owner[:, 0] * 8 + block_cell).reshape(1, -1)
     half_shape = jax.ShapeDtypeStruct((4 * SLAB, HALF), jnp.float32)
     mine, theirs = pl.pallas_call(
         deliver_kernel,
         out_shape=(half_shape, half_shape),
-        in_specs=[smem, vmem, vmem],
+        in_specs=[smem, vmem, vmem, vmem],
         out_specs=(vmem, vmem),
-        scratch_shapes=[pltpu.VMEM((density.shape[0], WIDE), jnp.float32)],
+        scratch_shapes=[pltpu.VMEM((WIDE, density.shape[0]), jnp.float32)],
         compiler_params=params,
         name="deliver",
-    )(core, target, density)
+    )(core, block_owner.reshape(1, -1), block_cell.reshape(1, -1), density.T)
     other = lax.ppermute(theirs, "band", [(i, i ^ 1) for i in range(band_count)])
 
-    cells = jnp.transpose(orbitals, (1, 0, 2))
-    scales = jnp.broadcast_to(cell_scale[:, None], (8, OWN))
-    scales16 = jnp.concatenate([scales, scales], 0)[None]
-    left = lax.ppermute(jnp.concatenate([cells[5:], scales16], 0), "dom", [(i, i + 1) for i in range(dom_count - 1)])
-    right = lax.ppermute(jnp.concatenate([cells[:3], scales16], 0), "dom", [(i + 1, i) for i in range(dom_count - 1)])
+    ghost_shape = jax.ShapeDtypeStruct((4, 16, OWN), jnp.float32)
+    split_shape = jax.ShapeDtypeStruct((WIDE, WIDE), jnp.bfloat16)
+    cells, send_left, send_right, khigh, klow = pl.pallas_call(
+        prepare_kernel,
+        out_shape=(jax.ShapeDtypeStruct((8, 16, OWN), jnp.float32), ghost_shape, ghost_shape, split_shape, split_shape),
+        in_specs=[smem, vmem, vmem],
+        out_specs=(vmem,) * 5,
+        scratch_shapes=[pltpu.VMEM((WIDE, WIDE), jnp.float32)],
+        compiler_params=params,
+        name="prepare",
+    )(cell_scale, orbitals, cell_operator)
+    left = lax.ppermute(send_left, "dom", [(i, i + 1) for i in range(dom_count - 1)])
+    right = lax.ppermute(send_right, "dom", [(i + 1, i) for i in range(dom_count - 1)])
 
     part = exchange((mine + other).reshape(4, SLAB, HALF), "dom", X_GROUPS)
     slab = jnp.sum(part, 0)
     windows = jnp.concatenate([slab[:128].reshape(16, 8, HALF), slab[8:].reshape(16, 8, HALF)], 1)
     part = exchange(windows, "dom", YZ_GROUPS)
     window = jnp.sum(part, 0)
+    window, left, right = lax.optimization_barrier((window, left, right))
     part = exchange(jnp.broadcast_to(window[None], (band_count, 16, HALF)), "band")
     rho = jnp.sum(part.reshape(4, 2, 16, HALF), 0)
 
     filtered = pl.pallas_call(
         filter_kernel,
         out_shape=jax.ShapeDtypeStruct((8, 16, OWN), jnp.float32),
-        in_specs=[smem] + [vmem] * 6,
+        in_specs=[smem] * 2 + [vmem] * 6,
         out_specs=vmem,
         scratch_shapes=[
-            pltpu.VMEM((WIDE, WIDE), jnp.float32),
-            pltpu.VMEM((WIDE, WIDE), jnp.bfloat16),
-            pltpu.VMEM((WIDE, WIDE), jnp.bfloat16),
             pltpu.VMEM((224, WIDE), jnp.float32),
             pltpu.VMEM((224, WIDE), jnp.float32),
             pltpu.VMEM((224, WIDE), jnp.float32),
@@ -215,17 +317,24 @@
         ],
         compiler_params=params,
         name="chebyshev",
-    )(alive, cells, left, right, scales[:, :128], rho, cell_operator)
+    )(alive, cell_scale, cells, left, right, rho, khigh, klow)
 
     flat = exchange(filtered, "band").reshape(128, OWN)
     total = OWN * dom_count * band_count
     gram = jnp.dot(flat, flat.T, precision=lax.Precision.HIGHEST)
-    part = jnp.sum(exchange(gram.reshape(dom_count, 2, 128), "dom"), 0)
-    part = jnp.sum(exchange(jnp.broadcast_to(part[None], (band_count, 2, 128)), "band"), 0)
-    intersection = exchange(jnp.broadcast_to(part[None], (dom_count, 2, 128)), "dom").reshape(128, 128) / total
-    lower = jnp.linalg.cholesky(intersection)
-    basis = jax.scipy.linalg.solve_triangular(lower, flat, lower=True)
-    return basis.reshape(128, 1, OWN)
+    part = jnp.sum(exchange(gram.reshape(16, 8, 128), "dom", YZ_GROUPS), 0)
+    part = jnp.sum(exchange(jnp.broadcast_to(part[None], (32, 8, 128)), ("dom", "band"), XB_GROUPS), 0)
+    gram = exchange(jnp.broadcast_to(part[None], (16, 8, 128)), "dom", YZ_GROUPS).reshape(128, 128)
+    basis = pl.pallas_call(
+        functools.partial(solve_kernel, float(total)),
+        out_shape=jax.ShapeDtypeStruct((OWN, 128), jnp.float32),
+        in_specs=[vmem, vmem],
+        out_specs=vmem,
+        scratch_shapes=[pltpu.VMEM((128, 128), jnp.float32)],
+        compiler_params=params,
+        name="orthonormalize",
+    )(gram, flat)
+    return basis.T.reshape(128, 1, OWN)
 
 
 def solution(mesh):

time: 167 us -> 146 us (0.87)
  other arithmetic: 26 us -> 2.03 us
  Pallas kernels: 5.44 us -> 13.3 us
  local copies, waits for them, and re-layouts: 2.8 us -> 6.98 us
  waiting for transfers between devices: 25.3 us -> 22.1 us
  blocking collectives: 74.6 us -> 71.8 us
    another operation x5 -> x0, other arithmetic: 22.9 us -> none  [the longest x3 12.4 us: body(): lower = jnp.linalg.cholesky(intersection)]
    pallas_call x0 -> x2, Pallas kernels: none -> 7.57 us  [the longest x1 6.11 us: body(): pl.pallas_call(functools.partial(solve_kernel, float(total)), out_shape=j...]
    unnamed x8 -> x20, local copies, waits for them, and re-layouts: 1.53 us -> 6.24 us
    all_to_all x2, waiting for transfers between devices: 16.5 us -> 12.7 us  [exchange(): lax.all_to_all(value, axis, split_axis=0, concat_axis=0, tiled=True, axis...]
    all_to_all x5, blocking collectives: 74.6 us -> 71.8 us  [exchange(): lax.all_to_all(value, axis, split_axis=0, concat_axis=0, tiled=True, axis...]
    all_to_all x2, starting transfers between devices: 17.8 us -> 15.1 us  [exchange(): lax.all_to_all(value, axis, split_axis=0, concat_axis=0, tiled=True, axis...]
  transfers between devices with their start and end apart: 5 -> 5, of which waited for: 5 -> 5; matrix products, arithmetic and copies ran while one was open for 1% -> 1% of each run, Pallas kernels for 0% -> 1%
where the time goes in v2:
time: 146 us; the launch traced here: 145 us
  blocking collectives  71.8 us (49%)
  starting transfers between devices  28.6 us (20%)
  waiting for transfers between devices  22.1 us (15%)
  Pallas kernels  13.3 us (9%)
  local copies, waits for them, and re-layouts  6.98 us (5%)
  other arithmetic  2.03 us (1%)
    all_to_all x5, blocking collectives, exchange(): lax.all_to_all(value, axis, split_axis=0, concat_axis=0, tiled=True, axis...  71.8 us
    all_to_all x2, starting transfers between devices, exchange(): lax.all_to_all(value, axis, split_axis=0, concat_axis=0, tiled=True, axis...  15.1 us
    all_to_all x2, waiting for transfers between devices, exchange(): lax.all_to_all(value, axis, split_axis=0, concat_axis=0, tiled=True, axis...  12.7 us
    ppermute x1, starting transfers between devices, body(): lax.ppermute(theirs, 'band', [(i, i ^ 1) for i in range(band_count)])  8.79 us
    unnamed x20, local copies, waits for them, and re-layouts  6.24 us
    pallas_call x1, Pallas kernels, body(): pl.pallas_call(functools.partial(solve_kernel, float(total)), out_shape=j...  6.11 us
    ppermute x1, waiting for transfers between devices, body(): lax.ppermute(send_right, 'dom', [(i + 1, i) for i in range(dom_count - 1)])  5.55 us
    pallas_call x1, Pallas kernels, body(): pl.pallas_call(filter_kernel, out_shape=jax.ShapeDtypeStruct((8, 16, OWN)...  4.38 us
  transfers between devices with their start and end apart: 5, of which 5 were waited for; matrix products, arithmetic and copies ran while one was open for 1% of the time, Pallas kernels for 1%

profile of v2, /device:TPU:1, one launch (start us, length us, event | category | flops | bytes accessed | tf_op | source)
XLA Modules:
  0.0 145.5 jit_solution(6265055469460423178)
XLA Ops:
  0.0 1.1 copy-done.3
  1.1 0.7 copy-done.8
  1.8 0.7 copy-done.9
  2.5 1.4 deliver.1
  3.9 8.8 %collective-permute-start = (f32[544,384]{1,0:T(8,128)S(1)}, f32[544,384]{1,0:T(8,128)S(1)}, u32[]{:S(2)}, u32[]{:S(2)}) collective-permute-start(f32[544,384]{1,0:T(8,128)S(1)} %get-tuple-element.17), channel_id=1, source_target_pairs={{0,1},{1,0},{2,3},{3,2},{4,5},{5,4},{6,7},{7,6},{8,9},{9,8},{10,11... | collective-permute-start | bytes 2506760 | tf_op jit(solution)/shard_map/ppermute | solution.py:278
  12.7 2.0 %collective-permute-done = f32[544,384]{1,0:T(8,128)S(1)} collective-permute-done((f32[544,384]{1,0:T(8,128)S(1)}, f32[544,384]{1,0:T(8,128)S(1)}, u32[]{:S(2)}, u32[]{:S(2)}) %collective-permute-start) | collective-permute-done | bytes 835616 | tf_op jit(solution)/shard_map/ppermute | solution.py:278
  14.6 0.1 add.8
  14.7 14.7 %all_to_all.35 = f32[4,136,384]{2,1,0:T(8,128)S(1)} all-to-all(f32[4,136,384]{2,1,0:T(8,128)S(1)} %bitcast.28), channel_id=1, replica_groups={{0,128,256,384},{8,136,264,392},{16,144,272,400},{24,152,280,408},{32,1..., dimensions={0} | all-to-all | bytes 1671168 | tf_op jit(solution)/shard_map/all_to_all | solution.py:28
  29.4 0.0 copy-start.7
  29.5 0.8 pad_maximum_fusion
  30.3 4.8 %all-to-all-start.1 = ((f32[16,16,384]{2,1,0:T(8,128)}), f32[16,16,384]{2,1,0:T(8,128)}, u32[]{:S(2)}, u32[]{:S(2)}) async-start(f32[16,16,384]{2,1,0:T(8,128)} %pad_maximum_fusion), calls=%async_computation.1 | async-start | bytes 786432 | tf_op jit(solution)/shard_map/all_to_all | solution.py:28
  35.1 1.0 copy-done.4
  36.1 1.5 %prepare.1 = (f32[8,16,648]{2,1,0:T(8,128)S(1)}, f32[4,16,648]{2,1,0:T(8,128)}, f32[4,16,648]{2,1,0:T(8,128)}, bf16[768,768]{1,0:T(8,128)(2,1)S(1)}, bf16[768,768]{1,0:T(8,128)(2,1)S(1)}) custom-call(f32[8]{0:T(128)S(1)} %copy-done.7, f32[16,8,648]{2,1,0:T(8,128)S(1)} %copy-done.4, f32[729,729]{1,0:T(8,128)S(1)} %copy-done), custom_call_target="tpu_custom_call" | custom-call | tf_op jit(solution)/shard_map/prepare/pallas_call | solution.py:282
  37.6 1.0 copy-done.1
  38.6 0.8 copy-done.5
  39.4 3.4 %collective-permute-start.1 = (f32[4,16,648]{2,1,0:T(8,128)}, f32[4,16,648]{2,1,0:T(8,128)S(1)}, u32[]{:S(2)}, u32[]{:S(2)}) collective-permute-start(f32[4,16,648]{2,1,0:T(8,128)} %get-tuple-element.18), channel_id=1, source_target_pairs={{0,8},{8,16},{16,24},{24,32},{32,40},{40,48},{48,56},{56,64},{64,7... | collective-permute-start | bytes 497672 | tf_op jit(solution)/shard_map/ppermute | solution.py:291
  42.7 1.3 collective-permute-start.2
  44.0 3.4 %all-to-all-done.1 = f32[16,16,384]{2,1,0:T(8,128)} async-done(((f32[16,16,384]{2,1,0:T(8,128)}), f32[16,16,384]{2,1,0:T(8,128)}, u32[]{:S(2)}, u32[]{:S(2)}) %all-to-all-start.1) | async-done | bytes 393248 | tf_op jit(solution)/shard_map/all_to_all | solution.py:28
  47.4 1.0 reduce_sum.46
  48.4 1.9 %collective-permute-done.1.left_ref = f32[4,16,648]{2,1,0:T(8,128)S(1)} collective-permute-done((f32[4,16,648]{2,1,0:T(8,128)}, f32[4,16,648]{2,1,0:T(8,128)S(1)}, u32[]{:S(2)}, u32[]{:S(2)}) %collective-permute-start.1) | collective-permute-done | bytes 165920 | tf_op jit(solution)/shard_map/ppermute | solution.py:291
  50.3 5.5 %collective-permute-done.2.right_ref = f32[4,16,648]{2,1,0:T(8,128)S(1)} collective-permute-done((f32[4,16,648]{2,1,0:T(8,128)}, f32[4,16,648]{2,1,0:T(8,128)S(1)}, u32[]{:S(2)}, u32[]{:S(2)}) %collective-permute-start.2) | collective-permute-done | bytes 165920 | tf_op jit(solution)/shard_map/ppermute | solution.py:292
  55.9 0.7 broadcast_in_dim.6
  56.6 10.3 %all-to-all-start.2 = ((f32[8,16,384]{2,1,0:T(8,128)}), f32[8,16,384]{2,1,0:T(8,128)S(1)}, u32[]{:S(2)}, u32[]{:S(2)}) async-start(f32[8,16,384]{2,1,0:T(8,128)} %broadcast_in_dim.6), calls=%async_computation.2 | async-start | bytes 393216 | tf_op jit(solution)/shard_map/all_to_all | solution.py:28
  66.9 9.3 %all-to-all-done.2 = f32[8,16,384]{2,1,0:T(8,128)S(1)} async-done(((f32[8,16,384]{2,1,0:T(8,128)}), f32[8,16,384]{2,1,0:T(8,128)S(1)}, u32[]{:S(2)}, u32[]{:S(2)}) %all-to-all-start.2) | async-done | bytes 196640 | tf_op jit(solution)/shard_map/all_to_all | solution.py:28
  76.3 1.0 copy-done.6
  77.3 4.4 %chebyshev.1 = f32[8,16,648]{2,1,0:T(8,128)S(1)} custom-call(s32[1]{0:T(128)} %bitcast.last_ref, f32[8]{0:T(128)S(1)} %copy-done.7, f32[8,16,648]{2,1,0:T(8,128)S(1)} %copy-done.6, f32[4,16,648]{2,1,0:T(8,128)S(1)} %collective-permute-done.1.left_ref, f32[4,16,648]{2,1,0:T(8,128)S(1)} %collective-permute-done.2.right_ref, ...), custom_call_target="tpu_custom_call" | custom-call | tf_op jit(solution)/shard_map/chebyshev/pallas_call | solution.py:303
  81.7 17.0 %all_to_all.36 = f32[8,16,648]{2,1,0:T(8,128)S(1)} all-to-all(f32[8,16,648]{2,1,0:T(8,128)S(1)} %chebyshev.1), channel_id=1, replica_groups=mesh['dom'=64,'band'=8] {'band'}, dimensions={0} | all-to-all | bytes 663552 | tf_op jit(solution)/shard_map/all_to_all | solution.py:28
  98.6 0.5 fusion
  99.1 12.8 %all_to_all.37 = f32[16,8,128]{2,1,0:T(8,128)S(1)} all-to-all(f32[16,8,128]{2,1,0:T(8,128)S(1)} %fusion), channel_id=1, replica_groups={{0,8,16,24,32,40,48,56,64,72,80,88,96,104,112,120},{128,136,144,152,160..., dimensions={0} | all-to-all | bytes 131072 | tf_op jit(solution)/shard_map/all_to_all | solution.py:28
  111.9 16.9 %all_to_all.38 = f32[32,8,128]{2,1,0:T(8,128)S(1)} all-to-all(f32[32,8,128]{2,1,0:T(8,128)S(1)} %broadcast_in_dim.7), channel_id=1, replica_groups={{0,1,2,3,4,5,6,7,128,129,130,131,132,133,134,135,256,257,258,259,260,26..., dimensions={0} | all-to-all | bytes 262144 | tf_op jit(solution)/shard_map/all_to_all | solution.py:28
  128.8 10.5 %all_to_all.39 = f32[16,8,128]{2,1,0:T(8,128)S(1)} all-to-all(f32[16,8,128]{2,1,0:T(8,128)S(1)} %broadcast_in_dim.8), channel_id=1, replica_groups={{0,8,16,24,32,40,48,56,64,72,80,88,96,104,112,120},{128,136,144,152,160..., dimensions={0} | all-to-all | bytes 131072 | tf_op jit(solution)/shard_map/all_to_all | solution.py:28
  139.3 6.1 %orthonormalize.1 = f32[648,128]{1,0:T(8,128)} custom-call(f32[128,128]{1,0:T(8,128)S(1)} %bitcast.25, f32[128,648]{1,0:T(8,128)S(1)} %bitcast.23), custom_call_target="tpu_custom_call" | custom-call | tf_op jit(solution)/shard_map/orthonormalize/pallas_call | solution.py:328
  (19 shorter events, 0.2 us)
Async XLA Ops:
  0.0 1.1 copy-start.3
  1.1 0.7 copy-start.8
  1.8 0.7 copy-start.9
  3.9 10.8 %collective-permute-start = (f32[544,384]{1,0:T(8,128)S(1)}, f32[544,384]{1,0:T(8,128)S(1)}, u32[]{:S(2)}, u32[]{:S(2)}) collective-permute-start(f32[544,384]{1,0:T(8,128)S(1)} %get-tuple-element.17), channel_id=1, source_target_pairs={{0,1},{1,0},{2,3},{3,2},{4,5},{5,4},{6,7},{7,6},{8,9},{9,8},{10,11... | collective-permute-start | bytes 2506760 | tf_op jit(solution)/shard_map/ppermute | solution.py:278
  29.4 5.7 %copy-start = (f32[729,729]{1,0:T(8,128)S(1)}, f32[729,729]{1,0:T(8,128)}, u32[]{:S(2)}) copy-start(f32[729,729]{1,0:T(8,128)} %operator_ref.1) | copy-start | bytes 6377296
  29.4 5.7 %copy-start.7 = (f32[8]{0:T(128)S(1)}, f32[8]{0:T(128)}, u32[]{:S(2)}) copy-start(f32[8]{0:T(128)} %scale_ref.3) | copy-start | bytes 100
  30.3 17.1 %all-to-all-start.1 = ((f32[16,16,384]{2,1,0:T(8,128)}), f32[16,16,384]{2,1,0:T(8,128)}, u32[]{:S(2)}, u32[]{:S(2)}) async-start(f32[16,16,384]{2,1,0:T(8,128)} %pad_maximum_fusion), calls=%async_computation.1 | async-start | bytes 786432 | tf_op jit(solution)/shard_map/all_to_all | solution.py:28
  35.1 1.0 copy-start.4
  37.6 1.0 copy-start.1
  38.6 0.8 copy-start.5
  39.4 36.9 %copy-start.2 = (bf16[768,768]{1,0:T(8,128)(2,1)S(1)}, bf16[768,768]{1,0:T(8,128)(2,1)}, u32[]{:S(2)}) copy-start(bf16[768,768]{1,0:T(8,128)(2,1)} %copy-done.1) | copy-start | bytes 3538948
  39.4 11.0 %collective-permute-start.1 = (f32[4,16,648]{2,1,0:T(8,128)}, f32[4,16,648]{2,1,0:T(8,128)S(1)}, u32[]{:S(2)}, u32[]{:S(2)}) collective-permute-start(f32[4,16,648]{2,1,0:T(8,128)} %get-tuple-element.18), channel_id=1, source_target_pairs={{0,8},{8,16},{16,24},{24,32},{32,40},{40,48},{48,56},{56,64},{64,7... | collective-permute-start | bytes 497672 | tf_op jit(solution)/shard_map/ppermute | solution.py:291
  42.7 13.2 %collective-permute-start.2 = (f32[4,16,648]{2,1,0:T(8,128)}, f32[4,16,648]{2,1,0:T(8,128)S(1)}, u32[]{:S(2)}, u32[]{:S(2)}) collective-permute-start(f32[4,16,648]{2,1,0:T(8,128)} %get-tuple-element.19), channel_id=1, source_target_pairs={{8,0},{16,8},{24,16},{32,24},{40,32},{48,40},{56,48},{64,56},{72,6... | collective-permute-start | bytes 497672 | tf_op jit(solution)/shard_map/ppermute | solution.py:292
  56.6 19.7 %all-to-all-start.2 = ((f32[8,16,384]{2,1,0:T(8,128)}), f32[8,16,384]{2,1,0:T(8,128)S(1)}, u32[]{:S(2)}, u32[]{:S(2)}) async-start(f32[8,16,384]{2,1,0:T(8,128)} %broadcast_in_dim.6), calls=%async_computation.2 | async-start | bytes 393216 | tf_op jit(solution)/shard_map/all_to_all | solution.py:28
  76.3 1.0 copy-start.6

commit v3 on v2

--- a/solution.py
+++ b/solution.py
@@ -42,10 +42,20 @@
     return lax.dot_general(a, b, (((1,), (1,)), ((), ())), preferred_element_type=jnp.float32)
 
 
-def deliver_kernel(core_ref, owner_ref, cell_ref, density_ref, mine_ref, theirs_ref, wide_ref):
+def deliver_kernel(core_ref, owner_hbm, cell_hbm, density_hbm, mine_ref, theirs_ref,
+                   owner_ref, cell_ref, density_ref, wide_ref, sems):
     rows = 4 * SLAB
     count = density_ref.shape[1]
+    copies = [
+        pltpu.make_async_copy(density_hbm, density_ref, sems.at[0]),
+        pltpu.make_async_copy(owner_hbm, owner_ref, sems.at[1]),
+        pltpu.make_async_copy(cell_hbm, cell_ref, sems.at[2]),
+    ]
+    for copy in copies:
+        copy.start()
     wide_ref[720:, :] = jnp.zeros((WIDE - 720, count), jnp.float32)
+    for copy in copies:
+        copy.wait()
     wide_ref[:NODES, :] = density_ref[...]
     row = lax.broadcasted_iota(jnp.int32, (rows, count), 0)
     slab = (row >= SLAB).astype(jnp.int32) + (row >= 2 * SLAB).astype(jnp.int32) + (row >= 3 * SLAB).astype(jnp.int32)
@@ -68,14 +78,10 @@
             theirs_ref[...] = total
 
 
-def prepare_kernel(scale_ref, orbitals_ref, operator_ref, cells_ref, left_ref, right_ref, khigh, klow, kwide):
-    for c in range(8):
-        value = orbitals_ref[:, c, :]
-        cells_ref[c] = value
-        if c >= 5:
-            left_ref[c - 5] = value
-        if c < 3:
-            right_ref[c] = value
+def prepare_kernel(scale_ref, orbitals_ref, operator_ref, left_ref, right_ref, khigh, klow, kwide):
+    for c in range(3):
+        left_ref[c] = orbitals_ref[:, 5 + c, :]
+        right_ref[c] = orbitals_ref[:, c, :]
     for c in range(8):
         line = jnp.full((1, OWN), scale_ref[c], jnp.float32)
         left_ref[3, c:c + 1, :] = line
@@ -91,8 +97,14 @@
         klow[i:i + 128, :] = low
 
 
-def filter_kernel(last_ref, scale_ref, own_ref, left_ref, right_ref, rho_ref, khigh, klow, out_ref,
-                  v0, v1, v2, chigh, clow, cell_buf, product, pot):
+def filter_kernel(last_ref, scale_ref, own_ref, left_ref, right_ref, rho_ref, khigh_hbm, klow_hbm, out_ref,
+                  khigh, klow, ksems, v0, v1, v2, chigh, clow, cell_buf, product, pot):
+    copies = [
+        pltpu.make_async_copy(khigh_hbm, khigh, ksems.at[0]),
+        pltpu.make_async_copy(klow_hbm, klow, ksems.at[1]),
+    ]
+    for copy in copies:
+        copy.start()
     for half in range(2):
         rho = rho_ref[half]
         pot[:, half * HALF:(half + 1) * HALF] = jnp.where(
@@ -110,7 +122,7 @@
         place(i, left_ref[i])
         place(11 + i, right_ref[i])
     for i in range(8):
-        place(3 + i, own_ref[i])
+        place(3 + i, own_ref[:, i, :])
 
     def scale_of(i):
         if i < 3:
@@ -139,6 +151,9 @@
                 clow[r, c] = low
         r = slice(16 * begin, 16 * end)
         a, b = chigh[r, :], clow[r, :]
+        if begin == 0:
+            for copy in copies:
+                copy.wait()
         product[r, :] = dot(a, khigh[...]) + dot(b, khigh[...]) + dot(a, klow[...])
         tail = None
         for i in range(begin, end):
@@ -263,27 +278,35 @@
     alive = jnp.reshape((dom < dom_count - 1).astype(jnp.int32), (1,))
     smem = pl.BlockSpec(memory_space=pltpu.SMEM)
     vmem = pl.BlockSpec(memory_space=pltpu.VMEM)
-    params = pltpu.CompilerParams(vmem_limit_bytes=48 << 20)
+    hbm = pl.BlockSpec(memory_space=pltpu.HBM)
+    params = pltpu.CompilerParams(vmem_limit_bytes=16 << 20)
+    roomy = pltpu.CompilerParams(vmem_limit_bytes=62 << 20)
 
     half_shape = jax.ShapeDtypeStruct((4 * SLAB, HALF), jnp.float32)
     mine, theirs = pl.pallas_call(
         deliver_kernel,
         out_shape=(half_shape, half_shape),
-        in_specs=[smem, vmem, vmem, vmem],
+        in_specs=[smem, hbm, hbm, hbm],
         out_specs=(vmem, vmem),
-        scratch_shapes=[pltpu.VMEM((WIDE, density.shape[0]), jnp.float32)],
-        compiler_params=params,
+        scratch_shapes=[
+            pltpu.VMEM((1, density.shape[0]), jnp.int32),
+            pltpu.VMEM((1, density.shape[0]), jnp.int32),
+            pltpu.VMEM((NODES, density.shape[0]), jnp.float32),
+            pltpu.VMEM((WIDE, density.shape[0]), jnp.float32),
+            pltpu.SemaphoreType.DMA((3,)),
+        ],
+        compiler_params=roomy,
         name="deliver",
     )(core, block_owner.reshape(1, -1), block_cell.reshape(1, -1), density.T)
     other = lax.ppermute(theirs, "band", [(i, i ^ 1) for i in range(band_count)])
 
     ghost_shape = jax.ShapeDtypeStruct((4, 16, OWN), jnp.float32)
     split_shape = jax.ShapeDtypeStruct((WIDE, WIDE), jnp.bfloat16)
-    cells, send_left, send_right, khigh, klow = pl.pallas_call(
+    send_left, send_right, khigh, klow = pl.pallas_call(
         prepare_kernel,
-        out_shape=(jax.ShapeDtypeStruct((8, 16, OWN), jnp.float32), ghost_shape, ghost_shape, split_shape, split_shape),
+        out_shape=(ghost_shape, ghost_shape, split_shape, split_shape),
         in_specs=[smem, vmem, vmem],
-        out_specs=(vmem,) * 5,
+        out_specs=(vmem,) * 4,
         scratch_shapes=[pltpu.VMEM((WIDE, WIDE), jnp.float32)],
         compiler_params=params,
         name="prepare",
@@ -294,18 +317,21 @@
     part = exchange((mine + other).reshape(4, SLAB, HALF), "dom", X_GROUPS)
     slab = jnp.sum(part, 0)
     windows = jnp.concatenate([slab[:128].reshape(16, 8, HALF), slab[8:].reshape(16, 8, HALF)], 1)
+    windows, left, right = lax.optimization_barrier((windows, left, right))
     part = exchange(windows, "dom", YZ_GROUPS)
     window = jnp.sum(part, 0)
-    window, left, right = lax.optimization_barrier((window, left, right))
     part = exchange(jnp.broadcast_to(window[None], (band_count, 16, HALF)), "band")
     rho = jnp.sum(part.reshape(4, 2, 16, HALF), 0)
 
     filtered = pl.pallas_call(
         filter_kernel,
         out_shape=jax.ShapeDtypeStruct((8, 16, OWN), jnp.float32),
-        in_specs=[smem] * 2 + [vmem] * 6,
+        in_specs=[smem] * 2 + [vmem] * 4 + [hbm] * 2,
         out_specs=vmem,
         scratch_shapes=[
+            pltpu.VMEM((WIDE, WIDE), jnp.bfloat16),
+            pltpu.VMEM((WIDE, WIDE), jnp.bfloat16),
+            pltpu.SemaphoreType.DMA((2,)),
             pltpu.VMEM((224, WIDE), jnp.float32),
             pltpu.VMEM((224, WIDE), jnp.float32),
             pltpu.VMEM((224, WIDE), jnp.float32),
@@ -315,9 +341,9 @@
             pltpu.VMEM((224, WIDE), jnp.float32),
             pltpu.VMEM((16, WIDE), jnp.float32),
         ],
-        compiler_params=params,
+        compiler_params=roomy,
         name="chebyshev",
-    )(alive, cell_scale, cells, left, right, rho, khigh, klow)
+    )(alive, cell_scale, orbitals, left, right, rho, khigh, klow)
 
     flat = exchange(filtered, "band").reshape(128, OWN)
     total = OWN * dom_count * band_count

time: 146 us -> 151 us (1.034)
  Pallas kernels: 13.3 us -> 18.5 us
  local copies, waits for them, and re-layouts: 6.98 us -> 2.83 us
  blocking collectives: 71.8 us -> 75.6 us
  other arithmetic: 2.03 us -> 4.24 us
  waiting for transfers between devices: 22.1 us -> 20.5 us
    unnamed x20 -> x14, local copies, waits for them, and re-layouts: 6.24 us -> 2.09 us
    all_to_all x5, blocking collectives: 71.8 us -> 75.6 us  [exchange(): lax.all_to_all(value, axis, split_axis=0, concat_axis=0, tiled=True, axis...]
    pallas_call x1, Pallas kernels: 4.38 us -> 7.32 us  [body(): pl.pallas_call(filter_kernel, out_shape=jax.ShapeDtypeStruct((8, 16, OWN)...]
    all_to_all x2, waiting for transfers between devices: 12.7 us -> 15.2 us  [exchange(): lax.all_to_all(value, axis, split_axis=0, concat_axis=0, tiled=True, axis...]
    ppermute x1, waiting for transfers between devices: 5.55 us -> 3.03 us  [body(): lax.ppermute(send_right, 'dom', [(i + 1, i) for i in range(dom_count - 1)])]
    pallas_call x1, Pallas kernels: 1.39 us -> 3.73 us  [body(): pl.pallas_call(deliver_kernel, out_shape=(half_shape, half_shape), in_spe...]
    add x1, other arithmetic: 0.09 us -> 2.28 us  [body(): part = exchange((mine + other).reshape(4, SLAB, HALF), 'dom', X_GROUPS)]
    ppermute x1, starting transfers between devices: 3.35 us -> 1.29 us  [body(): lax.ppermute(send_left, 'dom', [(i, i + 1) for i in range(dom_count - 1)])]
  transfers between devices with their start and end apart: 5 -> 5, of which waited for: 5 -> 4; matrix products, arithmetic and copies ran while one was open for 1% -> 1% of each run, Pallas kernels for 1% -> 1%
where the time goes in v3:
time: 151 us; the launch traced here: 150 us
  blocking collectives  75.6 us (50%)
  starting transfers between devices  27.7 us (18%)
  waiting for transfers between devices  20.5 us (14%)
  Pallas kernels  18.5 us (12%)
  other arithmetic  4.24 us (3%)
  local copies, waits for them, and re-layouts  2.83 us (2%)
    all_to_all x5, blocking collectives, exchange(): lax.all_to_all(value, axis, split_axis=0, concat_axis=0, tiled=True, axis...  75.6 us
    all_to_all x2, starting transfers between devices, exchange(): lax.all_to_all(value, axis, split_axis=0, concat_axis=0, tiled=True, axis...  16.3 us
    all_to_all x2, waiting for transfers between devices, exchange(): lax.all_to_all(value, axis, split_axis=0, concat_axis=0, tiled=True, axis...  15.2 us
    ppermute x1, starting transfers between devices, body(): lax.ppermute(theirs, 'band', [(i, i ^ 1) for i in range(band_count)])  8.78 us
    pallas_call x1, Pallas kernels, body(): pl.pallas_call(filter_kernel, out_shape=jax.ShapeDtypeStruct((8, 16, OWN)...  7.32 us
    pallas_call x1, Pallas kernels, body(): pl.pallas_call(functools.partial(solve_kernel, float(total)), out_shape=j...  6.12 us
    pallas_call x1, Pallas kernels, body(): pl.pallas_call(deliver_kernel, out_shape=(half_shape, half_shape), in_spe...  3.73 us
    ppermute x1, waiting for transfers between devices, body(): lax.ppermute(send_right, 'dom', [(i + 1, i) for i in range(dom_count - 1)])  3.03 us
  transfers between devices with their start and end apart: 5, of which 4 were waited for; matrix products, arithmetic and copies ran while one was open for 1% of the time, Pallas kernels for 1%

profile of v3, /device:TPU:1, one launch (start us, length us, event | category | flops | bytes accessed | tf_op | source)
XLA Modules:
  0.0 149.9 jit_solution(12694858093998738911)
XLA Ops:
  0.0 3.7 %deliver.1 = (f32[544,384]{1,0:T(8,128)}, f32[544,384]{1,0:T(8,128)}) custom-call(s32[1]{0:T(128)} %bitcast.1.core_ref, s32[1,256]{1,0:T(1,128)} %bitcast.27, s32[1,256]{1,0:T(1,128)} %bitcast.28, f32[729,256]{1,0:T(8,128)} %bitcast.26), custom_call_target="tpu_custom_call" | custom-call | tf_op jit(solution)/shard_map/deliver/pallas_call | solution.py:286
  3.7 8.8 %collective-permute-start = (f32[544,384]{1,0:T(8,128)}, f32[544,384]{1,0:T(8,128)S(1)}, u32[]{:S(2)}, u32[]{:S(2)}) collective-permute-start(f32[544,384]{1,0:T(8,128)} %get-tuple-element.15), channel_id=1, source_target_pairs={{0,1},{1,0},{2,3},{3,2},{4,5},{5,4},{6,7},{7,6},{8,9},{9,8},{10,11... | collective-permute-start | bytes 2506760 | tf_op jit(solution)/shard_map/ppermute | solution.py:301
  12.5 2.2 %collective-permute-done = f32[544,384]{1,0:T(8,128)S(1)} collective-permute-done((f32[544,384]{1,0:T(8,128)}, f32[544,384]{1,0:T(8,128)S(1)}, u32[]{:S(2)}, u32[]{:S(2)}) %collective-permute-start) | collective-permute-done | bytes 835616 | tf_op jit(solution)/shard_map/ppermute | solution.py:301
  14.7 2.3 %add.8 = f32[544,384]{1,0:T(8,128)} add(f32[544,384]{1,0:T(8,128)} %get-tuple-element.14, f32[544,384]{1,0:T(8,128)S(1)} %collective-permute-done) | non-fusion elementwise | flops 208896 | bytes 2506752 | tf_op jit(solution)/shard_map/add | solution.py:317
  17.0 4.3 %all-to-all-start = ((f32[4,136,384]{2,1,0:T(8,128)}), f32[4,136,384]{2,1,0:T(8,128)}, u32[]{:S(2)}, u32[]{:S(2)}) async-start(f32[4,136,384]{2,1,0:T(8,128)} %bitcast.5), calls=%async_computation | async-start | bytes 1671168 | tf_op jit(solution)/shard_map/all_to_all | solution.py:28
  21.3 0.0 copy-done
  21.3 0.0 copy-done.1
  21.3 0.0 copy-done.4
  21.3 1.3 prepare.1
  22.7 0.0 copy-start.2
  22.7 1.0 copy-done.2
  23.7 1.1 copy-done.3
  24.8 1.3 collective-permute-start.1
  26.1 1.3 collective-permute-start.2
  27.4 6.6 %all-to-all-done = f32[4,136,384]{2,1,0:T(8,128)} async-done(((f32[4,136,384]{2,1,0:T(8,128)}), f32[4,136,384]{2,1,0:T(8,128)}, u32[]{:S(2)}, u32[]{:S(2)}) %all-to-all-start) | async-done | bytes 835616 | tf_op jit(solution)/shard_map/all_to_all | solution.py:28
  33.9 1.2 reduce_sum.45
  35.2 0.0 collective-permute-done.1.left_ref
  35.2 0.0 copy-start.5
  35.3 3.0 %collective-permute-done.2.right_ref = f32[4,16,648]{2,1,0:T(8,128)S(1)} collective-permute-done((f32[4,16,648]{2,1,0:T(8,128)S(1)}, f32[4,16,648]{2,1,0:T(8,128)S(1)}, u32[]{:S(2)}, u32[]{:S(2)}) %collective-permute-start.2) | collective-permute-done | bytes 165920 | tf_op jit(solution)/shard_map/ppermute | solution.py:315
  38.3 16.5 %all_to_all.35 = f32[16,16,384]{2,1,0:T(8,128)S(1)} all-to-all(f32[16,16,384]{2,1,0:T(8,128)S(1)} %pad_maximum_fusion), channel_id=1, replica_groups={{0,8,16,24,32,40,48,56,64,72,80,88,96,104,112,120},{128,136,144,152,160..., dimensions={0} | all-to-all | bytes 786432 | tf_op jit(solution)/shard_map/all_to_all | solution.py:28
  54.8 0.7 broadcast_in_dim.6
  55.5 12.0 %all-to-all-start.2 = ((f32[8,16,384]{2,1,0:T(8,128)}), f32[8,16,384]{2,1,0:T(8,128)S(1)}, u32[]{:S(2)}, u32[]{:S(2)}) async-start(f32[8,16,384]{2,1,0:T(8,128)} %broadcast_in_dim.6), calls=%async_computation.2 | async-start | bytes 393216 | tf_op jit(solution)/shard_map/all_to_all | solution.py:28
  67.5 8.7 %all-to-all-done.2 = f32[8,16,384]{2,1,0:T(8,128)S(1)} async-done(((f32[8,16,384]{2,1,0:T(8,128)}), f32[8,16,384]{2,1,0:T(8,128)S(1)}, u32[]{:S(2)}, u32[]{:S(2)}) %all-to-all-start.2) | async-done | bytes 196640 | tf_op jit(solution)/shard_map/all_to_all | solution.py:28
  76.2 0.6 reduce_sum.47.rho_ref
  76.8 0.0 copy-done.5
  76.8 7.3 %chebyshev.1 = f32[8,16,648]{2,1,0:T(8,128)} custom-call(s32[1]{0:T(128)} %bitcast.last_ref, f32[8]{0:T(128)} %scale_ref.3, f32[16,8,648]{2,1,0:T(8,128)} %own_ref.1, f32[4,16,648]{2,1,0:T(8,128)} %copy-done.5, f32[4,16,648]{2,1,0:T(8,128)} %copy-done.6, f32[2,16,384]{2,1,0:T(8,128)} %reduce_sum.47.rho_ref, bf16[768,768]{1,0:T(8,128)(2,1)} %copy-done.2, ...), custom_call_target="tpu_custom_call" | custom-call | tf_op jit(solution)/shard_map/chebyshev/pallas_call | solution.py:326
  84.1 18.5 %all_to_all.36 = f32[8,16,648]{2,1,0:T(8,128)S(1)} all-to-all(f32[8,16,648]{2,1,0:T(8,128)} %chebyshev.1), channel_id=1, replica_groups=mesh['dom'=64,'band'=8] {'band'}, dimensions={0} | all-to-all | bytes 663552 | tf_op jit(solution)/shard_map/all_to_all | solution.py:28
  102.6 0.5 fusion
  103.1 12.1 %all_to_all.37 = f32[16,8,128]{2,1,0:T(8,128)S(1)} all-to-all(f32[16,8,128]{2,1,0:T(8,128)S(1)} %fusion), channel_id=1, replica_groups={{0,8,16,24,32,40,48,56,64,72,80,88,96,104,112,120},{128,136,144,152,160..., dimensions={0} | all-to-all | bytes 131072 | tf_op jit(solution)/shard_map/all_to_all | solution.py:28
  115.2 18.0 %all_to_all.38 = f32[32,8,128]{2,1,0:T(8,128)S(1)} all-to-all(f32[32,8,128]{2,1,0:T(8,128)S(1)} %broadcast_in_dim.7), channel_id=1, replica_groups={{0,1,2,3,4,5,6,7,128,129,130,131,132,133,134,135,256,257,258,259,260,26..., dimensions={0} | all-to-all | bytes 262144 | tf_op jit(solution)/shard_map/all_to_all | solution.py:28
  133.3 10.5 %all_to_all.39 = f32[16,8,128]{2,1,0:T(8,128)S(1)} all-to-all(f32[16,8,128]{2,1,0:T(8,128)S(1)} %broadcast_in_dim.8), channel_id=1, replica_groups={{0,8,16,24,32,40,48,56,64,72,80,88,96,104,112,120},{128,136,144,152,160..., dimensions={0} | all-to-all | bytes 131072 | tf_op jit(solution)/shard_map/all_to_all | solution.py:28
  143.8 6.1 %orthonormalize.1 = f32[648,128]{1,0:T(8,128)} custom-call(f32[128,128]{1,0:T(8,128)S(1)} %bitcast.24, f32[128,648]{1,0:T(8,128)S(1)} %bitcast.23), custom_call_target="tpu_custom_call" | custom-call | tf_op jit(solution)/shard_map/orthonormalize/pallas_call | solution.py:354
  (13 shorter events, 0.2 us)
Async XLA Ops:
  3.7 11.0 %collective-permute-start = (f32[544,384]{1,0:T(8,128)}, f32[544,384]{1,0:T(8,128)S(1)}, u32[]{:S(2)}, u32[]{:S(2)}) collective-permute-start(f32[544,384]{1,0:T(8,128)} %get-tuple-element.15), channel_id=1, source_target_pairs={{0,1},{1,0},{2,3},{3,2},{4,5},{5,4},{6,7},{7,6},{8,9},{9,8},{10,11... | collective-permute-start | bytes 2506760 | tf_op jit(solution)/shard_map/ppermute | solution.py:301
  14.7 6.6 %copy-start = (f32[729,729]{1,0:T(8,128)S(1)}, f32[729,729]{1,0:T(8,128)}, u32[]{:S(2)}) copy-start(f32[729,729]{1,0:T(8,128)} %operator_ref.1) | copy-start | bytes 6377296
  17.0 4.4 %copy-start.1 = (f32[16,8,648]{2,1,0:T(8,128)S(1)}, f32[16,8,648]{2,1,0:T(8,128)}, u32[]{:S(2)}) copy-start(f32[16,8,648]{2,1,0:T(8,128)} %own_ref.1) | copy-start | bytes 995332
  17.0 4.4 %copy-start.4 = (f32[8]{0:T(128)S(1)}, f32[8]{0:T(128)}, u32[]{:S(2)}) copy-start(f32[8]{0:T(128)} %scale_ref.3) | copy-start | bytes 100
  17.0 17.0 %all-to-all-start = ((f32[4,136,384]{2,1,0:T(8,128)}), f32[4,136,384]{2,1,0:T(8,128)}, u32[]{:S(2)}, u32[]{:S(2)}) async-start(f32[4,136,384]{2,1,0:T(8,128)} %bitcast.5), calls=%async_computation | async-start | bytes 1671168 | tf_op jit(solution)/shard_map/all_to_all | solution.py:28
  22.7 1.0 copy-start.2
  23.7 1.1 copy-start.3
  24.8 10.5 %collective-permute-start.1 = (f32[4,16,648]{2,1,0:T(8,128)S(1)}, f32[4,16,648]{2,1,0:T(8,128)S(1)}, u32[]{:S(2)}, u32[]{:S(2)}) collective-permute-start(f32[4,16,648]{2,1,0:T(8,128)S(1)} %get-tuple-element.16), channel_id=1, source_target_pairs={{0,8},{8,16},{16,24},{24,32},{32,40},{40,48},{48,56},{56,64},{64,7... | collective-permute-start | bytes 497672 | tf_op jit(solution)/shard_map/ppermute | solution.py:314
  26.1 12.2 %collective-permute-start.2 = (f32[4,16,648]{2,1,0:T(8,128)S(1)}, f32[4,16,648]{2,1,0:T(8,128)S(1)}, u32[]{:S(2)}, u32[]{:S(2)}) collective-permute-start(f32[4,16,648]{2,1,0:T(8,128)S(1)} %get-tuple-element.17), channel_id=1, source_target_pairs={{8,0},{16,8},{24,16},{32,24},{40,32},{48,40},{56,48},{64,56},{72,6... | collective-permute-start | bytes 497672 | tf_op jit(solution)/shard_map/ppermute | solution.py:315
  35.2 41.6 %copy-start.5 = (f32[4,16,648]{2,1,0:T(8,128)}, f32[4,16,648]{2,1,0:T(8,128)S(1)}, u32[]{:S(2)}) copy-start(f32[4,16,648]{2,1,0:T(8,128)S(1)} %collective-permute-done.1.left_ref) | copy-start | bytes 497668
  38.3 38.5 %copy-start.6 = (f32[4,16,648]{2,1,0:T(8,128)}, f32[4,16,648]{2,1,0:T(8,128)S(1)}, u32[]{:S(2)}) copy-start(f32[4,16,648]{2,1,0:T(8,128)S(1)} %collective-permute-done.2.right_ref) | copy-start | bytes 497668
  55.5 20.6 %all-to-all-start.2 = ((f32[8,16,384]{2,1,0:T(8,128)}), f32[8,16,384]{2,1,0:T(8,128)S(1)}, u32[]{:S(2)}, u32[]{:S(2)}) async-start(f32[8,16,384]{2,1,0:T(8,128)} %broadcast_in_dim.6), calls=%async_computation.2 | async-start | bytes 393216 | tf_op jit(solution)/shard_map/all_to_all | solution.py:28

commit v4 on v3

--- a/solution.py
+++ b/solution.py
@@ -42,52 +42,84 @@
     return lax.dot_general(a, b, (((1,), (1,)), ((), ())), preferred_element_type=jnp.float32)
 
 
-def deliver_kernel(core_ref, owner_hbm, cell_hbm, density_hbm, mine_ref, theirs_ref,
-                   owner_ref, cell_ref, density_ref, wide_ref, sems):
-    rows = 4 * SLAB
-    count = density_ref.shape[1]
+def pack_kernel(core_ref, owner_hbm, cell_hbm, density_hbm, scale_hbm, orbitals_hbm,
+                own_ref, send_ref, left_ref, right_ref,
+                owner_ref, cell_ref, density_ref, scale_ref, orbitals_ref, sems):
     copies = [
         pltpu.make_async_copy(density_hbm, density_ref, sems.at[0]),
         pltpu.make_async_copy(owner_hbm, owner_ref, sems.at[1]),
         pltpu.make_async_copy(cell_hbm, cell_ref, sems.at[2]),
+        pltpu.make_async_copy(scale_hbm, scale_ref, sems.at[3]),
+        pltpu.make_async_copy(orbitals_hbm, orbitals_ref, sems.at[4]),
     ]
     for copy in copies:
         copy.start()
-    wide_ref[720:, :] = jnp.zeros((WIDE - 720, count), jnp.float32)
     for copy in copies:
         copy.wait()
-    wide_ref[:NODES, :] = density_ref[...]
+    for c in range(3):
+        left_ref[c] = orbitals_ref[:, 5 + c, :]
+        right_ref[c] = orbitals_ref[:, c, :]
+    diagonal = lax.broadcasted_iota(jnp.int32, (8, 8), 0) == lax.broadcasted_iota(jnp.int32, (8, 8), 1)
+    column = jnp.sum(jnp.where(diagonal, jnp.broadcast_to(scale_ref[...], (8, 8)), 0.0), 1, keepdims=True)
+    for ref in (left_ref, right_ref):
+        ref[3, :8, :] = jnp.broadcast_to(column, (8, OWN))
+        ref[3, 8:, :] = jnp.zeros((8, OWN), jnp.float32)
+    count = density_ref.shape[1]
+    target = (owner_ref[...] * 8 + cell_ref[...]).astype(jnp.float32)
+    target = jnp.broadcast_to(target, (8, count))
+
+    def lower(ref):
+        ref[:HALF, :] = density_ref[:HALF, :]
+        ref[HALF:, :] = target
+
+    def upper(ref):
+        ref[:344, :] = density_ref[HALF:728, :]
+        ref[344:HALF, :] = jnp.zeros((HALF - 344, count), jnp.float32)
+        ref[344:345, :] = density_ref[728:NODES, :]
+        ref[HALF:, :] = target
+
+    @pl.when(core_ref[0] == 0)
+    def _():
+        lower(own_ref)
+        upper(send_ref)
+
+    @pl.when(core_ref[0] != 0)
+    def _():
+        upper(own_ref)
+        lower(send_ref)
+
+
+def deliver_kernel(own_ref, other_ref, out_ref):
+    rows = 4 * SLAB
+    count = own_ref.shape[1]
     row = lax.broadcasted_iota(jnp.int32, (rows, count), 0)
     slab = (row >= SLAB).astype(jnp.int32) + (row >= 2 * SLAB).astype(jnp.int32) + (row >= 3 * SLAB).astype(jnp.int32)
-    cell = row - 8 * slab - 3
-    onehot = jnp.where(owner_ref[...] * 8 + cell_ref[...] == cell, 1.0, 0.0).astype(jnp.bfloat16)
-    for half in range(2):
-        values = wide_ref[half * HALF:(half + 1) * HALF, :]
+    cell = (row - 8 * slab - 3).astype(jnp.float32)
+    total = None
+    for ref in (own_ref, other_ref):
+        onehot = jnp.where(ref[HALF:HALF + 1, :] == cell, 1.0, 0.0).astype(jnp.bfloat16)
+        values = ref[:HALF, :]
         first = values.astype(jnp.bfloat16)
         rest = values - first.astype(jnp.float32)
         second = rest.astype(jnp.bfloat16)
         third = (rest - second.astype(jnp.float32)).astype(jnp.bfloat16)
-        total = dot_nt(onehot, first) + dot_nt(onehot, second) + dot_nt(onehot, third)
-
-        @pl.when(core_ref[0] == half)
-        def _():
-            mine_ref[...] = total
-
-        @pl.when(core_ref[0] != half)
-        def _():
-            theirs_ref[...] = total
-
-
-def prepare_kernel(scale_ref, orbitals_ref, operator_ref, left_ref, right_ref, khigh, klow, kwide):
-    for c in range(3):
-        left_ref[c] = orbitals_ref[:, 5 + c, :]
-        right_ref[c] = orbitals_ref[:, c, :]
-    for c in range(8):
-        line = jnp.full((1, OWN), scale_ref[c], jnp.float32)
-        left_ref[3, c:c + 1, :] = line
-        right_ref[3, c:c + 1, :] = line
-    left_ref[3, 8:, :] = jnp.zeros((8, OWN), jnp.float32)
-    right_ref[3, 8:, :] = jnp.zeros((8, OWN), jnp.float32)
+        part = dot_nt(onehot, first) + dot_nt(onehot, second) + dot_nt(onehot, third)
+        total = part if total is None else total + part
+    out_ref[...] = total
+
+
+def window_kernel(part_ref, out_ref):
+    for k in range(17):
+        r = slice(8 * k, 8 * k + 8)
+        block = (part_ref[0, r, :] + part_ref[1, r, :]) + (part_ref[2, r, :] + part_ref[3, r, :])
+        if k < 16:
+            out_ref[k, :8, :] = block
+        if k > 0:
+            out_ref[k - 1, 8:, :] = block
+
+
+def filter_kernel(last_ref, scale_ref, own_ref, left_ref, right_ref, part_ref, operator_ref, out_ref,
+                  kwide, khigh, klow, v0, v1, v2, chigh, clow, cell_buf, product, pot):
     kwide[720:, :] = jnp.zeros((WIDE - 720, WIDE), jnp.float32)
     kwide[:, TILE5:] = jnp.zeros((WIDE, WIDE - TILE5), jnp.float32)
     kwide[:NODES, :NODES] = operator_ref[...]
@@ -95,18 +127,8 @@
         high, low = split2(kwide[i:i + 128, :])
         khigh[i:i + 128, :] = high
         klow[i:i + 128, :] = low
-
-
-def filter_kernel(last_ref, scale_ref, own_ref, left_ref, right_ref, rho_ref, khigh_hbm, klow_hbm, out_ref,
-                  khigh, klow, ksems, v0, v1, v2, chigh, clow, cell_buf, product, pot):
-    copies = [
-        pltpu.make_async_copy(khigh_hbm, khigh, ksems.at[0]),
-        pltpu.make_async_copy(klow_hbm, klow, ksems.at[1]),
-    ]
-    for copy in copies:
-        copy.start()
     for half in range(2):
-        rho = rho_ref[half]
+        rho = (part_ref[half] + part_ref[half + 2]) + (part_ref[half + 4] + part_ref[half + 6])
         pot[:, half * HALF:(half + 1) * HALF] = jnp.where(
             rho > 0.0, -0.7386 * jnp.exp(jnp.log(jnp.where(rho > 0.0, rho, 1.0)) * (1.0 / 3.0)), 0.0)
     lane = lax.broadcasted_iota(jnp.int32, (16, 128), 1)
@@ -151,9 +173,6 @@
                 clow[r, c] = low
         r = slice(16 * begin, 16 * end)
         a, b = chigh[r, :], clow[r, :]
-        if begin == 0:
-            for copy in copies:
-                copy.wait()
         product[r, :] = dot(a, khigh[...]) + dot(b, khigh[...]) + dot(a, klow[...])
         tail = None
         for i in range(begin, end):
@@ -282,56 +301,61 @@
     params = pltpu.CompilerParams(vmem_limit_bytes=16 << 20)
     roomy = pltpu.CompilerParams(vmem_limit_bytes=62 << 20)
 
-    half_shape = jax.ShapeDtypeStruct((4 * SLAB, HALF), jnp.float32)
-    mine, theirs = pl.pallas_call(
-        deliver_kernel,
-        out_shape=(half_shape, half_shape),
-        in_specs=[smem, hbm, hbm, hbm],
-        out_specs=(vmem, vmem),
+    count = density.shape[0]
+    pack_shape = jax.ShapeDtypeStruct((HALF + 8, count), jnp.float32)
+    ghost_shape = jax.ShapeDtypeStruct((4, 16, OWN), jnp.float32)
+    own, send, send_left, send_right = pl.pallas_call(
+        pack_kernel,
+        out_shape=(pack_shape, pack_shape, ghost_shape, ghost_shape),
+        in_specs=[smem] + [hbm] * 5,
+        out_specs=(vmem,) * 4,
         scratch_shapes=[
-            pltpu.VMEM((1, density.shape[0]), jnp.int32),
-            pltpu.VMEM((1, density.shape[0]), jnp.int32),
-            pltpu.VMEM((NODES, density.shape[0]), jnp.float32),
-            pltpu.VMEM((WIDE, density.shape[0]), jnp.float32),
-            pltpu.SemaphoreType.DMA((3,)),
+            pltpu.VMEM((1, count), jnp.int32),
+            pltpu.VMEM((1, count), jnp.int32),
+            pltpu.VMEM((NODES, count), jnp.float32),
+            pltpu.VMEM((1, 8), jnp.float32),
+            pltpu.VMEM((16, 8, OWN), jnp.float32),
+            pltpu.SemaphoreType.DMA((5,)),
         ],
         compiler_params=roomy,
+        name="pack",
+    )(core, block_owner.reshape(1, -1), block_cell.reshape(1, -1), density.T, cell_scale.reshape(1, -1), orbitals)
+    other = lax.ppermute(send, "band", [(i, i ^ 1) for i in range(band_count)])
+    delivered = pl.pallas_call(
+        deliver_kernel,
+        out_shape=jax.ShapeDtypeStruct((4 * SLAB, HALF), jnp.float32),
+        in_specs=[vmem, vmem],
+        out_specs=vmem,
+        compiler_params=params,
         name="deliver",
-    )(core, block_owner.reshape(1, -1), block_cell.reshape(1, -1), density.T)
-    other = lax.ppermute(theirs, "band", [(i, i ^ 1) for i in range(band_count)])
-
-    ghost_shape = jax.ShapeDtypeStruct((4, 16, OWN), jnp.float32)
-    split_shape = jax.ShapeDtypeStruct((WIDE, WIDE), jnp.bfloat16)
-    send_left, send_right, khigh, klow = pl.pallas_call(
-        prepare_kernel,
-        out_shape=(ghost_shape, ghost_shape, split_shape, split_shape),
-        in_specs=[smem, vmem, vmem],
-        out_specs=(vmem,) * 4,
-        scratch_shapes=[pltpu.VMEM((WIDE, WIDE), jnp.float32)],
-        compiler_params=params,
-        name="prepare",
-    )(cell_scale, orbitals, cell_operator)
+    )(own, other)
+
     left = lax.ppermute(send_left, "dom", [(i, i + 1) for i in range(dom_count - 1)])
     right = lax.ppermute(send_right, "dom", [(i + 1, i) for i in range(dom_count - 1)])
 
-    part = exchange((mine + other).reshape(4, SLAB, HALF), "dom", X_GROUPS)
-    slab = jnp.sum(part, 0)
-    windows = jnp.concatenate([slab[:128].reshape(16, 8, HALF), slab[8:].reshape(16, 8, HALF)], 1)
+    part = exchange(delivered.reshape(4, SLAB, HALF), "dom", X_GROUPS)
+    windows = pl.pallas_call(
+        window_kernel,
+        out_shape=jax.ShapeDtypeStruct((16, 16, HALF), jnp.float32),
+        in_specs=[vmem],
+        out_specs=vmem,
+        compiler_params=params,
+        name="windows",
+    )(part)
     windows, left, right = lax.optimization_barrier((windows, left, right))
     part = exchange(windows, "dom", YZ_GROUPS)
     window = jnp.sum(part, 0)
     part = exchange(jnp.broadcast_to(window[None], (band_count, 16, HALF)), "band")
-    rho = jnp.sum(part.reshape(4, 2, 16, HALF), 0)
 
     filtered = pl.pallas_call(
         filter_kernel,
         out_shape=jax.ShapeDtypeStruct((8, 16, OWN), jnp.float32),
-        in_specs=[smem] * 2 + [vmem] * 4 + [hbm] * 2,
+        in_specs=[smem] * 2 + [vmem] * 5,
         out_specs=vmem,
         scratch_shapes=[
+            pltpu.VMEM((WIDE, WIDE), jnp.float32),
             pltpu.VMEM((WIDE, WIDE), jnp.bfloat16),
             pltpu.VMEM((WIDE, WIDE), jnp.bfloat16),
-            pltpu.SemaphoreType.DMA((2,)),
             pltpu.VMEM((224, WIDE), jnp.float32),
             pltpu.VMEM((224, WIDE), jnp.float32),
             pltpu.VMEM((224, WIDE), jnp.float32),
@@ -341,9 +365,9 @@
             pltpu.VMEM((224, WIDE), jnp.float32),
             pltpu.VMEM((16, WIDE), jnp.float32),
         ],
-        compiler_params=roomy,
+        compiler_params=params,
         name="chebyshev",
-    )(alive, cell_scale, orbitals, left, right, rho, khigh, klow)
+    )(alive, cell_scale, orbitals, left, right, part, cell_operator)
 
     flat = exchange(filtered, "band").reshape(128, OWN)
     total = OWN * dom_count * band_count

time: 151 us -> 142 us (0.940)
  other arithmetic: 4.24 us -> 0.08 us
  waiting for transfers between devices: 20.5 us -> 23.7 us
  Pallas kernels: 18.5 us -> 15.8 us
  blocking collectives: 75.6 us -> 73.6 us
    all_to_all x2, waiting for transfers between devices: 15.2 us -> 22.1 us  [exchange(): lax.all_to_all(value, axis, split_axis=0, concat_axis=0, tiled=True, axis...]
    ppermute x1, waiting for transfers between devices: 3.03 us -> 0.01 us  [body(): lax.ppermute(send_right, 'dom', [(i + 1, i) for i in range(dom_count - 1)])]
    add x1 -> x0, other arithmetic: 2.28 us -> none  [body(): part = exchange((mine + other).reshape(4, SLAB, HALF), 'dom', X_GROUPS)]
    pallas_call x1, Pallas kernels: 7.32 us -> 5.17 us  [body(): pl.pallas_call(filter_kernel, out_shape=jax.ShapeDtypeStruct((8, 16, OWN)...]
    all_to_all x5, blocking collectives: 75.6 us -> 73.6 us  [exchange(): lax.all_to_all(value, axis, split_axis=0, concat_axis=0, tiled=True, axis...]
    all_to_all x2, starting transfers between devices: 16.3 us -> 14.3 us  [exchange(): lax.all_to_all(value, axis, split_axis=0, concat_axis=0, tiled=True, axis...]
    reduce_sum x2 -> x0, other arithmetic: 1.84 us -> none  [the longest x1 1.21 us: body(): slab = jnp.sum(part, 0)]
    pallas_call x2 -> x3, Pallas kernels: 5.06 us -> 4.55 us  [the longest x1 2.53 us: body(): pl.pallas_call(pack_kernel, out_shape=(pack_shape, pack_shape, ghost_shap...]
  transfers between devices with their start and end apart: 5 -> 5, of which waited for: 4 -> 3; matrix products, arithmetic and copies ran while one was open for 1% -> 0% of each run, Pallas kernels for 1% -> 0%
where the time goes in v4:
time: 142 us
  blocking collectives  73.6 us (52%)
  starting transfers between devices  26.3 us (19%)
  waiting for transfers between devices  23.7 us (17%)
  Pallas kernels  15.8 us (11%)
  local copies, waits for them, and re-layouts  1.72 us (1%)
    all_to_all x5, blocking collectives, exchange(): lax.all_to_all(value, axis, split_axis=0, concat_axis=0, tiled=True, axis...  73.6 us
    all_to_all x2, waiting for transfers between devices, exchange(): lax.all_to_all(value, axis, split_axis=0, concat_axis=0, tiled=True, axis...  22.1 us
    all_to_all x2, starting transfers between devices, exchange(): lax.all_to_all(value, axis, split_axis=0, concat_axis=0, tiled=True, axis...  14.3 us
    ppermute x1, starting transfers between devices, body(): other = lax.ppermute(send, 'band', [(i, i ^ 1) for i in range(band_count)])  8.74 us
    pallas_call x1, Pallas kernels, body(): pl.pallas_call(functools.partial(solve_kernel, float(total)), out_shape=j...  6.12 us
    pallas_call x1, Pallas kernels, body(): pl.pallas_call(filter_kernel, out_shape=jax.ShapeDtypeStruct((8, 16, OWN)...  5.17 us
  transfers between devices with their start and end apart: 5, of which 3 were waited for; matrix products, arithmetic and copies ran while one was open for 0% of the time, Pallas kernels for 0%

profile of v4, /device:TPU:1, one launch (start us, length us, event | category | flops | bytes accessed | tf_op | source)
XLA Modules:
  0.0 141.9 jit_solution(9380493663030378438)
XLA Ops:
  0.0 2.5 %pack.1 = (f32[392,256]{1,0:T(8,128)}, f32[392,256]{1,0:T(8,128)}, f32[4,16,648]{2,1,0:T(8,128)}, f32[4,16,648]{2,1,0:T(8,128)}) custom-call(s32[1]{0:T(128)} %bitcast.1.core_ref, s32[1,256]{1,0:T(1,128)} %bitcast.23, s32[1,256]{1,0:T(1,128)} %bitcast.24, f32[729,256]{1,0:T(8,128)} %bitcast.22, f32[1,8]{1,0:T(1,128)} %bitcast.21, f32[16,8,648]{2,1,0:T(8,128)} %own_ref.1), custom_call_target="tpu_custom_call" | custom-call | tf_op jit(solution)/shard_map/pack/pallas_call | solution.py:307
  2.5 8.7 %collective-permute-start = (f32[392,256]{1,0:T(8,128)}, f32[392,256]{1,0:T(8,128)S(1)}, u32[]{:S(2)}, u32[]{:S(2)}) collective-permute-start(f32[392,256]{1,0:T(8,128)} %get-tuple-element.13), channel_id=1, source_target_pairs={{0,1},{1,0},{2,3},{3,2},{4,5},{5,4},{6,7},{7,6},{8,9},{9,8},{10,11... | collective-permute-start | bytes 1204232 | tf_op jit(solution)/shard_map/ppermute | solution.py:323
  11.3 1.5 %collective-permute-done.other_ref = f32[392,256]{1,0:T(8,128)S(1)} collective-permute-done((f32[392,256]{1,0:T(8,128)}, f32[392,256]{1,0:T(8,128)S(1)}, u32[]{:S(2)}, u32[]{:S(2)}) %collective-permute-start) | collective-permute-done | bytes 401440 | tf_op jit(solution)/shard_map/ppermute | solution.py:323
  12.8 0.0 copy-start.2
  12.8 1.0 copy-done.2
  13.8 2.0 %deliver.1 = f32[544,384]{1,0:T(8,128)} custom-call(f32[392,256]{1,0:T(8,128)S(1)} %copy-done.2, f32[392,256]{1,0:T(8,128)S(1)} %collective-permute-done.other_ref), custom_call_target="tpu_custom_call" | custom-call | tf_op jit(solution)/shard_map/deliver/pallas_call | solution.py:324
  15.8 0.0 copy-start
  15.8 0.0 copy-start.1
  15.8 0.0 copy-start.3
  15.8 3.8 %all-to-all-start = ((f32[4,136,384]{2,1,0:T(8,128)}), f32[4,136,384]{2,1,0:T(8,128)S(1)}, u32[]{:S(2)}, u32[]{:S(2)}) async-start(f32[4,136,384]{2,1,0:T(8,128)} %bitcast.6), calls=%async_computation | async-start | bytes 1671168 | tf_op jit(solution)/shard_map/all_to_all | solution.py:28
  19.6 2.0 %collective-permute-start.1 = (f32[4,16,648]{2,1,0:T(8,128)}, f32[4,16,648]{2,1,0:T(8,128)}, u32[]{:S(2)}, u32[]{:S(2)}) collective-permute-start(f32[4,16,648]{2,1,0:T(8,128)} %get-tuple-element.14), channel_id=1, source_target_pairs={{0,8},{8,16},{16,24},{24,32},{32,40},{40,48},{48,56},{56,64},{64,7... | collective-permute-start | bytes 497672 | tf_op jit(solution)/shard_map/ppermute | solution.py:333
  21.6 1.3 collective-permute-start.2
  22.9 13.5 %all-to-all-done.part_ref = f32[4,136,384]{2,1,0:T(8,128)S(1)} async-done(((f32[4,136,384]{2,1,0:T(8,128)}), f32[4,136,384]{2,1,0:T(8,128)S(1)}, u32[]{:S(2)}, u32[]{:S(2)}) %all-to-all-start) | async-done | bytes 835616 | tf_op jit(solution)/shard_map/all_to_all | solution.py:28
  36.4 0.0 collective-permute-done.1.left_ref
  36.4 0.0 collective-permute-done.2.right_ref
  36.4 15.4 %all_to_all.35 = f32[16,16,384]{2,1,0:T(8,128)S(1)} all-to-all(f32[16,16,384]{2,1,0:T(8,128)S(1)} %windows.1), channel_id=1, replica_groups={{0,8,16,24,32,40,48,56,64,72,80,88,96,104,112,120},{128,136,144,152,160..., dimensions={0} | all-to-all | bytes 786432 | tf_op jit(solution)/shard_map/all_to_all | solution.py:28
  51.9 0.7 broadcast_in_dim.6
  52.6 10.6 %all-to-all-start.2 = ((f32[8,16,384]{2,1,0:T(8,128)}), f32[8,16,384]{2,1,0:T(8,128)S(1)}, u32[]{:S(2)}, u32[]{:S(2)}) async-start(f32[8,16,384]{2,1,0:T(8,128)} %broadcast_in_dim.6), calls=%async_computation.2 | async-start | bytes 393216 | tf_op jit(solution)/shard_map/all_to_all | solution.py:28
  63.1 8.7 %all-to-all-done.2.part_ref = f32[8,16,384]{2,1,0:T(8,128)S(1)} async-done(((f32[8,16,384]{2,1,0:T(8,128)}), f32[8,16,384]{2,1,0:T(8,128)S(1)}, u32[]{:S(2)}, u32[]{:S(2)}) %all-to-all-start.2) | async-done | bytes 196640 | tf_op jit(solution)/shard_map/all_to_all | solution.py:28
  71.8 0.0 copy-done
  71.8 0.0 copy-done.1
  71.8 0.0 copy-done.3
  71.8 5.2 %chebyshev.1 = f32[8,16,648]{2,1,0:T(8,128)S(1)} custom-call(s32[1]{0:T(128)} %bitcast.last_ref, f32[8]{0:T(128)S(1)} %copy-done.3, f32[16,8,648]{2,1,0:T(8,128)S(1)} %copy-done.1, f32[4,16,648]{2,1,0:T(8,128)} %collective-permute-done.1.left_ref, f32[4,16,648]{2,1,0:T(8,128)} %collective-permute-done.2.right_ref, ...), custom_call_target="tpu_custom_call" | custom-call | tf_op jit(solution)/shard_map/chebyshev/pallas_call | solution.py:350
  77.0 17.5 %all_to_all.36 = f32[8,16,648]{2,1,0:T(8,128)S(1)} all-to-all(f32[8,16,648]{2,1,0:T(8,128)S(1)} %chebyshev.1), channel_id=1, replica_groups=mesh['dom'=64,'band'=8] {'band'}, dimensions={0} | all-to-all | bytes 663552 | tf_op jit(solution)/shard_map/all_to_all | solution.py:28
  94.5 0.5 fusion
  95.0 12.1 %all_to_all.37 = f32[16,8,128]{2,1,0:T(8,128)S(1)} all-to-all(f32[16,8,128]{2,1,0:T(8,128)S(1)} %fusion), channel_id=1, replica_groups={{0,8,16,24,32,40,48,56,64,72,80,88,96,104,112,120},{128,136,144,152,160..., dimensions={0} | all-to-all | bytes 131072 | tf_op jit(solution)/shard_map/all_to_all | solution.py:28
  107.1 18.1 %all_to_all.38 = f32[32,8,128]{2,1,0:T(8,128)S(1)} all-to-all(f32[32,8,128]{2,1,0:T(8,128)S(1)} %broadcast_in_dim.7), channel_id=1, replica_groups={{0,1,2,3,4,5,6,7,128,129,130,131,132,133,134,135,256,257,258,259,260,26..., dimensions={0} | all-to-all | bytes 262144 | tf_op jit(solution)/shard_map/all_to_all | solution.py:28
  125.3 10.5 %all_to_all.39 = f32[16,8,128]{2,1,0:T(8,128)S(1)} all-to-all(f32[16,8,128]{2,1,0:T(8,128)S(1)} %broadcast_in_dim.8), channel_id=1, replica_groups={{0,8,16,24,32,40,48,56,64,72,80,88,96,104,112,120},{128,136,144,152,160..., dimensions={0} | all-to-all | bytes 131072 | tf_op jit(solution)/shard_map/all_to_all | solution.py:28
  135.8 6.1 %orthonormalize.1 = f32[648,128]{1,0:T(8,128)} custom-call(f32[128,128]{1,0:T(8,128)S(1)} %bitcast.20, f32[128,648]{1,0:T(8,128)S(1)} %bitcast.19), custom_call_target="tpu_custom_call" | custom-call | tf_op jit(solution)/shard_map/orthonormalize/pallas_call | solution.py:378
  (6 shorter events, 0.1 us)
Async XLA Ops:
  2.5 10.3 %collective-permute-start = (f32[392,256]{1,0:T(8,128)}, f32[392,256]{1,0:T(8,128)S(1)}, u32[]{:S(2)}, u32[]{:S(2)}) collective-permute-start(f32[392,256]{1,0:T(8,128)} %get-tuple-element.13), channel_id=1, source_target_pairs={{0,1},{1,0},{2,3},{3,2},{4,5},{5,4},{6,7},{7,6},{8,9},{9,8},{10,11... | collective-permute-start | bytes 1204232 | tf_op jit(solution)/shard_map/ppermute | solution.py:323
  12.8 1.0 copy-start.2
  15.8 56.0 %copy-start = (f32[729,729]{1,0:T(8,128)S(1)}, f32[729,729]{1,0:T(8,128)}, u32[]{:S(2)}) copy-start(f32[729,729]{1,0:T(8,128)} %operator_ref.1) | copy-start | bytes 6377296
  15.8 56.0 %copy-start.1 = (f32[16,8,648]{2,1,0:T(8,128)S(1)}, f32[16,8,648]{2,1,0:T(8,128)}, u32[]{:S(2)}) copy-start(f32[16,8,648]{2,1,0:T(8,128)} %own_ref.1) | copy-start | bytes 995332
  15.8 56.0 %copy-start.3 = (f32[8]{0:T(128)S(1)}, f32[8]{0:T(128)}, u32[]{:S(2)}) copy-start(f32[8]{0:T(128)} %scale_ref.1) | copy-start | bytes 100
  15.8 20.5 %all-to-all-start = ((f32[4,136,384]{2,1,0:T(8,128)}), f32[4,136,384]{2,1,0:T(8,128)S(1)}, u32[]{:S(2)}, u32[]{:S(2)}) async-start(f32[4,136,384]{2,1,0:T(8,128)} %bitcast.6), calls=%async_computation | async-start | bytes 1671168 | tf_op jit(solution)/shard_map/all_to_all | solution.py:28
  19.6 16.8 %collective-permute-start.1 = (f32[4,16,648]{2,1,0:T(8,128)}, f32[4,16,648]{2,1,0:T(8,128)}, u32[]{:S(2)}, u32[]{:S(2)}) collective-permute-start(f32[4,16,648]{2,1,0:T(8,128)} %get-tuple-element.14), channel_id=1, source_target_pairs={{0,8},{8,16},{16,24},{24,32},{32,40},{40,48},{48,56},{56,64},{64,7... | collective-permute-start | bytes 497672 | tf_op jit(solution)/shard_map/ppermute | solution.py:333
  21.6 14.8 %collective-permute-start.2 = (f32[4,16,648]{2,1,0:T(8,128)}, f32[4,16,648]{2,1,0:T(8,128)}, u32[]{:S(2)}, u32[]{:S(2)}) collective-permute-start(f32[4,16,648]{2,1,0:T(8,128)} %get-tuple-element.15), channel_id=1, source_target_pairs={{8,0},{16,8},{24,16},{32,24},{40,32},{48,40},{56,48},{64,56},{72,6... | collective-permute-start | bytes 497672 | tf_op jit(solution)/shard_map/ppermute | solution.py:334
  52.6 19.2 %all-to-all-start.2 = ((f32[8,16,384]{2,1,0:T(8,128)}), f32[8,16,384]{2,1,0:T(8,128)S(1)}, u32[]{:S(2)}, u32[]{:S(2)}) async-start(f32[8,16,384]{2,1,0:T(8,128)} %broadcast_in_dim.6), calls=%async_computation.2 | async-start | bytes 393216 | tf_op jit(solution)/shard_map/all_to_all | solution.py:28

commit v5 on v4

--- a/solution.py
+++ b/solution.py
@@ -21,7 +21,16 @@
 
 X_GROUPS = [[x * 16 + r for x in range(4)] for r in range(16)]
 YZ_GROUPS = [[x * 16 + r for r in range(16)] for x in range(4)]
-XB_GROUPS = [[(x * 16 + r) * 8 + b for x in range(4) for b in range(8)] for r in range(16)]
+
+
+def device(x, y, z_lo, z_hi, core):
+    return ((x * 8 + y) * 2 + z_lo) * 8 + z_hi * 2 + core
+
+
+NEAR_GROUPS = [[device(x, y, l, h, c) for x in range(4) for l in range(2) for c in range(2)]
+               for y in range(8) for h in range(4)]
+FAR_GROUPS = [[device(x, y, l, h, c) for y in range(8) for h in range(4)]
+              for x in range(4) for l in range(2) for c in range(2)]
 
 
 def exchange(value, axis, groups=None):
@@ -89,14 +98,21 @@
         lower(send_ref)
 
 
-def deliver_kernel(own_ref, other_ref, out_ref):
+def deliver_kernel(own_hbm, other_hbm, out_ref, own_ref, other_ref, sems):
+    copies = [
+        pltpu.make_async_copy(own_hbm, own_ref, sems.at[0]),
+        pltpu.make_async_copy(other_hbm, other_ref, sems.at[1]),
+    ]
+    for copy in copies:
+        copy.start()
     rows = 4 * SLAB
     count = own_ref.shape[1]
     row = lax.broadcasted_iota(jnp.int32, (rows, count), 0)
     slab = (row >= SLAB).astype(jnp.int32) + (row >= 2 * SLAB).astype(jnp.int32) + (row >= 3 * SLAB).astype(jnp.int32)
     cell = (row - 8 * slab - 3).astype(jnp.float32)
     total = None
-    for ref in (own_ref, other_ref):
+    for ref, copy in zip((own_ref, other_ref), copies):
+        copy.wait()
         onehot = jnp.where(ref[HALF:HALF + 1, :] == cell, 1.0, 0.0).astype(jnp.bfloat16)
         values = ref[:HALF, :]
         first = values.astype(jnp.bfloat16)
@@ -324,9 +340,14 @@
     delivered = pl.pallas_call(
         deliver_kernel,
         out_shape=jax.ShapeDtypeStruct((4 * SLAB, HALF), jnp.float32),
-        in_specs=[vmem, vmem],
+        in_specs=[hbm, hbm],
         out_specs=vmem,
-        compiler_params=params,
+        scratch_shapes=[
+            pltpu.VMEM((HALF + 8, count), jnp.float32),
+            pltpu.VMEM((HALF + 8, count), jnp.float32),
+            pltpu.SemaphoreType.DMA((2,)),
+        ],
+        compiler_params=roomy,
         name="deliver",
     )(own, other)
 
@@ -370,11 +391,12 @@
     )(alive, cell_scale, orbitals, left, right, part, cell_operator)
 
     flat = exchange(filtered, "band").reshape(128, OWN)
+    both = ("dom", "band")
     total = OWN * dom_count * band_count
     gram = jnp.dot(flat, flat.T, precision=lax.Precision.HIGHEST)
-    part = jnp.sum(exchange(gram.reshape(16, 8, 128), "dom", YZ_GROUPS), 0)
-    part = jnp.sum(exchange(jnp.broadcast_to(part[None], (32, 8, 128)), ("dom", "band"), XB_GROUPS), 0)
-    gram = exchange(jnp.broadcast_to(part[None], (16, 8, 128)), "dom", YZ_GROUPS).reshape(128, 128)
+    part = jnp.sum(exchange(gram.reshape(16, 8, 128), both, NEAR_GROUPS), 0)
+    part = jnp.sum(exchange(jnp.broadcast_to(part[None], (32, 8, 128)), both, FAR_GROUPS), 0)
+    gram = exchange(jnp.broadcast_to(part[None], (16, 8, 128)), both, NEAR_GROUPS).reshape(128, 128)
     basis = pl.pallas_call(
         functools.partial(solve_kernel, float(total)),
         out_shape=jax.ShapeDtypeStruct((OWN, 128), jnp.float32),

time: 142 us -> 140 us (0.986)
  blocking collectives: 73.6 us -> 70.6 us
    all_to_all x5, blocking collectives: 73.6 us -> 70.6 us  [exchange(): lax.all_to_all(value, axis, split_axis=0, concat_axis=0, tiled=True, axis...]
where the time goes in v5:
time: 140 us
  blocking collectives  70.6 us (50%)
  starting transfers between devices  26.3 us (19%)
  waiting for transfers between devices  23.7 us (17%)
  Pallas kernels  16.9 us (12%)
  local copies, waits for them, and re-layouts  1.48 us (1%)
    all_to_all x5, blocking collectives, exchange(): lax.all_to_all(value, axis, split_axis=0, concat_axis=0, tiled=True, axis...  70.6 us
    all_to_all x2, waiting for transfers between devices, exchange(): lax.all_to_all(value, axis, split_axis=0, concat_axis=0, tiled=True, axis...  22.1 us
    all_to_all x2, starting transfers between devices, exchange(): lax.all_to_all(value, axis, split_axis=0, concat_axis=0, tiled=True, axis...  14.3 us
    ppermute x1, starting transfers between devices, body(): other = lax.ppermute(send, 'band', [(i, i ^ 1) for i in range(band_count)])  8.74 us
    pallas_call x1, Pallas kernels, body(): pl.pallas_call(functools.partial(solve_kernel, float(total)), out_shape=j...  6.12 us
    pallas_call x1, Pallas kernels, body(): pl.pallas_call(filter_kernel, out_shape=jax.ShapeDtypeStruct((8, 16, OWN)...  5.17 us
    pallas_call x1, Pallas kernels, body(): pl.pallas_call(deliver_kernel, out_shape=jax.ShapeDtypeStruct((4 * SLAB,...  3.07 us
  transfers between devices with their start and end apart: 5, of which 3 were waited for; matrix products, arithmetic and copies ran while one was open for 0% of the time, Pallas kernels for 0%

profile of v5, /device:TPU:1, one launch (start us, length us, event | category | flops | bytes accessed | tf_op | source)
XLA Modules:
  0.0 139.7 jit_solution(18367783959515206019)
XLA Ops:
  0.0 2.5 %pack.1 = (f32[392,256]{1,0:T(8,128)}, f32[392,256]{1,0:T(8,128)}, f32[4,16,648]{2,1,0:T(8,128)}, f32[4,16,648]{2,1,0:T(8,128)}) custom-call(s32[1]{0:T(128)} %bitcast.1.core_ref, s32[1,256]{1,0:T(1,128)} %bitcast.24, s32[1,256]{1,0:T(1,128)} %bitcast.25, f32[729,256]{1,0:T(8,128)} %bitcast.23, f32[1,8]{1,0:T(1,128)} %bitcast.21, f32[16,8,648]{2,1,0:T(8,128)} %own_ref.1), custom_call_target="tpu_custom_call" | custom-call | tf_op jit(solution)/shard_map/pack/pallas_call | solution.py:323
  2.5 8.7 %collective-permute-start = (f32[392,256]{1,0:T(8,128)}, f32[392,256]{1,0:T(8,128)S(1)}, u32[]{:S(2)}, u32[]{:S(2)}) collective-permute-start(f32[392,256]{1,0:T(8,128)} %get-tuple-element.13), channel_id=1, source_target_pairs={{0,1},{1,0},{2,3},{3,2},{4,5},{5,4},{6,7},{7,6},{8,9},{9,8},{10,11... | collective-permute-start | bytes 1204232 | tf_op jit(solution)/shard_map/ppermute | solution.py:339
  11.3 1.5 %collective-permute-done.other_hbm = f32[392,256]{1,0:T(8,128)S(1)} collective-permute-done((f32[392,256]{1,0:T(8,128)}, f32[392,256]{1,0:T(8,128)S(1)}, u32[]{:S(2)}, u32[]{:S(2)}) %collective-permute-start) | collective-permute-done | bytes 401440 | tf_op jit(solution)/shard_map/ppermute | solution.py:339
  12.8 0.0 copy-start.3
  12.8 0.7 copy-done.3
  13.6 3.1 %deliver.1 = f32[544,384]{1,0:T(8,128)} custom-call(f32[392,256]{1,0:T(8,128)} %get-tuple-element.12.own_hbm, f32[392,256]{1,0:T(8,128)} %copy-done.3), custom_call_target="tpu_custom_call" | custom-call | tf_op jit(solution)/shard_map/deliver/pallas_call | solution.py:340
  16.6 0.0 copy-start
  16.7 0.0 copy-start.1
  16.7 0.0 copy-start.2
  16.7 3.8 %all-to-all-start = ((f32[4,136,384]{2,1,0:T(8,128)}), f32[4,136,384]{2,1,0:T(8,128)S(1)}, u32[]{:S(2)}, u32[]{:S(2)}) async-start(f32[4,136,384]{2,1,0:T(8,128)} %bitcast.22), calls=%async_computation | async-start | bytes 1671168 | tf_op jit(solution)/shard_map/all_to_all | solution.py:37
  20.5 2.0 %collective-permute-start.1 = (f32[4,16,648]{2,1,0:T(8,128)}, f32[4,16,648]{2,1,0:T(8,128)}, u32[]{:S(2)}, u32[]{:S(2)}) collective-permute-start(f32[4,16,648]{2,1,0:T(8,128)} %get-tuple-element.14), channel_id=1, source_target_pairs={{0,8},{8,16},{16,24},{24,32},{32,40},{40,48},{48,56},{56,64},{64,7... | collective-permute-start | bytes 497672 | tf_op jit(solution)/shard_map/ppermute | solution.py:354
  22.4 1.3 collective-permute-start.2
  23.7 13.5 %all-to-all-done.part_ref = f32[4,136,384]{2,1,0:T(8,128)S(1)} async-done(((f32[4,136,384]{2,1,0:T(8,128)}), f32[4,136,384]{2,1,0:T(8,128)S(1)}, u32[]{:S(2)}, u32[]{:S(2)}) %all-to-all-start) | async-done | bytes 835616 | tf_op jit(solution)/shard_map/all_to_all | solution.py:37
  37.3 0.0 collective-permute-done.1.left_ref
  37.3 0.0 collective-permute-done.2.right_ref
  37.3 15.4 %all_to_all.35 = f32[16,16,384]{2,1,0:T(8,128)S(1)} all-to-all(f32[16,16,384]{2,1,0:T(8,128)S(1)} %windows.1), channel_id=1, replica_groups={{0,8,16,24,32,40,48,56,64,72,80,88,96,104,112,120},{128,136,144,152,160..., dimensions={0} | all-to-all | bytes 786432 | tf_op jit(solution)/shard_map/all_to_all | solution.py:37
  52.7 0.7 broadcast_in_dim.6
  53.4 10.6 %all-to-all-start.2 = ((f32[8,16,384]{2,1,0:T(8,128)}), f32[8,16,384]{2,1,0:T(8,128)S(1)}, u32[]{:S(2)}, u32[]{:S(2)}) async-start(f32[8,16,384]{2,1,0:T(8,128)} %broadcast_in_dim.6), calls=%async_computation.2 | async-start | bytes 393216 | tf_op jit(solution)/shard_map/all_to_all | solution.py:37
  64.0 8.7 %all-to-all-done.2.part_ref = f32[8,16,384]{2,1,0:T(8,128)S(1)} async-done(((f32[8,16,384]{2,1,0:T(8,128)}), f32[8,16,384]{2,1,0:T(8,128)S(1)}, u32[]{:S(2)}, u32[]{:S(2)}) %all-to-all-start.2) | async-done | bytes 196640 | tf_op jit(solution)/shard_map/all_to_all | solution.py:37
  72.7 0.0 copy-done
  72.7 0.0 copy-done.1
  72.7 0.0 copy-done.2
  72.7 5.2 %chebyshev.1 = f32[8,16,648]{2,1,0:T(8,128)S(1)} custom-call(s32[1]{0:T(128)} %bitcast.last_ref, f32[8]{0:T(128)S(1)} %copy-done.2, f32[16,8,648]{2,1,0:T(8,128)S(1)} %copy-done.1, f32[4,16,648]{2,1,0:T(8,128)} %collective-permute-done.1.left_ref, f32[4,16,648]{2,1,0:T(8,128)} %collective-permute-done.2.right_ref, ...), custom_call_target="tpu_custom_call" | custom-call | tf_op jit(solution)/shard_map/chebyshev/pallas_call | solution.py:371
  77.9 17.5 %all_to_all.36 = f32[8,16,648]{2,1,0:T(8,128)S(1)} all-to-all(f32[8,16,648]{2,1,0:T(8,128)S(1)} %chebyshev.1), channel_id=1, replica_groups=mesh['dom'=64,'band'=8] {'band'}, dimensions={0} | all-to-all | bytes 663552 | tf_op jit(solution)/shard_map/all_to_all | solution.py:37
  95.4 0.5 fusion
  95.8 12.7 %all_to_all.37 = f32[16,8,128]{2,1,0:T(8,128)S(1)} all-to-all(f32[16,8,128]{2,1,0:T(8,128)S(1)} %fusion), channel_id=1, replica_groups={{0,1,8,9,128,129,136,137,256,257,264,265,384,385,392,393},{2,3,10,11,13..., dimensions={0} | all-to-all | bytes 131072 | tf_op jit(solution)/shard_map/all_to_all | solution.py:37
  108.5 14.8 %all_to_all.38 = f32[32,8,128]{2,1,0:T(8,128)S(1)} all-to-all(f32[32,8,128]{2,1,0:T(8,128)S(1)} %broadcast_in_dim.7), channel_id=1, replica_groups={{0,2,4,6,16,18,20,22,32,34,36,38,48,50,52,54,64,66,68,70,80,82,84,86,96..., dimensions={0} | all-to-all | bytes 262144 | tf_op jit(solution)/shard_map/all_to_all | solution.py:37
  123.4 10.3 %all_to_all.39 = f32[16,8,128]{2,1,0:T(8,128)S(1)} all-to-all(f32[16,8,128]{2,1,0:T(8,128)S(1)} %broadcast_in_dim.8), channel_id=1, replica_groups={{0,1,8,9,128,129,136,137,256,257,264,265,384,385,392,393},{2,3,10,11,13..., dimensions={0} | all-to-all | bytes 131072 | tf_op jit(solution)/shard_map/all_to_all | solution.py:37
  133.6 6.1 %orthonormalize.1 = f32[648,128]{1,0:T(8,128)} custom-call(f32[128,128]{1,0:T(8,128)S(1)} %bitcast.20, f32[128,648]{1,0:T(8,128)S(1)} %bitcast.19), custom_call_target="tpu_custom_call" | custom-call | tf_op jit(solution)/shard_map/orthonormalize/pallas_call | solution.py:400
  (6 shorter events, 0.1 us)
Async XLA Ops:
  2.5 10.3 %collective-permute-start = (f32[392,256]{1,0:T(8,128)}, f32[392,256]{1,0:T(8,128)S(1)}, u32[]{:S(2)}, u32[]{:S(2)}) collective-permute-start(f32[392,256]{1,0:T(8,128)} %get-tuple-element.13), channel_id=1, source_target_pairs={{0,1},{1,0},{2,3},{3,2},{4,5},{5,4},{6,7},{7,6},{8,9},{9,8},{10,11... | collective-permute-start | bytes 1204232 | tf_op jit(solution)/shard_map/ppermute | solution.py:339
  12.8 0.7 copy-start.3
  16.6 56.0 %copy-start = (f32[729,729]{1,0:T(8,128)S(1)}, f32[729,729]{1,0:T(8,128)}, u32[]{:S(2)}) copy-start(f32[729,729]{1,0:T(8,128)} %operator_ref.1) | copy-start | bytes 6377296
  16.7 56.0 %copy-start.1 = (f32[16,8,648]{2,1,0:T(8,128)S(1)}, f32[16,8,648]{2,1,0:T(8,128)}, u32[]{:S(2)}) copy-start(f32[16,8,648]{2,1,0:T(8,128)} %own_ref.1) | copy-start | bytes 995332
  16.7 56.0 %copy-start.2 = (f32[8]{0:T(128)S(1)}, f32[8]{0:T(128)}, u32[]{:S(2)}) copy-start(f32[8]{0:T(128)} %scale_ref.1) | copy-start | bytes 100
  16.7 20.5 %all-to-all-start = ((f32[4,136,384]{2,1,0:T(8,128)}), f32[4,136,384]{2,1,0:T(8,128)S(1)}, u32[]{:S(2)}, u32[]{:S(2)}) async-start(f32[4,136,384]{2,1,0:T(8,128)} %bitcast.22), calls=%async_computation | async-start | bytes 1671168 | tf_op jit(solution)/shard_map/all_to_all | solution.py:37
  20.5 16.8 %collective-permute-start.1 = (f32[4,16,648]{2,1,0:T(8,128)}, f32[4,16,648]{2,1,0:T(8,128)}, u32[]{:S(2)}, u32[]{:S(2)}) collective-permute-start(f32[4,16,648]{2,1,0:T(8,128)} %get-tuple-element.14), channel_id=1, source_target_pairs={{0,8},{8,16},{16,24},{24,32},{32,40},{40,48},{48,56},{56,64},{64,7... | collective-permute-start | bytes 497672 | tf_op jit(solution)/shard_map/ppermute | solution.py:354
  22.4 14.8 %collective-permute-start.2 = (f32[4,16,648]{2,1,0:T(8,128)}, f32[4,16,648]{2,1,0:T(8,128)}, u32[]{:S(2)}, u32[]{:S(2)}) collective-permute-start(f32[4,16,648]{2,1,0:T(8,128)} %get-tuple-element.15), channel_id=1, source_target_pairs={{8,0},{16,8},{24,16},{32,24},{40,32},{48,40},{56,48},{64,56},{72,6... | collective-permute-start | bytes 497672 | tf_op jit(solution)/shard_map/ppermute | solution.py:355
  53.4 19.2 %all-to-all-start.2 = ((f32[8,16,384]{2,1,0:T(8,128)}), f32[8,16,384]{2,1,0:T(8,128)S(1)}, u32[]{:S(2)}, u32[]{:S(2)}) async-start(f32[8,16,384]{2,1,0:T(8,128)} %broadcast_in_dim.6), calls=%async_computation.2 | async-start | bytes 393216 | tf_op jit(solution)/shard_map/all_to_all | solution.py:37

commit v6 on v4

--- a/solution.py
+++ b/solution.py
@@ -21,7 +21,16 @@
 
 X_GROUPS = [[x * 16 + r for x in range(4)] for r in range(16)]
 YZ_GROUPS = [[x * 16 + r for r in range(16)] for x in range(4)]
-XB_GROUPS = [[(x * 16 + r) * 8 + b for x in range(4) for b in range(8)] for r in range(16)]
+
+
+def device(x, y, z_lo, z_hi, core):
+    return ((x * 8 + y) * 2 + z_lo) * 8 + z_hi * 2 + core
+
+
+NEAR_GROUPS = [[device(x, y, l, h, c) for x in range(4) for l in range(2) for c in range(2)]
+               for y in range(8) for h in range(4)]
+FAR_GROUPS = [[device(x, y, l, h, c) for y in range(8) for h in range(4)]
+              for x in range(4) for l in range(2) for c in range(2)]
 
 
 def exchange(value, axis, groups=None):
@@ -56,14 +65,17 @@
         copy.start()
     for copy in copies:
         copy.wait()
-    for c in range(3):
-        left_ref[c] = orbitals_ref[:, 5 + c, :]
-        right_ref[c] = orbitals_ref[:, c, :]
-    diagonal = lax.broadcasted_iota(jnp.int32, (8, 8), 0) == lax.broadcasted_iota(jnp.int32, (8, 8), 1)
-    column = jnp.sum(jnp.where(diagonal, jnp.broadcast_to(scale_ref[...], (8, 8)), 0.0), 1, keepdims=True)
-    for ref in (left_ref, right_ref):
-        ref[3, :8, :] = jnp.broadcast_to(column, (8, OWN))
-        ref[3, 8:, :] = jnp.zeros((8, OWN), jnp.float32)
+    def ghost(ref, place, c):
+        value = orbitals_ref[:, c, :]
+        scale = jnp.broadcast_to(scale_ref[:, c:c + 1], (16, 128 - SPLIT))
+        ref[:, WIDE * place:WIDE * place + TILE5] = value[:, :TILE5]
+        ref[:, WIDE * place + TILE5:WIDE * place + WIDE] = jnp.concatenate([value[:, TILE5:], scale], 1)
+
+    for place in range(3):
+        ghost(left_ref, place, 5 + place)
+    for place in range(2):
+        ghost(right_ref, place, place)
+    right_ref[:, 2 * WIDE:] = orbitals_ref[:, 2, :128]
     count = density_ref.shape[1]
     target = (owner_ref[...] * 8 + cell_ref[...]).astype(jnp.float32)
     target = jnp.broadcast_to(target, (8, count))
@@ -89,23 +101,22 @@
         lower(send_ref)
 
 
-def deliver_kernel(own_ref, other_ref, out_ref):
+def cell_sums(ref):
     rows = 4 * SLAB
-    count = own_ref.shape[1]
-    row = lax.broadcasted_iota(jnp.int32, (rows, count), 0)
+    row = lax.broadcasted_iota(jnp.int32, (rows, ref.shape[1]), 0)
     slab = (row >= SLAB).astype(jnp.int32) + (row >= 2 * SLAB).astype(jnp.int32) + (row >= 3 * SLAB).astype(jnp.int32)
     cell = (row - 8 * slab - 3).astype(jnp.float32)
-    total = None
-    for ref in (own_ref, other_ref):
-        onehot = jnp.where(ref[HALF:HALF + 1, :] == cell, 1.0, 0.0).astype(jnp.bfloat16)
-        values = ref[:HALF, :]
-        first = values.astype(jnp.bfloat16)
-        rest = values - first.astype(jnp.float32)
-        second = rest.astype(jnp.bfloat16)
-        third = (rest - second.astype(jnp.float32)).astype(jnp.bfloat16)
-        part = dot_nt(onehot, first) + dot_nt(onehot, second) + dot_nt(onehot, third)
-        total = part if total is None else total + part
-    out_ref[...] = total
+    onehot = jnp.where(ref[HALF:HALF + 1, :] == cell, 1.0, 0.0).astype(jnp.bfloat16)
+    high, low = split2(ref[:HALF, :])
+    return dot_nt(onehot, high) + dot_nt(onehot, low)
+
+
+def own_kernel(own_ref, out_ref):
+    out_ref[...] = cell_sums(own_ref)
+
+
+def deliver_kernel(own_ref, other_ref, out_ref):
+    out_ref[...] = own_ref[...] + cell_sums(other_ref)
 
 
 def window_kernel(part_ref, out_ref):
@@ -118,15 +129,65 @@
             out_ref[k - 1, 8:, :] = block
 
 
-def filter_kernel(last_ref, scale_ref, own_ref, left_ref, right_ref, part_ref, operator_ref, out_ref,
-                  kwide, khigh, klow, v0, v1, v2, chigh, clow, cell_buf, product, pot):
+def cell_vectors(source, begin, end, cell_buf, chigh, clow):
+    is_face = lax.broadcasted_iota(jnp.int32, (16, 128), 1) < FACE
+    for i in range(begin, end):
+        r = slice(16 * i, 16 * i + 16)
+        n = slice(16 * i + 16, 16 * i + 32)
+        for t in range(6):
+            c = slice(128 * t, 128 * t + 128)
+            value = source[r, c]
+            if t == 5:
+                face = jnp.where(is_face, source[n, :128], 0.0)
+                value = value + pltpu.roll(face, SPLIT, 1)
+            cell_buf[r, c] = value
+            high, low = split2(value)
+            chigh[r, c] = high
+            clow[r, c] = low
+
+
+def products(begin, end, product, chigh, clow, ksplit):
+    r = slice(16 * begin, 16 * end)
+    a, b = chigh[r, :], clow[r, :]
+    khigh, klow = ksplit[:WIDE, :], ksplit[WIDE:, :]
+    product[r, :] = dot(a, khigh) + dot(b, khigh) + dot(a, klow)
+
+
+def first_vectors(own_ref, left_ref, right_ref, v0, cell_buf, chigh, clow):
+    zero5 = jnp.zeros((16, WIDE - TILE5), jnp.float32)
+
+    def place(i, value):
+        v0[16 * i:16 * i + 16, TILE5:] = zero5
+        v0[16 * i:16 * i + 16, :OWN] = value
+
+    own_lane = lax.broadcasted_iota(jnp.int32, (16, 128), 1) < SPLIT
+
+    def ghost(i, ref, begin):
+        v0[16 * i:16 * i + 16, :TILE5] = ref[:, begin:begin + TILE5]
+        v0[16 * i:16 * i + 16, TILE5:] = jnp.where(own_lane, ref[:, begin + TILE5:begin + WIDE], 0.0)
+
+    for i in range(3):
+        ghost(i, left_ref, WIDE * i)
+    for i in range(2):
+        ghost(11 + i, right_ref, WIDE * i)
+    v0[16 * 13:, :128] = right_ref[:, 2 * WIDE:]
+    for i in range(8):
+        place(3 + i, own_ref[:, i, :])
+    cell_vectors(v0, 0, 13, cell_buf, chigh, clow)
+
+
+def split_kernel(operator_ref, ksplit, kwide):
     kwide[720:, :] = jnp.zeros((WIDE - 720, WIDE), jnp.float32)
     kwide[:, TILE5:] = jnp.zeros((WIDE, WIDE - TILE5), jnp.float32)
     kwide[:NODES, :NODES] = operator_ref[...]
     for i in range(0, WIDE, 128):
         high, low = split2(kwide[i:i + 128, :])
-        khigh[i:i + 128, :] = high
-        klow[i:i + 128, :] = low
+        ksplit[i:i + 128, :] = high
+        ksplit[WIDE + i:WIDE + i + 128, :] = low
+
+
+def filter_kernel(last_ref, scale_ref, own_ref, left_ref, right_ref, part_ref, ksplit, out_ref,
+                  v0, v1, v2, chigh, clow, cell_buf, product, pot):
     for half in range(2):
         rho = (part_ref[half] + part_ref[half + 2]) + (part_ref[half + 4] + part_ref[half + 6])
         pot[:, half * HALF:(half + 1) * HALF] = jnp.where(
@@ -134,46 +195,19 @@
     lane = lax.broadcasted_iota(jnp.int32, (16, 128), 1)
     is_face = lane < FACE
     is_own5 = lane < SPLIT
-    zero5 = jnp.zeros((16, WIDE - TILE5), jnp.float32)
-
-    def place(i, value):
-        v0[16 * i:16 * i + 16, TILE5:] = zero5
-        v0[16 * i:16 * i + 16, :OWN] = value
-
-    for i in range(3):
-        place(i, left_ref[i])
-        place(11 + i, right_ref[i])
-    for i in range(8):
-        place(3 + i, own_ref[:, i, :])
 
     def scale_of(i):
         if i < 3:
-            line = left_ref[3, 5 + i:6 + i, :128]
+            line = left_ref[:, WIDE * i + OWN:WIDE * i + OWN + 1]
         elif i < 11:
             line = scale_ref[i - 3]
         else:
-            line = right_ref[3, i - 11:i - 10, :128]
+            line = right_ref[:, WIDE * (i - 11) + OWN:WIDE * (i - 11) + OWN + 1]
         return line
 
     alive = last_ref[0].astype(jnp.float32)
 
-    def apply(source, begin, end, combine):
-        for i in range(begin, end):
-            r = slice(16 * i, 16 * i + 16)
-            n = slice(16 * i + 16, 16 * i + 32)
-            for t in range(6):
-                c = slice(128 * t, 128 * t + 128)
-                value = source[r, c]
-                if t == 5:
-                    face = jnp.where(is_face, source[n, :128], 0.0)
-                    value = value + pltpu.roll(face, SPLIT, 1)
-                cell_buf[r, c] = value
-                high, low = split2(value)
-                chigh[r, c] = high
-                clow[r, c] = low
-        r = slice(16 * begin, 16 * end)
-        a, b = chigh[r, :], clow[r, :]
-        product[r, :] = dot(a, khigh[...]) + dot(b, khigh[...]) + dot(a, klow[...])
+    def assemble(begin, end, product, cells, combine):
         tail = None
         for i in range(begin, end):
             r = slice(16 * i, 16 * i + 16)
@@ -181,7 +215,7 @@
             parts = []
             for t in range(6):
                 c = slice(128 * t, 128 * t + 128)
-                parts.append(scale * product[r, c] + pot[i:i + 1, c] * cell_buf[r, c])
+                parts.append(scale * product[r, c] + pot[i:i + 1, c] * cells[r, c])
             if tail is not None:
                 add = jnp.where(is_face, pltpu.roll(tail, 128 - SPLIT, 1), 0.0)
                 if i == 11:
@@ -194,6 +228,11 @@
                     combine(i, t, value)
             tail = parts[5]
 
+    def apply(source, begin, end, combine):
+        cell_vectors(source, begin, end, cell_buf, chigh, clow)
+        products(begin, end, product, chigh, clow, ksplit)
+        assemble(begin, end, product, cell_buf, combine)
+
     def at(ref, i, t):
         return ref[16 * i:16 * i + 16, 128 * t:128 * t + 128]
 
@@ -210,7 +249,9 @@
         else:
             out_ref[i - 3, :, TILE5:OWN] = result[:, :SPLIT]
 
-    apply(v0, 0, 13, first)
+    first_vectors(own_ref, left_ref, right_ref, v0, cell_buf, chigh, clow)
+    products(0, 13, product, chigh, clow, ksplit)
+    assemble(0, 13, product, cell_buf, first)
     apply(v1, 1, 12, second)
     apply(v2, 2, 11, third)
 
@@ -303,10 +344,11 @@
 
     count = density.shape[0]
     pack_shape = jax.ShapeDtypeStruct((HALF + 8, count), jnp.float32)
-    ghost_shape = jax.ShapeDtypeStruct((4, 16, OWN), jnp.float32)
+    left_shape = jax.ShapeDtypeStruct((16, 3 * WIDE), jnp.float32)
+    right_shape = jax.ShapeDtypeStruct((16, 2 * WIDE + 128), jnp.float32)
     own, send, send_left, send_right = pl.pallas_call(
         pack_kernel,
-        out_shape=(pack_shape, pack_shape, ghost_shape, ghost_shape),
+        out_shape=(pack_shape, pack_shape, left_shape, right_shape),
         in_specs=[smem] + [hbm] * 5,
         out_specs=(vmem,) * 4,
         scratch_shapes=[
@@ -321,6 +363,14 @@
         name="pack",
     )(core, block_owner.reshape(1, -1), block_cell.reshape(1, -1), density.T, cell_scale.reshape(1, -1), orbitals)
     other = lax.ppermute(send, "band", [(i, i ^ 1) for i in range(band_count)])
+    own = pl.pallas_call(
+        own_kernel,
+        out_shape=jax.ShapeDtypeStruct((4 * SLAB, HALF), jnp.float32),
+        in_specs=[vmem],
+        out_specs=vmem,
+        compiler_params=params,
+        name="own_sums",
+    )(own)
     delivered = pl.pallas_call(
         deliver_kernel,
         out_shape=jax.ShapeDtypeStruct((4 * SLAB, HALF), jnp.float32),
@@ -345,17 +395,24 @@
     windows, left, right = lax.optimization_barrier((windows, left, right))
     part = exchange(windows, "dom", YZ_GROUPS)
     window = jnp.sum(part, 0)
+    window, operator = lax.optimization_barrier((window, cell_operator))
     part = exchange(jnp.broadcast_to(window[None], (band_count, 16, HALF)), "band")
 
+    ksplit = pl.pallas_call(
+        split_kernel,
+        out_shape=jax.ShapeDtypeStruct((2 * WIDE, WIDE), jnp.bfloat16),
+        in_specs=[vmem],
+        out_specs=vmem,
+        scratch_shapes=[pltpu.VMEM((WIDE, WIDE), jnp.float32)],
+        compiler_params=params,
+        name="split_operator",
+    )(operator)
     filtered = pl.pallas_call(
         filter_kernel,
         out_shape=jax.ShapeDtypeStruct((8, 16, OWN), jnp.float32),
         in_specs=[smem] * 2 + [vmem] * 5,
         out_specs=vmem,
         scratch_shapes=[
-            pltpu.VMEM((WIDE, WIDE), jnp.float32),
-            pltpu.VMEM((WIDE, WIDE), jnp.bfloat16),
-            pltpu.VMEM((WIDE, WIDE), jnp.bfloat16),
             pltpu.VMEM((224, WIDE), jnp.float32),
             pltpu.VMEM((224, WIDE), jnp.float32),
             pltpu.VMEM((224, WIDE), jnp.float32),
@@ -367,14 +424,15 @@
         ],
         compiler_params=params,
         name="chebyshev",
-    )(alive, cell_scale, orbitals, left, right, part, cell_operator)
+    )(alive, cell_scale, orbitals, left, right, part, ksplit)
 
     flat = exchange(filtered, "band").reshape(128, OWN)
+    both = ("dom", "band")
     total = OWN * dom_count * band_count
     gram = jnp.dot(flat, flat.T, precision=lax.Precision.HIGHEST)
-    part = jnp.sum(exchange(gram.reshape(16, 8, 128), "dom", YZ_GROUPS), 0)
-    part = jnp.sum(exchange(jnp.broadcast_to(part[None], (32, 8, 128)), ("dom", "band"), XB_GROUPS), 0)
-    gram = exchange(jnp.broadcast_to(part[None], (16, 8, 128)), "dom", YZ_GROUPS).reshape(128, 128)
+    part = jnp.sum(exchange(gram.reshape(16, 8, 128), both, NEAR_GROUPS), 0)
+    part = jnp.sum(exchange(jnp.broadcast_to(part[None], (32, 8, 128)), both, FAR_GROUPS), 0)
+    gram = exchange(jnp.broadcast_to(part[None], (16, 8, 128)), both, NEAR_GROUPS).reshape(128, 128)
     basis = pl.pallas_call(
         functools.partial(solve_kernel, float(total)),
         out_shape=jax.ShapeDtypeStruct((OWN, 128), jnp.float32),

time: 142 us -> 134 us (0.944)
  blocking collectives: 73.6 us -> 69.2 us
  waiting for transfers between devices: 23.7 us -> 19.4 us
  local copies, waits for them, and re-layouts: 1.72 us -> 3.37 us
  starting transfers between devices: 26.3 us -> 24.8 us
    all_to_all x5, blocking collectives: 73.6 us -> 69.2 us  [exchange(): lax.all_to_all(value, axis, split_axis=0, concat_axis=0, tiled=True, axis...]
    all_to_all x2, waiting for transfers between devices: 22.1 us -> 19.3 us  [exchange(): lax.all_to_all(value, axis, split_axis=0, concat_axis=0, tiled=True, axis...]
    unnamed x8 -> x12, local copies, waits for them, and re-layouts: 1.01 us -> 2.66 us
    ppermute x1, waiting for transfers between devices: 1.55 us -> 0.06 us  [body(): other = lax.ppermute(send, 'band', [(i, i ^ 1) for i in range(band_count)])]
    pallas_call x1 -> x3, Pallas kernels: 2.53 us -> 3.62 us  [the longest x1 2.41 us: body(): pl.pallas_call(pack_kernel, out_shape=(pack_shape, pack_shape, left_shape...]
  transfers between devices with their start and end apart: 5 -> 5, of which waited for: 3 -> 3; matrix products, arithmetic and copies ran while one was open for 0% -> 0% of each run, Pallas kernels for 0% -> 1%
where the time goes in v6:
time: 134 us; the launch traced here: 133 us
  blocking collectives  69.2 us (52%)
  starting transfers between devices  24.8 us (19%)
  waiting for transfers between devices  19.4 us (14%)
  Pallas kernels  15.7 us (12%)
  local copies, waits for them, and re-layouts  3.37 us (3%)
    all_to_all x5, blocking collectives, exchange(): lax.all_to_all(value, axis, split_axis=0, concat_axis=0, tiled=True, axis...  69.2 us
    all_to_all x2, waiting for transfers between devices, exchange(): lax.all_to_all(value, axis, split_axis=0, concat_axis=0, tiled=True, axis...  19.3 us
    all_to_all x2, starting transfers between devices, exchange(): lax.all_to_all(value, axis, split_axis=0, concat_axis=0, tiled=True, axis...  13.4 us
    ppermute x1, starting transfers between devices, body(): other = lax.ppermute(send, 'band', [(i, i ^ 1) for i in range(band_count)])  8.79 us
    pallas_call x1, Pallas kernels, body(): pl.pallas_call(functools.partial(solve_kernel, float(total)), out_shape=j...  6.12 us
    pallas_call x1, Pallas kernels, body(): pl.pallas_call(filter_kernel, out_shape=jax.ShapeDtypeStruct((8, 16, OWN)...  4.57 us
  transfers between devices with their start and end apart: 5, of which 3 were waited for; matrix products, arithmetic and copies ran while one was open for 0% of the time, Pallas kernels for 1%

profile of v6, /device:TPU:1, one launch (start us, length us, event | category | flops | bytes accessed | tf_op | source)
XLA Modules:
  0.0 133.2 jit_solution(13352544909796416845)
XLA Ops:
  0.0 2.4 %pack.1 = (f32[392,256]{1,0:T(8,128)}, f32[392,256]{1,0:T(8,128)}, f32[16,2304]{1,0:T(8,128)}, f32[16,1664]{1,0:T(8,128)}) custom-call(s32[1]{0:T(128)} %bitcast.1.core_ref, s32[1,256]{1,0:T(1,128)} %bitcast.23, s32[1,256]{1,0:T(1,128)} %bitcast.24, f32[729,256]{1,0:T(8,128)} %bitcast.22, f32[1,8]{1,0:T(1,128)} %bitcast.21, f32[16,8,648]{2,1,0:T(8,128)} %own_ref.1), custom_call_target="tpu_custom_call" | custom-call | tf_op jit(solution)/shard_map/pack/pallas_call | solution.py:349
  2.4 8.8 %collective-permute-start = (f32[392,256]{1,0:T(8,128)}, f32[392,256]{1,0:T(8,128)S(1)}, u32[]{:S(2)}, u32[]{:S(2)}) collective-permute-start(f32[392,256]{1,0:T(8,128)} %get-tuple-element.15), channel_id=1, source_target_pairs={{0,1},{1,0},{2,3},{3,2},{4,5},{5,4},{6,7},{7,6},{8,9},{9,8},{10,11... | collective-permute-start | bytes 1204232 | tf_op jit(solution)/shard_map/ppermute | solution.py:365
  11.2 0.0 copy-start.2
  11.2 1.0 copy-done.2
  12.2 0.0 copy-start.4
  12.2 0.5 own_sums.1.own_ref
  12.7 0.1 collective-permute-done.other_ref
  12.8 1.4 %deliver.1 = f32[544,384]{1,0:T(8,128)} custom-call(f32[544,384]{1,0:T(8,128)S(1)} %own_sums.1.own_ref, f32[392,256]{1,0:T(8,128)S(1)} %collective-permute-done.other_ref), custom_call_target="tpu_custom_call" | custom-call | tf_op jit(solution)/shard_map/deliver/pallas_call | solution.py:374
  14.2 3.5 %all-to-all-start = ((f32[4,136,384]{2,1,0:T(8,128)}), f32[4,136,384]{2,1,0:T(8,128)S(1)}, u32[]{:S(2)}, u32[]{:S(2)}) async-start(f32[4,136,384]{2,1,0:T(8,128)} %bitcast.6), calls=%async_computation | async-start | bytes 1671168 | tf_op jit(solution)/shard_map/all_to_all | solution.py:37
  17.7 0.0 copy-done.4
  17.7 1.3 collective-permute-start.1
  19.0 0.0 copy-done.5
  19.0 1.3 collective-permute-start.2
  20.3 13.1 %all-to-all-done.part_ref = f32[4,136,384]{2,1,0:T(8,128)S(1)} async-done(((f32[4,136,384]{2,1,0:T(8,128)}), f32[4,136,384]{2,1,0:T(8,128)S(1)}, u32[]{:S(2)}, u32[]{:S(2)}) %all-to-all-start) | async-done | bytes 835616 | tf_op jit(solution)/shard_map/all_to_all | solution.py:37
  33.4 0.0 collective-permute-done.2.right_ref
  33.4 0.0 collective-permute-done.1.left_ref
  33.4 15.5 %all_to_all.35 = f32[16,16,384]{2,1,0:T(8,128)S(1)} all-to-all(f32[16,16,384]{2,1,0:T(8,128)S(1)} %windows.1), channel_id=1, replica_groups={{0,8,16,24,32,40,48,56,64,72,80,88,96,104,112,120},{128,136,144,152,160..., dimensions={0} | all-to-all | bytes 786432 | tf_op jit(solution)/shard_map/all_to_all | solution.py:37
  48.9 0.7 broadcast_in_dim.6
  49.6 0.0 copy-start.1
  49.6 9.9 %all-to-all-start.2 = ((f32[8,16,384]{2,1,0:T(8,128)}), f32[8,16,384]{2,1,0:T(8,128)S(1)}, u32[]{:S(2)}, u32[]{:S(2)}) async-start(f32[8,16,384]{2,1,0:T(8,128)} %broadcast_in_dim.6), calls=%async_computation.2 | async-start | bytes 393216 | tf_op jit(solution)/shard_map/all_to_all | solution.py:37
  59.5 1.6 %copy-done = f32[729,729]{1,0:T(8,128)S(1)} copy-done((f32[729,729]{1,0:T(8,128)S(1)}, f32[729,729]{1,0:T(8,128)}, u32[]{:S(2)}) %copy-start) | copy-done | bytes 2125788
  61.2 0.7 split_operator.1.ksplit
  61.9 6.3 %all-to-all-done.2.part_ref = f32[8,16,384]{2,1,0:T(8,128)S(1)} async-done(((f32[8,16,384]{2,1,0:T(8,128)}), f32[8,16,384]{2,1,0:T(8,128)S(1)}, u32[]{:S(2)}, u32[]{:S(2)}) %all-to-all-start.2) | async-done | bytes 196640 | tf_op jit(solution)/shard_map/all_to_all | solution.py:37
  68.1 0.0 copy-done.1
  68.2 0.0 copy-done.3
  68.2 4.6 %chebyshev.1 = f32[8,16,648]{2,1,0:T(8,128)S(1)} custom-call(s32[1]{0:T(128)} %bitcast.last_ref, f32[8]{0:T(128)S(1)} %copy-done.3, f32[16,8,648]{2,1,0:T(8,128)S(1)} %copy-done.1, f32[16,2304]{1,0:T(8,128)S(1)} %collective-permute-done.1.left_ref, f32[16,1664]{1,0:T(8,128)S(1)} %collective-permute-done.2.right_ref, ...), custom_call_target="tpu_custom_call" | custom-call | tf_op jit(solution)/shard_map/chebyshev/pallas_call | solution.py:410
  72.7 17.4 %all_to_all.36 = f32[8,16,648]{2,1,0:T(8,128)S(1)} all-to-all(f32[8,16,648]{2,1,0:T(8,128)S(1)} %chebyshev.1), channel_id=1, replica_groups=mesh['dom'=64,'band'=8] {'band'}, dimensions={0} | all-to-all | bytes 663552 | tf_op jit(solution)/shard_map/all_to_all | solution.py:37
  90.1 0.5 fusion
  90.6 11.4 %all_to_all.37 = f32[16,8,128]{2,1,0:T(8,128)S(1)} all-to-all(f32[16,8,128]{2,1,0:T(8,128)S(1)} %fusion), channel_id=1, replica_groups={{0,1,8,9,128,129,136,137,256,257,264,265,384,385,392,393},{2,3,10,11,13..., dimensions={0} | all-to-all | bytes 131072 | tf_op jit(solution)/shard_map/all_to_all | solution.py:37
  102.0 14.7 %all_to_all.38 = f32[32,8,128]{2,1,0:T(8,128)S(1)} all-to-all(f32[32,8,128]{2,1,0:T(8,128)S(1)} %broadcast_in_dim.7), channel_id=1, replica_groups={{0,2,4,6,16,18,20,22,32,34,36,38,48,50,52,54,64,66,68,70,80,82,84,86,96..., dimensions={0} | all-to-all | bytes 262144 | tf_op jit(solution)/shard_map/all_to_all | solution.py:37
  116.8 10.3 %all_to_all.39 = f32[16,8,128]{2,1,0:T(8,128)S(1)} all-to-all(f32[16,8,128]{2,1,0:T(8,128)S(1)} %broadcast_in_dim.8), channel_id=1, replica_groups={{0,1,8,9,128,129,136,137,256,257,264,265,384,385,392,393},{2,3,10,11,13..., dimensions={0} | all-to-all | bytes 131072 | tf_op jit(solution)/shard_map/all_to_all | solution.py:37
  127.1 6.1 %orthonormalize.1 = f32[648,128]{1,0:T(8,128)} custom-call(f32[128,128]{1,0:T(8,128)S(1)} %bitcast.20, f32[128,648]{1,0:T(8,128)S(1)} %bitcast.19), custom_call_target="tpu_custom_call" | custom-call | tf_op jit(solution)/shard_map/orthonormalize/pallas_call | solution.py:436
  (9 shorter events, 0.2 us)
Async XLA Ops:
  2.4 10.3 %collective-permute-start = (f32[392,256]{1,0:T(8,128)}, f32[392,256]{1,0:T(8,128)S(1)}, u32[]{:S(2)}, u32[]{:S(2)}) collective-permute-start(f32[392,256]{1,0:T(8,128)} %get-tuple-element.15), channel_id=1, source_target_pairs={{0,1},{1,0},{2,3},{3,2},{4,5},{5,4},{6,7},{7,6},{8,9},{9,8},{10,11... | collective-permute-start | bytes 1204232 | tf_op jit(solution)/shard_map/ppermute | solution.py:365
  11.2 1.0 copy-start.2
  12.2 5.4 %copy-start.4 = (f32[16,2304]{1,0:T(8,128)S(1)}, f32[16,2304]{1,0:T(8,128)}, u32[]{:S(2)}) copy-start(f32[16,2304]{1,0:T(8,128)} %get-tuple-element.16) | copy-start | bytes 442372
  12.2 6.8 %copy-start.5 = (f32[16,1664]{1,0:T(8,128)S(1)}, f32[16,1664]{1,0:T(8,128)}, u32[]{:S(2)}) copy-start(f32[16,1664]{1,0:T(8,128)} %get-tuple-element.17) | copy-start | bytes 319492
  14.2 19.2 %all-to-all-start = ((f32[4,136,384]{2,1,0:T(8,128)}), f32[4,136,384]{2,1,0:T(8,128)S(1)}, u32[]{:S(2)}, u32[]{:S(2)}) async-start(f32[4,136,384]{2,1,0:T(8,128)} %bitcast.6), calls=%async_computation | async-start | bytes 1671168 | tf_op jit(solution)/shard_map/all_to_all | solution.py:37
  17.7 15.7 %collective-permute-start.1 = (f32[16,2304]{1,0:T(8,128)S(1)}, f32[16,2304]{1,0:T(8,128)S(1)}, u32[]{:S(2)}, u32[]{:S(2)}) collective-permute-start(f32[16,2304]{1,0:T(8,128)S(1)} %copy-done.4), channel_id=1, source_target_pairs={{0,8},{8,16},{16,24},{24,32},{32,40},{40,48},{48,56},{56,64},{64,7... | collective-permute-start | bytes 442376 | tf_op jit(solution)/shard_map/ppermute | solution.py:383
  19.0 14.4 %collective-permute-start.2 = (f32[16,1664]{1,0:T(8,128)S(1)}, f32[16,1664]{1,0:T(8,128)S(1)}, u32[]{:S(2)}, u32[]{:S(2)}) collective-permute-start(f32[16,1664]{1,0:T(8,128)S(1)} %copy-done.5), channel_id=1, source_target_pairs={{8,0},{16,8},{24,16},{32,24},{40,32},{48,40},{56,48},{64,56},{72,6... | collective-permute-start | bytes 319496 | tf_op jit(solution)/shard_map/ppermute | solution.py:384
  49.6 18.6 %copy-start.1 = (f32[16,8,648]{2,1,0:T(8,128)S(1)}, f32[16,8,648]{2,1,0:T(8,128)}, u32[]{:S(2)}) copy-start(f32[16,8,648]{2,1,0:T(8,128)} %own_ref.1) | copy-start | bytes 995332
  49.6 18.6 %all-to-all-start.2 = ((f32[8,16,384]{2,1,0:T(8,128)}), f32[8,16,384]{2,1,0:T(8,128)S(1)}, u32[]{:S(2)}, u32[]{:S(2)}) async-start(f32[8,16,384]{2,1,0:T(8,128)} %broadcast_in_dim.6), calls=%async_computation.2 | async-start | bytes 393216 | tf_op jit(solution)/shard_map/all_to_all | solution.py:37
  59.5 8.6 %copy-start.3 = (f32[8]{0:T(128)S(1)}, f32[8]{0:T(128)}, u32[]{:S(2)}) copy-start(f32[8]{0:T(128)} %scale_ref.1) | copy-start | bytes 100
  59.5 1.7 %copy-start = (f32[729,729]{1,0:T(8,128)S(1)}, f32[729,729]{1,0:T(8,128)}, u32[]{:S(2)}) copy-start(f32[729,729]{1,0:T(8,128)} %operator_ref) | copy-start | bytes 6377296

commit v7 on v6

--- a/solution.py
+++ b/solution.py
@@ -13,6 +13,8 @@
 WIDE = 768
 HALF = 384
 SLAB = 136
+KEPT = 13
+PACKED = 40
 TILE5 = 640
 SPLIT = OWN - TILE5
 
@@ -63,42 +65,46 @@
     ]
     for copy in copies:
         copy.start()
-    for copy in copies:
+    for copy in copies[:3]:
         copy.wait()
+
     def ghost(ref, place, c):
         value = orbitals_ref[:, c, :]
         scale = jnp.broadcast_to(scale_ref[:, c:c + 1], (16, 128 - SPLIT))
         ref[:, WIDE * place:WIDE * place + TILE5] = value[:, :TILE5]
         ref[:, WIDE * place + TILE5:WIDE * place + WIDE] = jnp.concatenate([value[:, TILE5:], scale], 1)
 
+    count = density_ref.shape[1]
+    target = (owner_ref[...] * 8 + cell_ref[...]).astype(jnp.float32)
+    target = jnp.broadcast_to(target, (8, count))
+
+    def lower(ref):
+        ref[:HALF, :] = density_ref[:HALF, :]
+        ref[HALF:, :] = target
+
+    def upper(ref):
+        ref[:344, :] = density_ref[HALF:728, :]
+        ref[344:HALF, :] = jnp.zeros((HALF - 344, count), jnp.float32)
+        ref[344:345, :] = density_ref[728:NODES, :]
+        ref[HALF:, :] = target
+
+    @pl.when(core_ref[0] == 0)
+    def _():
+        lower(own_ref)
+        upper(send_ref)
+
+    @pl.when(core_ref[0] != 0)
+    def _():
+        upper(own_ref)
+        lower(send_ref)
+
+    for copy in copies[3:]:
+        copy.wait()
     for place in range(3):
         ghost(left_ref, place, 5 + place)
     for place in range(2):
         ghost(right_ref, place, place)
     right_ref[:, 2 * WIDE:] = orbitals_ref[:, 2, :128]
-    count = density_ref.shape[1]
-    target = (owner_ref[...] * 8 + cell_ref[...]).astype(jnp.float32)
-    target = jnp.broadcast_to(target, (8, count))
-
-    def lower(ref):
-        ref[:HALF, :] = density_ref[:HALF, :]
-        ref[HALF:, :] = target
-
-    def upper(ref):
-        ref[:344, :] = density_ref[HALF:728, :]
-        ref[344:HALF, :] = jnp.zeros((HALF - 344, count), jnp.float32)
-        ref[344:345, :] = density_ref[728:NODES, :]
-        ref[HALF:, :] = target
-
-    @pl.when(core_ref[0] == 0)
-    def _():
-        lower(own_ref)
-        upper(send_ref)
-
-    @pl.when(core_ref[0] != 0)
-    def _():
-        upper(own_ref)
-        lower(send_ref)
 
 
 def cell_sums(ref):
@@ -119,14 +125,12 @@
     out_ref[...] = own_ref[...] + cell_sums(other_ref)
 
 
-def window_kernel(part_ref, out_ref):
-    for k in range(17):
-        r = slice(8 * k, 8 * k + 8)
-        block = (part_ref[0, r, :] + part_ref[1, r, :]) + (part_ref[2, r, :] + part_ref[3, r, :])
-        if k < 16:
-            out_ref[k, :8, :] = block
-        if k > 0:
-            out_ref[k - 1, 8:, :] = block
+def window_kernel(part_ref, out_ref, sum_ref):
+    sum_ref[...] = (part_ref[0] + part_ref[1]) + (part_ref[2] + part_ref[3])
+    for k in range(16):
+        for t in range(3):
+            out_ref[k, KEPT * t:KEPT * t + KEPT, :] = sum_ref[8 * k:8 * k + KEPT, 128 * t:128 * t + 128]
+        out_ref[k, 3 * KEPT:, :] = jnp.zeros((PACKED - 3 * KEPT, 128), jnp.float32)
 
 
 def cell_vectors(source, begin, end, cell_buf, chigh, clow):
@@ -190,8 +194,11 @@
                   v0, v1, v2, chigh, clow, cell_buf, product, pot):
     for half in range(2):
         rho = (part_ref[half] + part_ref[half + 2]) + (part_ref[half + 4] + part_ref[half + 6])
-        pot[:, half * HALF:(half + 1) * HALF] = jnp.where(
+        value = jnp.where(
             rho > 0.0, -0.7386 * jnp.exp(jnp.log(jnp.where(rho > 0.0, rho, 1.0)) * (1.0 / 3.0)), 0.0)
+        for t in range(3):
+            begin = half * HALF + 128 * t
+            pot[:KEPT, begin:begin + 128] = value[KEPT * t:KEPT * t + KEPT, :]
     lane = lax.broadcasted_iota(jnp.int32, (16, 128), 1)
     is_face = lane < FACE
     is_own5 = lane < SPLIT
@@ -386,9 +393,10 @@
     part = exchange(delivered.reshape(4, SLAB, HALF), "dom", X_GROUPS)
     windows = pl.pallas_call(
         window_kernel,
-        out_shape=jax.ShapeDtypeStruct((16, 16, HALF), jnp.float32),
+        out_shape=jax.ShapeDtypeStruct((16, PACKED, 128), jnp.float32),
         in_specs=[vmem],
         out_specs=vmem,
+        scratch_shapes=[pltpu.VMEM((SLAB, HALF), jnp.float32)],
         compiler_params=params,
         name="windows",
     )(part)
@@ -396,7 +404,7 @@
     part = exchange(windows, "dom", YZ_GROUPS)
     window = jnp.sum(part, 0)
     window, operator = lax.optimization_barrier((window, cell_operator))
-    part = exchange(jnp.broadcast_to(window[None], (band_count, 16, HALF)), "band")
+    part = exchange(jnp.broadcast_to(window[None], (band_count, PACKED, 128)), "band")
 
     ksplit = pl.pallas_call(
         split_kernel,

time: 134 us -> 131 us (0.978)
  blocking collectives: 69.2 us -> 66.9 us
    all_to_all x5, blocking collectives: 69.2 us -> 66.9 us  [exchange(): lax.all_to_all(value, axis, split_axis=0, concat_axis=0, tiled=True, axis...]
where the time goes in v7:
time: 131 us
  blocking collectives  66.9 us (51%)
  starting transfers between devices  24.9 us (19%)
  waiting for transfers between devices  19.1 us (15%)
  Pallas kernels  15.7 us (12%)
  local copies, waits for them, and re-layouts  3.36 us (3%)
    all_to_all x5, blocking collectives, exchange(): lax.all_to_all(value, axis, split_axis=0, concat_axis=0, tiled=True, axis...  66.9 us
    all_to_all x2, waiting for transfers between devices, exchange(): lax.all_to_all(value, axis, split_axis=0, concat_axis=0, tiled=True, axis...  19 us
    all_to_all x2, starting transfers between devices, exchange(): lax.all_to_all(value, axis, split_axis=0, concat_axis=0, tiled=True, axis...  13.5 us
    ppermute x1, starting transfers between devices, body(): other = lax.ppermute(send, 'band', [(i, i ^ 1) for i in range(band_count)])  8.79 us
    pallas_call x1, Pallas kernels, body(): pl.pallas_call(functools.partial(solve_kernel, float(total)), out_shape=j...  6.12 us
    pallas_call x1, Pallas kernels, body(): pl.pallas_call(filter_kernel, out_shape=jax.ShapeDtypeStruct((8, 16, OWN)...  4.57 us
    unnamed x12, local copies, waits for them, and re-layouts  2.66 us
  transfers between devices with their start and end apart: 5, of which 3 were waited for; matrix products, arithmetic and copies ran while one was open for 0% of the time, Pallas kernels for 1%

profile of v7, /device:TPU:1, one launch (start us, length us, event | category | flops | bytes accessed | tf_op | source)
XLA Modules:
  0.0 130.5 jit_solution(4084539555961382423)
XLA Ops:
  0.0 2.3 %pack.1 = (f32[392,256]{1,0:T(8,128)}, f32[392,256]{1,0:T(8,128)}, f32[16,2304]{1,0:T(8,128)}, f32[16,1664]{1,0:T(8,128)}) custom-call(s32[1]{0:T(128)} %bitcast.1.core_ref, s32[1,256]{1,0:T(1,128)} %bitcast.23, s32[1,256]{1,0:T(1,128)} %bitcast.24, f32[729,256]{1,0:T(8,128)} %bitcast.22, f32[1,8]{1,0:T(1,128)} %bitcast.21, f32[16,8,648]{2,1,0:T(8,128)} %own_ref.1), custom_call_target="tpu_custom_call" | custom-call | tf_op jit(solution)/shard_map/pack/pallas_call | solution.py:356
  2.3 8.8 %collective-permute-start = (f32[392,256]{1,0:T(8,128)}, f32[392,256]{1,0:T(8,128)S(1)}, u32[]{:S(2)}, u32[]{:S(2)}) collective-permute-start(f32[392,256]{1,0:T(8,128)} %get-tuple-element.15), channel_id=1, source_target_pairs={{0,1},{1,0},{2,3},{3,2},{4,5},{5,4},{6,7},{7,6},{8,9},{9,8},{10,11... | collective-permute-start | bytes 1204232 | tf_op jit(solution)/shard_map/ppermute | solution.py:372
  11.1 0.0 copy-start.2
  11.1 1.0 copy-done.2
  12.1 0.5 own_sums.1.own_ref
  12.6 0.1 collective-permute-done.other_ref
  12.6 1.4 %deliver.1 = f32[544,384]{1,0:T(8,128)} custom-call(f32[544,384]{1,0:T(8,128)S(1)} %own_sums.1.own_ref, f32[392,256]{1,0:T(8,128)S(1)} %collective-permute-done.other_ref), custom_call_target="tpu_custom_call" | custom-call | tf_op jit(solution)/shard_map/deliver/pallas_call | solution.py:381
  14.0 3.5 %all-to-all-start = ((f32[4,136,384]{2,1,0:T(8,128)}), f32[4,136,384]{2,1,0:T(8,128)S(1)}, u32[]{:S(2)}, u32[]{:S(2)}) async-start(f32[4,136,384]{2,1,0:T(8,128)} %bitcast.6), calls=%async_computation | async-start | bytes 1671168 | tf_op jit(solution)/shard_map/all_to_all | solution.py:39
  17.5 0.0 copy-done.4
  17.5 1.3 collective-permute-start.1
  18.9 0.0 copy-done.5
  18.9 1.3 collective-permute-start.2
  20.2 13.1 %all-to-all-done.part_ref = f32[4,136,384]{2,1,0:T(8,128)S(1)} async-done(((f32[4,136,384]{2,1,0:T(8,128)}), f32[4,136,384]{2,1,0:T(8,128)S(1)}, u32[]{:S(2)}, u32[]{:S(2)}) %all-to-all-start) | async-done | bytes 835616 | tf_op jit(solution)/shard_map/all_to_all | solution.py:39
  33.2 0.1 windows.1
  33.3 0.0 collective-permute-done.2.right_ref
  33.3 0.0 collective-permute-done.1.left_ref
  33.3 14.0 %all_to_all.35 = f32[16,40,128]{2,1,0:T(8,128)S(1)} all-to-all(f32[16,40,128]{2,1,0:T(8,128)S(1)} %windows.1), channel_id=1, replica_groups={{0,8,16,24,32,40,48,56,64,72,80,88,96,104,112,120},{128,136,144,152,160..., dimensions={0} | all-to-all | bytes 655360 | tf_op jit(solution)/shard_map/all_to_all | solution.py:39
  47.3 0.0 copy-start.1
  47.4 0.7 broadcast_in_dim.6
  48.0 10.0 %all-to-all-start.2 = ((f32[8,40,128]{2,1,0:T(8,128)}), f32[8,40,128]{2,1,0:T(8,128)S(1)}, u32[]{:S(2)}, u32[]{:S(2)}) async-start(f32[8,40,128]{2,1,0:T(8,128)} %broadcast_in_dim.6), calls=%async_computation.2 | async-start | bytes 327680 | tf_op jit(solution)/shard_map/all_to_all | solution.py:39
  58.1 1.6 %copy-done = f32[729,729]{1,0:T(8,128)S(1)} copy-done((f32[729,729]{1,0:T(8,128)S(1)}, f32[729,729]{1,0:T(8,128)}, u32[]{:S(2)}) %copy-start) | copy-done | bytes 2125788
  59.7 0.7 split_operator.1.ksplit
  60.4 6.0 %all-to-all-done.2.part_ref = f32[8,40,128]{2,1,0:T(8,128)S(1)} async-done(((f32[8,40,128]{2,1,0:T(8,128)}), f32[8,40,128]{2,1,0:T(8,128)S(1)}, u32[]{:S(2)}, u32[]{:S(2)}) %all-to-all-start.2) | async-done | bytes 163872 | tf_op jit(solution)/shard_map/all_to_all | solution.py:39
  66.4 0.0 copy-done.1
  66.4 0.0 copy-done.3
  66.4 4.6 %chebyshev.1 = f32[8,16,648]{2,1,0:T(8,128)S(1)} custom-call(s32[1]{0:T(128)} %bitcast.last_ref, f32[8]{0:T(128)S(1)} %copy-done.3, f32[16,8,648]{2,1,0:T(8,128)S(1)} %copy-done.1, f32[16,2304]{1,0:T(8,128)S(1)} %collective-permute-done.1.left_ref, f32[16,1664]{1,0:T(8,128)S(1)} %collective-permute-done.2.right_ref, ...), custom_call_target="tpu_custom_call" | custom-call | tf_op jit(solution)/shard_map/chebyshev/pallas_call | solution.py:418
  71.0 18.2 %all_to_all.36 = f32[8,16,648]{2,1,0:T(8,128)S(1)} all-to-all(f32[8,16,648]{2,1,0:T(8,128)S(1)} %chebyshev.1), channel_id=1, replica_groups=mesh['dom'=64,'band'=8] {'band'}, dimensions={0} | all-to-all | bytes 663552 | tf_op jit(solution)/shard_map/all_to_all | solution.py:39
  89.2 0.5 fusion
  89.7 9.7 %all_to_all.37 = f32[16,8,128]{2,1,0:T(8,128)S(1)} all-to-all(f32[16,8,128]{2,1,0:T(8,128)S(1)} %fusion), channel_id=1, replica_groups={{0,1,8,9,128,129,136,137,256,257,264,265,384,385,392,393},{2,3,10,11,13..., dimensions={0} | all-to-all | bytes 131072 | tf_op jit(solution)/shard_map/all_to_all | solution.py:39
  99.4 14.7 %all_to_all.38 = f32[32,8,128]{2,1,0:T(8,128)S(1)} all-to-all(f32[32,8,128]{2,1,0:T(8,128)S(1)} %broadcast_in_dim.7), channel_id=1, replica_groups={{0,2,4,6,16,18,20,22,32,34,36,38,48,50,52,54,64,66,68,70,80,82,84,86,96..., dimensions={0} | all-to-all | bytes 262144 | tf_op jit(solution)/shard_map/all_to_all | solution.py:39
  114.2 10.3 %all_to_all.39 = f32[16,8,128]{2,1,0:T(8,128)S(1)} all-to-all(f32[16,8,128]{2,1,0:T(8,128)S(1)} %broadcast_in_dim.8), channel_id=1, replica_groups={{0,1,8,9,128,129,136,137,256,257,264,265,384,385,392,393},{2,3,10,11,13..., dimensions={0} | all-to-all | bytes 131072 | tf_op jit(solution)/shard_map/all_to_all | solution.py:39
  124.4 6.1 %orthonormalize.1 = f32[648,128]{1,0:T(8,128)} custom-call(f32[128,128]{1,0:T(8,128)S(1)} %bitcast.20, f32[128,648]{1,0:T(8,128)S(1)} %bitcast.19), custom_call_target="tpu_custom_call" | custom-call | tf_op jit(solution)/shard_map/orthonormalize/pallas_call | solution.py:444
  (9 shorter events, 0.1 us)
Async XLA Ops:
  2.3 10.3 %collective-permute-start = (f32[392,256]{1,0:T(8,128)}, f32[392,256]{1,0:T(8,128)S(1)}, u32[]{:S(2)}, u32[]{:S(2)}) collective-permute-start(f32[392,256]{1,0:T(8,128)} %get-tuple-element.15), channel_id=1, source_target_pairs={{0,1},{1,0},{2,3},{3,2},{4,5},{5,4},{6,7},{7,6},{8,9},{9,8},{10,11... | collective-permute-start | bytes 1204232 | tf_op jit(solution)/shard_map/ppermute | solution.py:372
  11.1 1.0 copy-start.2
  12.1 5.4 %copy-start.4 = (f32[16,2304]{1,0:T(8,128)S(1)}, f32[16,2304]{1,0:T(8,128)}, u32[]{:S(2)}) copy-start(f32[16,2304]{1,0:T(8,128)} %get-tuple-element.16) | copy-start | bytes 442372
  12.1 6.8 %copy-start.5 = (f32[16,1664]{1,0:T(8,128)S(1)}, f32[16,1664]{1,0:T(8,128)}, u32[]{:S(2)}) copy-start(f32[16,1664]{1,0:T(8,128)} %get-tuple-element.17) | copy-start | bytes 319492
  14.0 19.2 %all-to-all-start = ((f32[4,136,384]{2,1,0:T(8,128)}), f32[4,136,384]{2,1,0:T(8,128)S(1)}, u32[]{:S(2)}, u32[]{:S(2)}) async-start(f32[4,136,384]{2,1,0:T(8,128)} %bitcast.6), calls=%async_computation | async-start | bytes 1671168 | tf_op jit(solution)/shard_map/all_to_all | solution.py:39
  17.5 15.8 %collective-permute-start.1 = (f32[16,2304]{1,0:T(8,128)S(1)}, f32[16,2304]{1,0:T(8,128)S(1)}, u32[]{:S(2)}, u32[]{:S(2)}) collective-permute-start(f32[16,2304]{1,0:T(8,128)S(1)} %copy-done.4), channel_id=1, source_target_pairs={{0,8},{8,16},{16,24},{24,32},{32,40},{40,48},{48,56},{56,64},{64,7... | collective-permute-start | bytes 442376 | tf_op jit(solution)/shard_map/ppermute | solution.py:390
  18.9 14.5 %collective-permute-start.2 = (f32[16,1664]{1,0:T(8,128)S(1)}, f32[16,1664]{1,0:T(8,128)S(1)}, u32[]{:S(2)}, u32[]{:S(2)}) collective-permute-start(f32[16,1664]{1,0:T(8,128)S(1)} %copy-done.5), channel_id=1, source_target_pairs={{8,0},{16,8},{24,16},{32,24},{40,32},{48,40},{56,48},{64,56},{72,6... | collective-permute-start | bytes 319496 | tf_op jit(solution)/shard_map/ppermute | solution.py:391
  47.3 19.1 %copy-start.1 = (f32[16,8,648]{2,1,0:T(8,128)S(1)}, f32[16,8,648]{2,1,0:T(8,128)}, u32[]{:S(2)}) copy-start(f32[16,8,648]{2,1,0:T(8,128)} %own_ref.1) | copy-start | bytes 995332
  48.0 18.4 %all-to-all-start.2 = ((f32[8,40,128]{2,1,0:T(8,128)}), f32[8,40,128]{2,1,0:T(8,128)S(1)}, u32[]{:S(2)}, u32[]{:S(2)}) async-start(f32[8,40,128]{2,1,0:T(8,128)} %broadcast_in_dim.6), calls=%async_computation.2 | async-start | bytes 327680 | tf_op jit(solution)/shard_map/all_to_all | solution.py:39
  58.1 8.4 %copy-start.3 = (f32[8]{0:T(128)S(1)}, f32[8]{0:T(128)}, u32[]{:S(2)}) copy-start(f32[8]{0:T(128)} %scale_ref.1) | copy-start | bytes 100
  58.1 1.7 %copy-start = (f32[729,729]{1,0:T(8,128)S(1)}, f32[729,729]{1,0:T(8,128)}, u32[]{:S(2)}) copy-start(f32[729,729]{1,0:T(8,128)} %operator_ref) | copy-start | bytes 6377296

commit v8 on v7

--- a/solution.py
+++ b/solution.py
@@ -53,53 +53,50 @@
     return lax.dot_general(a, b, (((1,), (1,)), ((), ())), preferred_element_type=jnp.float32)
 
 
-def pack_kernel(core_ref, owner_hbm, cell_hbm, density_hbm, scale_hbm, orbitals_hbm,
-                own_ref, send_ref, left_ref, right_ref,
-                owner_ref, cell_ref, density_ref, scale_ref, orbitals_ref, sems):
+def pack_kernel(core_ref, owner_hbm, cell_hbm, density_hbm, own_ref, send_ref,
+                owner_ref, cell_ref, density_ref, sems):
     copies = [
         pltpu.make_async_copy(density_hbm, density_ref, sems.at[0]),
         pltpu.make_async_copy(owner_hbm, owner_ref, sems.at[1]),
         pltpu.make_async_copy(cell_hbm, cell_ref, sems.at[2]),
-        pltpu.make_async_copy(scale_hbm, scale_ref, sems.at[3]),
-        pltpu.make_async_copy(orbitals_hbm, orbitals_ref, sems.at[4]),
     ]
     for copy in copies:
         copy.start()
-    for copy in copies[:3]:
+    for copy in copies:
         copy.wait()
 
+    count = density_ref.shape[1]
+    target = (owner_ref[...] * 8 + cell_ref[...]).astype(jnp.float32)
+    target = jnp.broadcast_to(target, (8, count))
+
+    def lower(ref):
+        ref[:HALF, :] = density_ref[:HALF, :]
+        ref[HALF:, :] = target
+
+    def upper(ref):
+        ref[:344, :] = density_ref[HALF:728, :]
+        ref[344:HALF, :] = jnp.zeros((HALF - 344, count), jnp.float32)
+        ref[344:345, :] = density_ref[728:NODES, :]
+        ref[HALF:, :] = target
+
+    @pl.when(core_ref[0] == 0)
+    def _():
+        lower(own_ref)
+        upper(send_ref)
+
+    @pl.when(core_ref[0] != 0)
+    def _():
+        upper(own_ref)
+        lower(send_ref)
+
+
+def ghost_kernel(scale_ref, orbitals_ref, left_ref, right_ref):
     def ghost(ref, place, c):
         value = orbitals_ref[:, c, :]
         scale = jnp.broadcast_to(scale_ref[:, c:c + 1], (16, 128 - SPLIT))
         ref[:, WIDE * place:WIDE * place + TILE5] = value[:, :TILE5]
         ref[:, WIDE * place + TILE5:WIDE * place + WIDE] = jnp.concatenate([value[:, TILE5:], scale], 1)
 
-    count = density_ref.shape[1]
-    target = (owner_ref[...] * 8 + cell_ref[...]).astype(jnp.float32)
-    target = jnp.broadcast_to(target, (8, count))
-
-    def lower(ref):
-        ref[:HALF, :] = density_ref[:HALF, :]
-        ref[HALF:, :] = target
-
-    def upper(ref):
-        ref[:344, :] = density_ref[HALF:728, :]
-        ref[344:HALF, :] = jnp.zeros((HALF - 344, count), jnp.float32)
-        ref[344:345, :] = density_ref[728:NODES, :]
-        ref[HALF:, :] = target
-
-    @pl.when(core_ref[0] == 0)
-    def _():
-        lower(own_ref)
-        upper(send_ref)
-
-    @pl.when(core_ref[0] != 0)
-    def _():
-        upper(own_ref)
-        lower(send_ref)
-
-    for copy in copies[3:]:
-        copy.wait()
     for place in range(3):
         ghost(left_ref, place, 5 + place)
     for place in range(2):
@@ -268,6 +265,9 @@
     col = lax.broadcasted_iota(jnp.int32, shape, 1)
     row = lax.broadcasted_iota(jnp.int32, shape, 0)
     a = [gram_ref[8 * i:8 * i + 8, :] * (1.0 / total) for i in range(16)]
+    diagonal = [jnp.where(col == row + 8 * i, a[i], 0.0) for i in range(16)]
+    across = jnp.broadcast_to(lax.rsqrt(jnp.sum(sum(diagonal), 0, keepdims=True)), shape)
+    a = [a[i] * lax.rsqrt(jnp.sum(diagonal[i], 1, keepdims=True)) * across for i in range(16)]
     w = [jnp.where(col == row + 8 * i, 1.0, 0.0) for i in range(16)]
 
     def columns(block, k):
@@ -281,13 +281,17 @@
         s = [[line(own[j], i) for j in range(i + 1)] for i in range(8)]
         low = [[None] * 8 for _ in range(8)]
         inv = [None] * 8
-        for j in range(8):
+        for j in range(0, 8, 2):
             inv[j] = 1.0 / s[j][j]
+            inv[j + 1] = s[j][j] * (1.0 / (s[j][j] * s[j + 1][j + 1] - s[j + 1][j] * s[j + 1][j]))
             for i in range(j + 1, 8):
                 low[i][j] = s[i][j] * inv[j]
-            for i in range(j + 1, 8):
-                for m in range(j + 1, i + 1):
-                    s[i][m] = s[i][m] - low[i][j] * s[m][j]
+            for i in range(j + 2, 8):
+                s[i][j + 1] = s[i][j + 1] - low[i][j] * s[j + 1][j]
+                low[i][j + 1] = s[i][j + 1] * inv[j + 1]
+            for i in range(j + 2, 8):
+                for m in range(j + 2, i + 1):
+                    s[i][m] = s[i][m] - low[i][j] * s[m][j] - low[i][j + 1] * s[m][j + 1]
         n = [[None] * 8 for _ in range(8)]
         for i in range(8):
             for j in range(i):
@@ -320,7 +324,7 @@
         final = jnp.zeros(shape, jnp.float32)
         for i in range(8):
             final = jnp.where(row == i, lines_w[i] * jnp.sqrt(inv[i]), final)
-        inverse_ref[8 * k:8 * k + 8, :] = final
+        inverse_ref[8 * k:8 * k + 8, :] = final * across
         if k < 15:
             za = backward(forward(a[k]))
             zw = backward(lines_w)
@@ -353,22 +357,20 @@
     pack_shape = jax.ShapeDtypeStruct((HALF + 8, count), jnp.float32)
     left_shape = jax.ShapeDtypeStruct((16, 3 * WIDE), jnp.float32)
     right_shape = jax.ShapeDtypeStruct((16, 2 * WIDE + 128), jnp.float32)
-    own, send, send_left, send_right = pl.pallas_call(
+    own, send = pl.pallas_call(
         pack_kernel,
-        out_shape=(pack_shape, pack_shape, left_shape, right_shape),
-        in_specs=[smem] + [hbm] * 5,
-        out_specs=(vmem,) * 4,
+        out_shape=(pack_shape, pack_shape),
+        in_specs=[smem] + [hbm] * 3,
+        out_specs=(vmem,) * 2,
         scratch_shapes=[
             pltpu.VMEM((1, count), jnp.int32),
             pltpu.VMEM((1, count), jnp.int32),
             pltpu.VMEM((NODES, count), jnp.float32),
-            pltpu.VMEM((1, 8), jnp.float32),
-            pltpu.VMEM((16, 8, OWN), jnp.float32),
-            pltpu.SemaphoreType.DMA((5,)),
+            pltpu.SemaphoreType.DMA((3,)),
         ],
         compiler_params=roomy,
         name="pack",
-    )(core, block_owner.reshape(1, -1), block_cell.reshape(1, -1), density.T, cell_scale.reshape(1, -1), orbitals)
+    )(core, block_owner.reshape(1, -1), block_cell.reshape(1, -1), density.T)
     other = lax.ppermute(send, "band", [(i, i ^ 1) for i in range(band_count)])
     own = pl.pallas_call(
         own_kernel,
@@ -387,6 +389,14 @@
         name="deliver",
     )(own, other)
 
+    send_left, send_right = pl.pallas_call(
+        ghost_kernel,
+        out_shape=(left_shape, right_shape),
+        in_specs=[vmem, vmem],
+        out_specs=(vmem, vmem),
+        compiler_params=params,
+        name="ghosts",
+    )(cell_scale.reshape(1, -1), orbitals)
     left = lax.ppermute(send_left, "dom", [(i, i + 1) for i in range(dom_count - 1)])
     right = lax.ppermute(send_right, "dom", [(i + 1, i) for i in range(dom_count - 1)])
 

time: 131 us -> 131 us (level)
    unnamed x12 -> x8, local copies, waits for them, and re-layouts: 2.66 us -> 2.64 us
where the time goes in v8:
time: 131 us; the launch traced here: 130 us
  blocking collectives  67 us (51%)
  starting transfers between devices  24.9 us (19%)
  waiting for transfers between devices  19 us (15%)
  Pallas kernels  15.6 us (12%)
  local copies, waits for them, and re-layouts  3.34 us (3%)
    all_to_all x5, blocking collectives, exchange(): lax.all_to_all(value, axis, split_axis=0, concat_axis=0, tiled=True, axis...  67 us
    all_to_all x2, waiting for transfers between devices, exchange(): lax.all_to_all(value, axis, split_axis=0, concat_axis=0, tiled=True, axis...  19 us
    all_to_all x2, starting transfers between devices, exchange(): lax.all_to_all(value, axis, split_axis=0, concat_axis=0, tiled=True, axis...  13.5 us
    ppermute x1, starting transfers between devices, body(): other = lax.ppermute(send, 'band', [(i, i ^ 1) for i in range(band_count)])  8.79 us
    pallas_call x1, Pallas kernels, body(): pl.pallas_call(functools.partial(solve_kernel, float(total)), out_shape=j...  6.17 us
    pallas_call x1, Pallas kernels, body(): pl.pallas_call(filter_kernel, out_shape=jax.ShapeDtypeStruct((8, 16, OWN)...  4.57 us
    unnamed x8, local copies, waits for them, and re-layouts  2.64 us
  transfers between devices with their start and end apart: 5, of which 3 were waited for; matrix products, arithmetic and copies ran while one was open for 0% of the time, Pallas kernels for 1%

profile of v8, /device:TPU:1, one launch (start us, length us, event | category | flops | bytes accessed | tf_op | source)
XLA Modules:
  0.0 130.5 jit_solution(4720883688391304717)
XLA Ops:
  0.0 2.1 %pack.1 = (f32[392,256]{1,0:T(8,128)}, f32[392,256]{1,0:T(8,128)}) custom-call(s32[1]{0:T(128)} %bitcast.1.core_ref, s32[1,256]{1,0:T(1,128)} %bitcast.23, s32[1,256]{1,0:T(1,128)} %bitcast.24, f32[729,256]{1,0:T(8,128)} %bitcast.22), custom_call_target="tpu_custom_call" | custom-call | tf_op jit(solution)/shard_map/pack/pallas_call | solution.py:360
  2.1 8.8 %collective-permute-start = (f32[392,256]{1,0:T(8,128)}, f32[392,256]{1,0:T(8,128)S(1)}, u32[]{:S(2)}, u32[]{:S(2)}) collective-permute-start(f32[392,256]{1,0:T(8,128)} %get-tuple-element.15), channel_id=1, source_target_pairs={{0,1},{1,0},{2,3},{3,2},{4,5},{5,4},{6,7},{7,6},{8,9},{9,8},{10,11... | collective-permute-start | bytes 1204232 | tf_op jit(solution)/shard_map/ppermute | solution.py:374
  10.9 0.0 copy-start.2
  10.9 1.0 copy-done.2
  11.9 0.0 copy-start.1
  11.9 0.0 copy-start.3
  11.9 0.5 own_sums.1.own_ref
  12.4 0.1 collective-permute-done.other_ref
  12.5 1.4 %deliver.1 = f32[544,384]{1,0:T(8,128)} custom-call(f32[544,384]{1,0:T(8,128)S(1)} %own_sums.1.own_ref, f32[392,256]{1,0:T(8,128)S(1)} %collective-permute-done.other_ref), custom_call_target="tpu_custom_call" | custom-call | tf_op jit(solution)/shard_map/deliver/pallas_call | solution.py:383
  13.8 3.5 %all-to-all-start = ((f32[4,136,384]{2,1,0:T(8,128)}), f32[4,136,384]{2,1,0:T(8,128)S(1)}, u32[]{:S(2)}, u32[]{:S(2)}) async-start(f32[4,136,384]{2,1,0:T(8,128)} %bitcast.5), calls=%async_computation | async-start | bytes 1671168 | tf_op jit(solution)/shard_map/all_to_all | solution.py:39
  17.4 0.0 copy-done.1
  17.4 0.0 copy-done.3
  17.4 0.1 ghosts.1
  17.5 1.3 collective-permute-start.1
  18.8 1.3 collective-permute-start.2
  20.1 13.0 %all-to-all-done.part_ref = f32[4,136,384]{2,1,0:T(8,128)S(1)} async-done(((f32[4,136,384]{2,1,0:T(8,128)}), f32[4,136,384]{2,1,0:T(8,128)S(1)}, u32[]{:S(2)}, u32[]{:S(2)}) %all-to-all-start) | async-done | bytes 835616 | tf_op jit(solution)/shard_map/all_to_all | solution.py:39
  33.0 0.1 windows.1
  33.1 0.0 collective-permute-done.2.right_ref
  33.1 0.0 collective-permute-done.1.left_ref
  33.1 14.0 %all_to_all.35 = f32[16,40,128]{2,1,0:T(8,128)S(1)} all-to-all(f32[16,40,128]{2,1,0:T(8,128)S(1)} %windows.1), channel_id=1, replica_groups={{0,8,16,24,32,40,48,56,64,72,80,88,96,104,112,120},{128,136,144,152,160..., dimensions={0} | all-to-all | bytes 655360 | tf_op jit(solution)/shard_map/all_to_all | solution.py:39
  47.1 0.7 broadcast_in_dim.6
  47.8 10.0 %all-to-all-start.2 = ((f32[8,40,128]{2,1,0:T(8,128)}), f32[8,40,128]{2,1,0:T(8,128)S(1)}, u32[]{:S(2)}, u32[]{:S(2)}) async-start(f32[8,40,128]{2,1,0:T(8,128)} %broadcast_in_dim.6), calls=%async_computation.2 | async-start | bytes 327680 | tf_op jit(solution)/shard_map/all_to_all | solution.py:39
  57.9 1.6 %copy-done = f32[729,729]{1,0:T(8,128)S(1)} copy-done((f32[729,729]{1,0:T(8,128)S(1)}, f32[729,729]{1,0:T(8,128)}, u32[]{:S(2)}) %copy-start) | copy-done | bytes 2125788
  59.5 0.7 split_operator.1.ksplit
  60.2 6.0 %all-to-all-done.2.part_ref = f32[8,40,128]{2,1,0:T(8,128)S(1)} async-done(((f32[8,40,128]{2,1,0:T(8,128)}), f32[8,40,128]{2,1,0:T(8,128)S(1)}, u32[]{:S(2)}, u32[]{:S(2)}) %all-to-all-start.2) | async-done | bytes 163872 | tf_op jit(solution)/shard_map/all_to_all | solution.py:39
  66.2 4.6 %chebyshev.1 = f32[8,16,648]{2,1,0:T(8,128)S(1)} custom-call(s32[1]{0:T(128)} %bitcast.last_ref, f32[8]{0:T(128)S(1)} %copy-done.3, f32[16,8,648]{2,1,0:T(8,128)S(1)} %copy-done.1, f32[16,2304]{1,0:T(8,128)S(1)} %collective-permute-done.1.left_ref, f32[16,1664]{1,0:T(8,128)S(1)} %collective-permute-done.2.right_ref, ...), custom_call_target="tpu_custom_call" | custom-call | tf_op jit(solution)/shard_map/chebyshev/pallas_call | solution.py:428
  70.8 18.2 %all_to_all.36 = f32[8,16,648]{2,1,0:T(8,128)S(1)} all-to-all(f32[8,16,648]{2,1,0:T(8,128)S(1)} %chebyshev.1), channel_id=1, replica_groups=mesh['dom'=64,'band'=8] {'band'}, dimensions={0} | all-to-all | bytes 663552 | tf_op jit(solution)/shard_map/all_to_all | solution.py:39
  89.0 0.5 fusion
  89.4 9.9 %all_to_all.37 = f32[16,8,128]{2,1,0:T(8,128)S(1)} all-to-all(f32[16,8,128]{2,1,0:T(8,128)S(1)} %fusion), channel_id=1, replica_groups={{0,1,8,9,128,129,136,137,256,257,264,265,384,385,392,393},{2,3,10,11,13..., dimensions={0} | all-to-all | bytes 131072 | tf_op jit(solution)/shard_map/all_to_all | solution.py:39
  99.3 14.7 %all_to_all.38 = f32[32,8,128]{2,1,0:T(8,128)S(1)} all-to-all(f32[32,8,128]{2,1,0:T(8,128)S(1)} %broadcast_in_dim.7), channel_id=1, replica_groups={{0,2,4,6,16,18,20,22,32,34,36,38,48,50,52,54,64,66,68,70,80,82,84,86,96..., dimensions={0} | all-to-all | bytes 262144 | tf_op jit(solution)/shard_map/all_to_all | solution.py:39
  114.1 10.3 %all_to_all.39 = f32[16,8,128]{2,1,0:T(8,128)S(1)} all-to-all(f32[16,8,128]{2,1,0:T(8,128)S(1)} %broadcast_in_dim.8), channel_id=1, replica_groups={{0,1,8,9,128,129,136,137,256,257,264,265,384,385,392,393},{2,3,10,11,13..., dimensions={0} | all-to-all | bytes 131072 | tf_op jit(solution)/shard_map/all_to_all | solution.py:39
  124.3 6.2 %orthonormalize.1 = f32[648,128]{1,0:T(8,128)} custom-call(f32[128,128]{1,0:T(8,128)S(1)} %bitcast.20, f32[128,648]{1,0:T(8,128)S(1)} %bitcast.19), custom_call_target="tpu_custom_call" | custom-call | tf_op jit(solution)/shard_map/orthonormalize/pallas_call | solution.py:454
  (6 shorter events, 0.1 us)
Async XLA Ops:
  2.1 10.3 %collective-permute-start = (f32[392,256]{1,0:T(8,128)}, f32[392,256]{1,0:T(8,128)S(1)}, u32[]{:S(2)}, u32[]{:S(2)}) collective-permute-start(f32[392,256]{1,0:T(8,128)} %get-tuple-element.15), channel_id=1, source_target_pairs={{0,1},{1,0},{2,3},{3,2},{4,5},{5,4},{6,7},{7,6},{8,9},{9,8},{10,11... | collective-permute-start | bytes 1204232 | tf_op jit(solution)/shard_map/ppermute | solution.py:374
  10.9 1.0 copy-start.2
  11.9 5.4 %copy-start.1 = (f32[16,8,648]{2,1,0:T(8,128)S(1)}, f32[16,8,648]{2,1,0:T(8,128)}, u32[]{:S(2)}) copy-start(f32[16,8,648]{2,1,0:T(8,128)} %own_ref.1) | copy-start | bytes 995332
  11.9 5.5 %copy-start.3 = (f32[8]{0:T(128)S(1)}, f32[8]{0:T(128)}, u32[]{:S(2)}) copy-start(f32[8]{0:T(128)} %scale_ref.1) | copy-start | bytes 100
  13.8 19.2 %all-to-all-start = ((f32[4,136,384]{2,1,0:T(8,128)}), f32[4,136,384]{2,1,0:T(8,128)S(1)}, u32[]{:S(2)}, u32[]{:S(2)}) async-start(f32[4,136,384]{2,1,0:T(8,128)} %bitcast.5), calls=%async_computation | async-start | bytes 1671168 | tf_op jit(solution)/shard_map/all_to_all | solution.py:39
  17.5 15.7 %collective-permute-start.1 = (f32[16,2304]{1,0:T(8,128)S(1)}, f32[16,2304]{1,0:T(8,128)S(1)}, u32[]{:S(2)}, u32[]{:S(2)}) collective-permute-start(f32[16,2304]{1,0:T(8,128)S(1)} %get-tuple-element.16), channel_id=1, source_target_pairs={{0,8},{8,16},{16,24},{24,32},{32,40},{40,48},{48,56},{56,64},{64,7... | collective-permute-start | bytes 442376 | tf_op jit(solution)/shard_map/ppermute | solution.py:400
  18.8 14.4 %collective-permute-start.2 = (f32[16,1664]{1,0:T(8,128)S(1)}, f32[16,1664]{1,0:T(8,128)S(1)}, u32[]{:S(2)}, u32[]{:S(2)}) collective-permute-start(f32[16,1664]{1,0:T(8,128)S(1)} %get-tuple-element.17), channel_id=1, source_target_pairs={{8,0},{16,8},{24,16},{32,24},{40,32},{48,40},{56,48},{64,56},{72,6... | collective-permute-start | bytes 319496 | tf_op jit(solution)/shard_map/ppermute | solution.py:401
  47.8 18.4 %all-to-all-start.2 = ((f32[8,40,128]{2,1,0:T(8,128)}), f32[8,40,128]{2,1,0:T(8,128)S(1)}, u32[]{:S(2)}, u32[]{:S(2)}) async-start(f32[8,40,128]{2,1,0:T(8,128)} %broadcast_in_dim.6), calls=%async_computation.2 | async-start | bytes 327680 | tf_op jit(solution)/shard_map/all_to_all | solution.py:39
  57.9 1.6 %copy-start = (f32[729,729]{1,0:T(8,128)S(1)}, f32[729,729]{1,0:T(8,128)}, u32[]{:S(2)}) copy-start(f32[729,729]{1,0:T(8,128)} %operator_ref) | copy-start | bytes 6377296

commit v9 on v8

--- a/solution.py
+++ b/solution.py
@@ -265,9 +265,6 @@
     col = lax.broadcasted_iota(jnp.int32, shape, 1)
     row = lax.broadcasted_iota(jnp.int32, shape, 0)
     a = [gram_ref[8 * i:8 * i + 8, :] * (1.0 / total) for i in range(16)]
-    diagonal = [jnp.where(col == row + 8 * i, a[i], 0.0) for i in range(16)]
-    across = jnp.broadcast_to(lax.rsqrt(jnp.sum(sum(diagonal), 0, keepdims=True)), shape)
-    a = [a[i] * lax.rsqrt(jnp.sum(diagonal[i], 1, keepdims=True)) * across for i in range(16)]
     w = [jnp.where(col == row + 8 * i, 1.0, 0.0) for i in range(16)]
 
     def columns(block, k):
@@ -281,17 +278,13 @@
         s = [[line(own[j], i) for j in range(i + 1)] for i in range(8)]
         low = [[None] * 8 for _ in range(8)]
         inv = [None] * 8
-        for j in range(0, 8, 2):
+        for j in range(8):
             inv[j] = 1.0 / s[j][j]
-            inv[j + 1] = s[j][j] * (1.0 / (s[j][j] * s[j + 1][j + 1] - s[j + 1][j] * s[j + 1][j]))
             for i in range(j + 1, 8):
                 low[i][j] = s[i][j] * inv[j]
-            for i in range(j + 2, 8):
-                s[i][j + 1] = s[i][j + 1] - low[i][j] * s[j + 1][j]
-                low[i][j + 1] = s[i][j + 1] * inv[j + 1]
-            for i in range(j + 2, 8):
-                for m in range(j + 2, i + 1):
-                    s[i][m] = s[i][m] - low[i][j] * s[m][j] - low[i][j + 1] * s[m][j + 1]
+            for i in range(j + 1, 8):
+                for m in range(j + 1, i + 1):
+                    s[i][m] = s[i][m] - low[i][j] * s[m][j]
         n = [[None] * 8 for _ in range(8)]
         for i in range(8):
             for j in range(i):
@@ -324,7 +317,7 @@
         final = jnp.zeros(shape, jnp.float32)
         for i in range(8):
             final = jnp.where(row == i, lines_w[i] * jnp.sqrt(inv[i]), final)
-        inverse_ref[8 * k:8 * k + 8, :] = final * across
+        inverse_ref[8 * k:8 * k + 8, :] = final
         if k < 15:
             za = backward(forward(a[k]))
             zw = backward(lines_w)
@@ -447,7 +440,7 @@
     flat = exchange(filtered, "band").reshape(128, OWN)
     both = ("dom", "band")
     total = OWN * dom_count * band_count
-    gram = jnp.dot(flat, flat.T, precision=lax.Precision.HIGHEST)
+    gram = jnp.dot(flat, flat.T, precision=lax.Precision.HIGH)
     part = jnp.sum(exchange(gram.reshape(16, 8, 128), both, NEAR_GROUPS), 0)
     part = jnp.sum(exchange(jnp.broadcast_to(part[None], (32, 8, 128)), both, FAR_GROUPS), 0)
     gram = exchange(jnp.broadcast_to(part[None], (16, 8, 128)), both, NEAR_GROUPS).reshape(128, 128)

time: 131 us -> 131 us (level)
  no operation moved by 1% of the time
where the time goes in v9:
time: 131 us; the launch traced here: 130 us
  blocking collectives  67 us (51%)
  starting transfers between devices  24.9 us (19%)
  waiting for transfers between devices  19 us (15%)
  Pallas kernels  15.5 us (12%)
  local copies, waits for them, and re-layouts  3.34 us (3%)
    all_to_all x5, blocking collectives, exchange(): lax.all_to_all(value, axis, split_axis=0, concat_axis=0, tiled=True, axis...  67 us
    all_to_all x2, waiting for transfers between devices, exchange(): lax.all_to_all(value, axis, split_axis=0, concat_axis=0, tiled=True, axis...  19 us
    all_to_all x2, starting transfers between devices, exchange(): lax.all_to_all(value, axis, split_axis=0, concat_axis=0, tiled=True, axis...  13.5 us
    ppermute x1, starting transfers between devices, body(): other = lax.ppermute(send, 'band', [(i, i ^ 1) for i in range(band_count)])  8.79 us
    pallas_call x1, Pallas kernels, body(): pl.pallas_call(functools.partial(solve_kernel, float(total)), out_shape=j...  6.12 us
    pallas_call x1, Pallas kernels, body(): pl.pallas_call(filter_kernel, out_shape=jax.ShapeDtypeStruct((8, 16, OWN)...  4.57 us
    unnamed x8, local copies, waits for them, and re-layouts  2.64 us
  transfers between devices with their start and end apart: 5, of which 3 were waited for; matrix products, arithmetic and copies ran while one was open for 0% of the time, Pallas kernels for 1%

profile of v9, /device:TPU:1, one launch (start us, length us, event | category | flops | bytes accessed | tf_op | source)
XLA Modules:
  0.0 130.3 jit_solution(4291017190550476190)
XLA Ops:
  0.0 2.1 %pack.1 = (f32[392,256]{1,0:T(8,128)}, f32[392,256]{1,0:T(8,128)}) custom-call(s32[1]{0:T(128)} %bitcast.1.core_ref, s32[1,256]{1,0:T(1,128)} %bitcast.23, s32[1,256]{1,0:T(1,128)} %bitcast.24, f32[729,256]{1,0:T(8,128)} %bitcast.22), custom_call_target="tpu_custom_call" | custom-call | tf_op jit(solution)/shard_map/pack/pallas_call | solution.py:353
  2.1 8.8 %collective-permute-start = (f32[392,256]{1,0:T(8,128)}, f32[392,256]{1,0:T(8,128)S(1)}, u32[]{:S(2)}, u32[]{:S(2)}) collective-permute-start(f32[392,256]{1,0:T(8,128)} %get-tuple-element.15), channel_id=1, source_target_pairs={{0,1},{1,0},{2,3},{3,2},{4,5},{5,4},{6,7},{7,6},{8,9},{9,8},{10,11... | collective-permute-start | bytes 1204232 | tf_op jit(solution)/shard_map/ppermute | solution.py:367
  10.9 0.0 copy-start.2
  10.9 1.0 copy-done.2
  11.9 0.0 copy-start.1
  11.9 0.0 copy-start.3
  11.9 0.5 own_sums.1.own_ref
  12.4 0.1 collective-permute-done.other_ref
  12.5 1.4 %deliver.1 = f32[544,384]{1,0:T(8,128)} custom-call(f32[544,384]{1,0:T(8,128)S(1)} %own_sums.1.own_ref, f32[392,256]{1,0:T(8,128)S(1)} %collective-permute-done.other_ref), custom_call_target="tpu_custom_call" | custom-call | tf_op jit(solution)/shard_map/deliver/pallas_call | solution.py:376
  13.8 3.5 %all-to-all-start = ((f32[4,136,384]{2,1,0:T(8,128)}), f32[4,136,384]{2,1,0:T(8,128)S(1)}, u32[]{:S(2)}, u32[]{:S(2)}) async-start(f32[4,136,384]{2,1,0:T(8,128)} %bitcast.5), calls=%async_computation | async-start | bytes 1671168 | tf_op jit(solution)/shard_map/all_to_all | solution.py:39
  17.4 0.0 copy-done.1
  17.4 0.0 copy-done.3
  17.4 0.1 ghosts.1
  17.5 1.3 collective-permute-start.1
  18.8 1.3 collective-permute-start.2
  20.1 13.0 %all-to-all-done.part_ref = f32[4,136,384]{2,1,0:T(8,128)S(1)} async-done(((f32[4,136,384]{2,1,0:T(8,128)}), f32[4,136,384]{2,1,0:T(8,128)S(1)}, u32[]{:S(2)}, u32[]{:S(2)}) %all-to-all-start) | async-done | bytes 835616 | tf_op jit(solution)/shard_map/all_to_all | solution.py:39
  33.0 0.1 windows.1
  33.1 0.0 collective-permute-done.2.right_ref
  33.1 0.0 collective-permute-done.1.left_ref
  33.1 14.0 %all_to_all.35 = f32[16,40,128]{2,1,0:T(8,128)S(1)} all-to-all(f32[16,40,128]{2,1,0:T(8,128)S(1)} %windows.1), channel_id=1, replica_groups={{0,8,16,24,32,40,48,56,64,72,80,88,96,104,112,120},{128,136,144,152,160..., dimensions={0} | all-to-all | bytes 655360 | tf_op jit(solution)/shard_map/all_to_all | solution.py:39
  47.1 0.7 broadcast_in_dim.6
  47.8 10.0 %all-to-all-start.2 = ((f32[8,40,128]{2,1,0:T(8,128)}), f32[8,40,128]{2,1,0:T(8,128)S(1)}, u32[]{:S(2)}, u32[]{:S(2)}) async-start(f32[8,40,128]{2,1,0:T(8,128)} %broadcast_in_dim.6), calls=%async_computation.2 | async-start | bytes 327680 | tf_op jit(solution)/shard_map/all_to_all | solution.py:39
  57.9 1.6 %copy-done = f32[729,729]{1,0:T(8,128)S(1)} copy-done((f32[729,729]{1,0:T(8,128)S(1)}, f32[729,729]{1,0:T(8,128)}, u32[]{:S(2)}) %copy-start) | copy-done | bytes 2125788
  59.5 0.7 split_operator.1.ksplit
  60.2 6.0 %all-to-all-done.2.part_ref = f32[8,40,128]{2,1,0:T(8,128)S(1)} async-done(((f32[8,40,128]{2,1,0:T(8,128)}), f32[8,40,128]{2,1,0:T(8,128)S(1)}, u32[]{:S(2)}, u32[]{:S(2)}) %all-to-all-start.2) | async-done | bytes 163872 | tf_op jit(solution)/shard_map/all_to_all | solution.py:39
  66.2 4.6 %chebyshev.1 = f32[8,16,648]{2,1,0:T(8,128)S(1)} custom-call(s32[1]{0:T(128)} %bitcast.last_ref, f32[8]{0:T(128)S(1)} %copy-done.3, f32[16,8,648]{2,1,0:T(8,128)S(1)} %copy-done.1, f32[16,2304]{1,0:T(8,128)S(1)} %collective-permute-done.1.left_ref, f32[16,1664]{1,0:T(8,128)S(1)} %collective-permute-done.2.right_ref, ...), custom_call_target="tpu_custom_call" | custom-call | tf_op jit(solution)/shard_map/chebyshev/pallas_call | solution.py:421
  70.8 18.2 %all_to_all.36 = f32[8,16,648]{2,1,0:T(8,128)S(1)} all-to-all(f32[8,16,648]{2,1,0:T(8,128)S(1)} %chebyshev.1), channel_id=1, replica_groups=mesh['dom'=64,'band'=8] {'band'}, dimensions={0} | all-to-all | bytes 663552 | tf_op jit(solution)/shard_map/all_to_all | solution.py:39
  89.0 0.3 fusion
  89.3 9.9 %all_to_all.37 = f32[16,8,128]{2,1,0:T(8,128)S(1)} all-to-all(f32[16,8,128]{2,1,0:T(8,128)S(1)} %fusion), channel_id=1, replica_groups={{0,1,8,9,128,129,136,137,256,257,264,265,384,385,392,393},{2,3,10,11,13..., dimensions={0} | all-to-all | bytes 131072 | tf_op jit(solution)/shard_map/all_to_all | solution.py:39
  99.2 14.7 %all_to_all.38 = f32[32,8,128]{2,1,0:T(8,128)S(1)} all-to-all(f32[32,8,128]{2,1,0:T(8,128)S(1)} %broadcast_in_dim.7), channel_id=1, replica_groups={{0,2,4,6,16,18,20,22,32,34,36,38,48,50,52,54,64,66,68,70,80,82,84,86,96..., dimensions={0} | all-to-all | bytes 262144 | tf_op jit(solution)/shard_map/all_to_all | solution.py:39
  113.9 10.3 %all_to_all.39 = f32[16,8,128]{2,1,0:T(8,128)S(1)} all-to-all(f32[16,8,128]{2,1,0:T(8,128)S(1)} %broadcast_in_dim.8), channel_id=1, replica_groups={{0,1,8,9,128,129,136,137,256,257,264,265,384,385,392,393},{2,3,10,11,13..., dimensions={0} | all-to-all | bytes 131072 | tf_op jit(solution)/shard_map/all_to_all | solution.py:39
  124.2 6.1 %orthonormalize.1 = f32[648,128]{1,0:T(8,128)} custom-call(f32[128,128]{1,0:T(8,128)S(1)} %bitcast.20, f32[128,648]{1,0:T(8,128)S(1)} %bitcast.19), custom_call_target="tpu_custom_call" | custom-call | tf_op jit(solution)/shard_map/orthonormalize/pallas_call | solution.py:447
  (6 shorter events, 0.1 us)
Async XLA Ops:
  2.1 10.3 %collective-permute-start = (f32[392,256]{1,0:T(8,128)}, f32[392,256]{1,0:T(8,128)S(1)}, u32[]{:S(2)}, u32[]{:S(2)}) collective-permute-start(f32[392,256]{1,0:T(8,128)} %get-tuple-element.15), channel_id=1, source_target_pairs={{0,1},{1,0},{2,3},{3,2},{4,5},{5,4},{6,7},{7,6},{8,9},{9,8},{10,11... | collective-permute-start | bytes 1204232 | tf_op jit(solution)/shard_map/ppermute | solution.py:367
  10.9 1.0 copy-start.2
  11.9 5.4 %copy-start.1 = (f32[16,8,648]{2,1,0:T(8,128)S(1)}, f32[16,8,648]{2,1,0:T(8,128)}, u32[]{:S(2)}) copy-start(f32[16,8,648]{2,1,0:T(8,128)} %own_ref.1) | copy-start | bytes 995332
  11.9 5.5 %copy-start.3 = (f32[8]{0:T(128)S(1)}, f32[8]{0:T(128)}, u32[]{:S(2)}) copy-start(f32[8]{0:T(128)} %scale_ref.1) | copy-start | bytes 100
  13.8 19.2 %all-to-all-start = ((f32[4,136,384]{2,1,0:T(8,128)}), f32[4,136,384]{2,1,0:T(8,128)S(1)}, u32[]{:S(2)}, u32[]{:S(2)}) async-start(f32[4,136,384]{2,1,0:T(8,128)} %bitcast.5), calls=%async_computation | async-start | bytes 1671168 | tf_op jit(solution)/shard_map/all_to_all | solution.py:39
  17.5 15.7 %collective-permute-start.1 = (f32[16,2304]{1,0:T(8,128)S(1)}, f32[16,2304]{1,0:T(8,128)S(1)}, u32[]{:S(2)}, u32[]{:S(2)}) collective-permute-start(f32[16,2304]{1,0:T(8,128)S(1)} %get-tuple-element.16), channel_id=1, source_target_pairs={{0,8},{8,16},{16,24},{24,32},{32,40},{40,48},{48,56},{56,64},{64,7... | collective-permute-start | bytes 442376 | tf_op jit(solution)/shard_map/ppermute | solution.py:393
  18.8 14.4 %collective-permute-start.2 = (f32[16,1664]{1,0:T(8,128)S(1)}, f32[16,1664]{1,0:T(8,128)S(1)}, u32[]{:S(2)}, u32[]{:S(2)}) collective-permute-start(f32[16,1664]{1,0:T(8,128)S(1)} %get-tuple-element.17), channel_id=1, source_target_pairs={{8,0},{16,8},{24,16},{32,24},{40,32},{48,40},{56,48},{64,56},{72,6... | collective-permute-start | bytes 319496 | tf_op jit(solution)/shard_map/ppermute | solution.py:394
  47.8 18.4 %all-to-all-start.2 = ((f32[8,40,128]{2,1,0:T(8,128)}), f32[8,40,128]{2,1,0:T(8,128)S(1)}, u32[]{:S(2)}, u32[]{:S(2)}) async-start(f32[8,40,128]{2,1,0:T(8,128)} %broadcast_in_dim.6), calls=%async_computation.2 | async-start | bytes 327680 | tf_op jit(solution)/shard_map/all_to_all | solution.py:39
  57.9 1.6 %copy-start = (f32[729,729]{1,0:T(8,128)S(1)}, f32[729,729]{1,0:T(8,128)}, u32[]{:S(2)}) copy-start(f32[729,729]{1,0:T(8,128)} %operator_ref) | copy-start | bytes 6377296

commit v10 on v9

--- a/solution.py
+++ b/solution.py
@@ -316,7 +316,7 @@
         lines_w = forward(w[k])
         final = jnp.zeros(shape, jnp.float32)
         for i in range(8):
-            final = jnp.where(row == i, lines_w[i] * jnp.sqrt(inv[i]), final)
+            final = jnp.where(row == i, lines_w[i] * lax.rsqrt(s[i][i]), final)
         inverse_ref[8 * k:8 * k + 8, :] = final
         if k < 15:
             za = backward(forward(a[k]))

time: 131 us -> 131 us (level)
  no operation moved by 1% of the time
where the time goes in v10:
time: 131 us; the launch traced here: 130 us
  blocking collectives  67 us (51%)
  starting transfers between devices  24.9 us (19%)
  waiting for transfers between devices  19 us (15%)
  Pallas kernels  15.5 us (12%)
  local copies, waits for them, and re-layouts  3.34 us (3%)
    all_to_all x5, blocking collectives, exchange(): lax.all_to_all(value, axis, split_axis=0, concat_axis=0, tiled=True, axis...  67 us
    all_to_all x2, waiting for transfers between devices, exchange(): lax.all_to_all(value, axis, split_axis=0, concat_axis=0, tiled=True, axis...  19 us
    all_to_all x2, starting transfers between devices, exchange(): lax.all_to_all(value, axis, split_axis=0, concat_axis=0, tiled=True, axis...  13.5 us
    ppermute x1, starting transfers between devices, body(): other = lax.ppermute(send, 'band', [(i, i ^ 1) for i in range(band_count)])  8.79 us
    pallas_call x1, Pallas kernels, body(): pl.pallas_call(functools.partial(solve_kernel, float(total)), out_shape=j...  6.13 us
    pallas_call x1, Pallas kernels, body(): pl.pallas_call(filter_kernel, out_shape=jax.ShapeDtypeStruct((8, 16, OWN)...  4.57 us
    unnamed x8, local copies, waits for them, and re-layouts  2.64 us
  transfers between devices with their start and end apart: 5, of which 3 were waited for; matrix products, arithmetic and copies ran while one was open for 0% of the time, Pallas kernels for 1%

profile of v10, /device:TPU:1, one launch (start us, length us, event | category | flops | bytes accessed | tf_op | source)
XLA Modules:
  0.0 130.3 jit_solution(8952391647252530750)
XLA Ops:
  0.0 2.1 %pack.1 = (f32[392,256]{1,0:T(8,128)}, f32[392,256]{1,0:T(8,128)}) custom-call(s32[1]{0:T(128)} %bitcast.1.core_ref, s32[1,256]{1,0:T(1,128)} %bitcast.23, s32[1,256]{1,0:T(1,128)} %bitcast.24, f32[729,256]{1,0:T(8,128)} %bitcast.22), custom_call_target="tpu_custom_call" | custom-call | tf_op jit(solution)/shard_map/pack/pallas_call | solution.py:353
  2.1 8.8 %collective-permute-start = (f32[392,256]{1,0:T(8,128)}, f32[392,256]{1,0:T(8,128)S(1)}, u32[]{:S(2)}, u32[]{:S(2)}) collective-permute-start(f32[392,256]{1,0:T(8,128)} %get-tuple-element.15), channel_id=1, source_target_pairs={{0,1},{1,0},{2,3},{3,2},{4,5},{5,4},{6,7},{7,6},{8,9},{9,8},{10,11... | collective-permute-start | bytes 1204232 | tf_op jit(solution)/shard_map/ppermute | solution.py:367
  10.9 0.0 copy-start.2
  10.9 1.0 copy-done.2
  11.9 0.0 copy-start.1
  11.9 0.0 copy-start.3
  11.9 0.5 own_sums.1.own_ref
  12.4 0.1 collective-permute-done.other_ref
  12.5 1.4 %deliver.1 = f32[544,384]{1,0:T(8,128)} custom-call(f32[544,384]{1,0:T(8,128)S(1)} %own_sums.1.own_ref, f32[392,256]{1,0:T(8,128)S(1)} %collective-permute-done.other_ref), custom_call_target="tpu_custom_call" | custom-call | tf_op jit(solution)/shard_map/deliver/pallas_call | solution.py:376
  13.8 3.5 %all-to-all-start = ((f32[4,136,384]{2,1,0:T(8,128)}), f32[4,136,384]{2,1,0:T(8,128)S(1)}, u32[]{:S(2)}, u32[]{:S(2)}) async-start(f32[4,136,384]{2,1,0:T(8,128)} %bitcast.5), calls=%async_computation | async-start | bytes 1671168 | tf_op jit(solution)/shard_map/all_to_all | solution.py:39
  17.4 0.0 copy-done.1
  17.4 0.0 copy-done.3
  17.4 0.1 ghosts.1
  17.5 1.3 collective-permute-start.1
  18.8 1.3 collective-permute-start.2
  20.1 13.0 %all-to-all-done.part_ref = f32[4,136,384]{2,1,0:T(8,128)S(1)} async-done(((f32[4,136,384]{2,1,0:T(8,128)}), f32[4,136,384]{2,1,0:T(8,128)S(1)}, u32[]{:S(2)}, u32[]{:S(2)}) %all-to-all-start) | async-done | bytes 835616 | tf_op jit(solution)/shard_map/all_to_all | solution.py:39
  33.0 0.1 windows.1
  33.1 0.0 collective-permute-done.2.right_ref
  33.1 0.0 collective-permute-done.1.left_ref
  33.1 14.0 %all_to_all.35 = f32[16,40,128]{2,1,0:T(8,128)S(1)} all-to-all(f32[16,40,128]{2,1,0:T(8,128)S(1)} %windows.1), channel_id=1, replica_groups={{0,8,16,24,32,40,48,56,64,72,80,88,96,104,112,120},{128,136,144,152,160..., dimensions={0} | all-to-all | bytes 655360 | tf_op jit(solution)/shard_map/all_to_all | solution.py:39
  47.1 0.7 broadcast_in_dim.6
  47.8 10.0 %all-to-all-start.2 = ((f32[8,40,128]{2,1,0:T(8,128)}), f32[8,40,128]{2,1,0:T(8,128)S(1)}, u32[]{:S(2)}, u32[]{:S(2)}) async-start(f32[8,40,128]{2,1,0:T(8,128)} %broadcast_in_dim.6), calls=%async_computation.2 | async-start | bytes 327680 | tf_op jit(solution)/shard_map/all_to_all | solution.py:39
  57.9 1.6 %copy-done = f32[729,729]{1,0:T(8,128)S(1)} copy-done((f32[729,729]{1,0:T(8,128)S(1)}, f32[729,729]{1,0:T(8,128)}, u32[]{:S(2)}) %copy-start) | copy-done | bytes 2125788
  59.5 0.7 split_operator.1.ksplit
  60.2 6.0 %all-to-all-done.2.part_ref = f32[8,40,128]{2,1,0:T(8,128)S(1)} async-done(((f32[8,40,128]{2,1,0:T(8,128)}), f32[8,40,128]{2,1,0:T(8,128)S(1)}, u32[]{:S(2)}, u32[]{:S(2)}) %all-to-all-start.2) | async-done | bytes 163872 | tf_op jit(solution)/shard_map/all_to_all | solution.py:39
  66.2 4.6 %chebyshev.1 = f32[8,16,648]{2,1,0:T(8,128)S(1)} custom-call(s32[1]{0:T(128)} %bitcast.last_ref, f32[8]{0:T(128)S(1)} %copy-done.3, f32[16,8,648]{2,1,0:T(8,128)S(1)} %copy-done.1, f32[16,2304]{1,0:T(8,128)S(1)} %collective-permute-done.1.left_ref, f32[16,1664]{1,0:T(8,128)S(1)} %collective-permute-done.2.right_ref, ...), custom_call_target="tpu_custom_call" | custom-call | tf_op jit(solution)/shard_map/chebyshev/pallas_call | solution.py:421
  70.8 18.2 %all_to_all.36 = f32[8,16,648]{2,1,0:T(8,128)S(1)} all-to-all(f32[8,16,648]{2,1,0:T(8,128)S(1)} %chebyshev.1), channel_id=1, replica_groups=mesh['dom'=64,'band'=8] {'band'}, dimensions={0} | all-to-all | bytes 663552 | tf_op jit(solution)/shard_map/all_to_all | solution.py:39
  89.0 0.3 fusion
  89.3 9.9 %all_to_all.37 = f32[16,8,128]{2,1,0:T(8,128)S(1)} all-to-all(f32[16,8,128]{2,1,0:T(8,128)S(1)} %fusion), channel_id=1, replica_groups={{0,1,8,9,128,129,136,137,256,257,264,265,384,385,392,393},{2,3,10,11,13..., dimensions={0} | all-to-all | bytes 131072 | tf_op jit(solution)/shard_map/all_to_all | solution.py:39
  99.2 14.7 %all_to_all.38 = f32[32,8,128]{2,1,0:T(8,128)S(1)} all-to-all(f32[32,8,128]{2,1,0:T(8,128)S(1)} %broadcast_in_dim.7), channel_id=1, replica_groups={{0,2,4,6,16,18,20,22,32,34,36,38,48,50,52,54,64,66,68,70,80,82,84,86,96..., dimensions={0} | all-to-all | bytes 262144 | tf_op jit(solution)/shard_map/all_to_all | solution.py:39
  113.9 10.3 %all_to_all.39 = f32[16,8,128]{2,1,0:T(8,128)S(1)} all-to-all(f32[16,8,128]{2,1,0:T(8,128)S(1)} %broadcast_in_dim.8), channel_id=1, replica_groups={{0,1,8,9,128,129,136,137,256,257,264,265,384,385,392,393},{2,3,10,11,13..., dimensions={0} | all-to-all | bytes 131072 | tf_op jit(solution)/shard_map/all_to_all | solution.py:39
  124.2 6.1 %orthonormalize.1 = f32[648,128]{1,0:T(8,128)} custom-call(f32[128,128]{1,0:T(8,128)S(1)} %bitcast.20, f32[128,648]{1,0:T(8,128)S(1)} %bitcast.19), custom_call_target="tpu_custom_call" | custom-call | tf_op jit(solution)/shard_map/orthonormalize/pallas_call | solution.py:447
  (6 shorter events, 0.1 us)
Async XLA Ops:
  2.1 10.3 %collective-permute-start = (f32[392,256]{1,0:T(8,128)}, f32[392,256]{1,0:T(8,128)S(1)}, u32[]{:S(2)}, u32[]{:S(2)}) collective-permute-start(f32[392,256]{1,0:T(8,128)} %get-tuple-element.15), channel_id=1, source_target_pairs={{0,1},{1,0},{2,3},{3,2},{4,5},{5,4},{6,7},{7,6},{8,9},{9,8},{10,11... | collective-permute-start | bytes 1204232 | tf_op jit(solution)/shard_map/ppermute | solution.py:367
  10.9 1.0 copy-start.2
  11.9 5.4 %copy-start.1 = (f32[16,8,648]{2,1,0:T(8,128)S(1)}, f32[16,8,648]{2,1,0:T(8,128)}, u32[]{:S(2)}) copy-start(f32[16,8,648]{2,1,0:T(8,128)} %own_ref.1) | copy-start | bytes 995332
  11.9 5.5 %copy-start.3 = (f32[8]{0:T(128)S(1)}, f32[8]{0:T(128)}, u32[]{:S(2)}) copy-start(f32[8]{0:T(128)} %scale_ref.1) | copy-start | bytes 100
  13.8 19.2 %all-to-all-start = ((f32[4,136,384]{2,1,0:T(8,128)}), f32[4,136,384]{2,1,0:T(8,128)S(1)}, u32[]{:S(2)}, u32[]{:S(2)}) async-start(f32[4,136,384]{2,1,0:T(8,128)} %bitcast.5), calls=%async_computation | async-start | bytes 1671168 | tf_op jit(solution)/shard_map/all_to_all | solution.py:39
  17.5 15.7 %collective-permute-start.1 = (f32[16,2304]{1,0:T(8,128)S(1)}, f32[16,2304]{1,0:T(8,128)S(1)}, u32[]{:S(2)}, u32[]{:S(2)}) collective-permute-start(f32[16,2304]{1,0:T(8,128)S(1)} %get-tuple-element.16), channel_id=1, source_target_pairs={{0,8},{8,16},{16,24},{24,32},{32,40},{40,48},{48,56},{56,64},{64,7... | collective-permute-start | bytes 442376 | tf_op jit(solution)/shard_map/ppermute | solution.py:393
  18.8 14.4 %collective-permute-start.2 = (f32[16,1664]{1,0:T(8,128)S(1)}, f32[16,1664]{1,0:T(8,128)S(1)}, u32[]{:S(2)}, u32[]{:S(2)}) collective-permute-start(f32[16,1664]{1,0:T(8,128)S(1)} %get-tuple-element.17), channel_id=1, source_target_pairs={{8,0},{16,8},{24,16},{32,24},{40,32},{48,40},{56,48},{64,56},{72,6... | collective-permute-start | bytes 319496 | tf_op jit(solution)/shard_map/ppermute | solution.py:394
  47.8 18.4 %all-to-all-start.2 = ((f32[8,40,128]{2,1,0:T(8,128)}), f32[8,40,128]{2,1,0:T(8,128)S(1)}, u32[]{:S(2)}, u32[]{:S(2)}) async-start(f32[8,40,128]{2,1,0:T(8,128)} %broadcast_in_dim.6), calls=%async_computation.2 | async-start | bytes 327680 | tf_op jit(solution)/shard_map/all_to_all | solution.py:39
  57.9 1.6 %copy-start = (f32[729,729]{1,0:T(8,128)S(1)}, f32[729,729]{1,0:T(8,128)}, u32[]{:S(2)}) copy-start(f32[729,729]{1,0:T(8,128)} %operator_ref) | copy-start | bytes 6377296
